TPU v7x, 32 devices: a whole 2x2x4 slice. The times are simulated.
32 devices in a mesh: vocab: 8 (over z, x), width: 4 (over y, core).
Axes of the slice: x: 2, y: 2, z: 4, core: 2. Of those that a mesh axis runs over, the one named last changes fastest.
Arguments:
- hidden: bfloat16 [8192, 1024], P('vocab', 'width'), may hold values from -60 to 60
- norm_gain: float32 [1024], P('width'), may hold values from 0.5 to 1.5
- head_weight: bfloat16 [1024, 32128], P('width', 'vocab'), may hold values from -1 to 1
- token_ids: int32 [8192], P('width'), may hold values from 0 to 32127
- seq_lengths: int32 [4], replicated, may hold values from 1 to 2048, as said below
Outputs:
- log_probs: float32 [8192], P('width')
- entropies: float32 [8192], P('width')
Inputs may be any that keep to these rules, and one draw needn't show every extreme that they name: `seq_lengths`: each sequence has 1 to 2048 live tokens at its start; some sequence has exactly 2048.
All inputs are finite; a program needn't handle non-finite values.
Results may differ from a plain program's by a relative error of at most 0.0041.
Values may be sent and summed in bfloat16 or wider, within the bound.
No kernel may reach another device: no remote copies, remote signals or barrier semaphores. Data moves between devices by JAX's collectives and lax.ppermute only.
A program may use at most 320 MiB of HBM per device.

v0:
```python
import jax
import jax.numpy as jnp
from jax import lax
from jax.sharding import PartitionSpec as P

D = 1024
SEQ_LEN = 2048


def on_device(hidden, norm_gain, head_weight, token_ids, seq_lengths):
    hidden_wide = hidden.astype(jnp.float32)
    square_part = jnp.sum(hidden_wide * hidden_wide, axis=1)
    square_sum = lax.psum(square_part, "width")
    normed = (hidden_wide * lax.rsqrt(square_sum / D + 1e-06)[:, None] * norm_gain[None, :]).astype(
        jnp.bfloat16
    )
    gathered = lax.all_gather(normed, "vocab", axis=0, tiled=True)
    width_count = lax.axis_size("width")
    row_count = gathered.shape[0] // width_count
    full_rows = lax.all_to_all(gathered, "width", split_axis=0, concat_axis=1, tiled=True)
    logits = jnp.dot(
        full_rows,
        lax.all_gather(head_weight, "width", axis=0, tiled=True),
        preferred_element_type=jnp.float32,
    )
    shard_columns = logits.shape[1]
    first_column = lax.axis_index("vocab") * shard_columns
    local_ids = token_ids - first_column
    target_hit = lax.broadcasted_iota(jnp.int32, logits.shape, 1) == local_ids[:, None]
    target = jnp.sum(jnp.where(target_hit, logits, 0.0), axis=1)
    largest = lax.pmax(jnp.max(logits, axis=1), "vocab")
    shifted = logits - largest[:, None]
    exponent_terms = jnp.exp(shifted)
    total_exp, weighted, target = lax.psum(
        (jnp.sum(exponent_terms, axis=1), jnp.sum(exponent_terms * shifted, axis=1), target),
        "vocab",
    )
    logsum = jnp.log(total_exp)
    log_probs = target - (largest + logsum)
    entropies = logsum - weighted / total_exp
    row_index = lax.axis_index("width") * row_count + lax.iota(jnp.int32, row_count)
    position = row_index % SEQ_LEN
    sequence = row_index // SEQ_LEN
    seq_match = sequence[:, None] == lax.iota(jnp.int32, seq_lengths.shape[0])[None, :]
    seq_limit = jnp.sum(jnp.where(seq_match, seq_lengths[None, :], 0), axis=1)
    live_rows = position < seq_limit
    return (jnp.where(live_rows, log_probs, 0.0), jnp.where(live_rows, entropies, 0.0))


def solution(mesh):
    in_specs = (P("vocab", "width"), P("width"), P("width", "vocab"), P("width"), P())
    out_specs = (P("width"), P("width"))
    return jax.shard_map(
        on_device, mesh=mesh, in_specs=in_specs, out_specs=out_specs, check_vma=False
    )
```

profile of v0, /device:TPU:0, one launch (start us, length us, event | category | flops | bytes accessed | tf_op | source)
XLA Modules:
  0.0 294.6 jit_solution(14997901224949695728)
XLA Ops:
  7.2 0.0 copy-start.1
  7.2 0.0 copy-start
  7.2 0.0 all-gather.3.cloned.1.call-start
  7.2 1.3 fusion.1
  8.5 8.4 %psum.28 = f32[1024]{0:T(1024)S(1)} all-reduce(f32[1024]{0:T(1024)S(1)} %fusion.1), channel_id=1, replica_groups=mesh['vocab'=8,'width'=4] {'width'}, use_global_device_ids=true, to_apply=%region_2.3 | all-reduce | flops 1024 | bytes 8192 | tf_op jit(solution)/shard_map/psum | solution.py:13
  16.9 2.0 fusion.3
  18.9 0.0 all-gather.3.cloned.1.call-update
  18.9 0.0 all-gather.5.cloned.1.call-start
  19.0 0.7 all-gather.5.cloned.1.call-update
  19.7 73.1 %all-gather.3.cloned.1.call-done = bf16[8192,256]{1,0:T(8,128)(2,1)} async-done(((bf16[1024,256]{1,0:T(8,128)(2,1)}), bf16[8192,256]{1,0:T(8,128)(2,1)}) %all-gather.3.cloned.1.call-update) | async-done | bytes 4194320 | tf_op jit(solution)/shard_map/all_gather | solution.py:17
  92.8 4.8 %all-to-all-start = ((bf16[4,2048,256]{2,1,0:T(8,128)(2,1)}), bf16[4,2048,256]{2,1,0:T(8,128)(2,1)}, u32[]{:S(2)}, u32[]{:S(2)}) async-start(bf16[4,2048,256]{2,1,0:T(8,128)(2,1)} %bitcast.5), calls=%async_computation | async-start | bytes 8388608 | tf_op jit(solution)/shard_map/all_to_all | solution.py:20
  97.7 0.0 copy-done.1
  97.7 0.1 select_reduce_fusion.1
  97.8 0.0 copy-done
  97.8 90.0 %all-to-all-done = bf16[4,2048,256]{2,1,0:T(8,128)(2,1)} async-done(((bf16[4,2048,256]{2,1,0:T(8,128)(2,1)}), bf16[4,2048,256]{2,1,0:T(8,128)(2,1)}, u32[]{:S(2)}, u32[]{:S(2)}) %all-to-all-start) | async-done | bytes 4194336 | tf_op jit(solution)/shard_map/all_to_all | solution.py:20
  187.8 6.3 %copy.8 = bf16[2048,4,256]{0,2,1:T(8,128)(2,1)} copy(bf16[2048,4,256]{2,0,1:T(8,128)(2,1)} %bitcast.1) | data formatting | bytes 8388608 | tf_op jit(solution)/shard_map/all_to_all | solution.py:20
  194.2 0.0 all-gather.5.cloned.1.call-done
  194.2 24.8 %fusion.10 = (f32[2048]{0:T(1024)S(1)}, f32[2048,4016]{0,1:T(8,128)}) fusion(bf16[1024,4016]{0,1:T(8,128)(2,1)} %all-gather.5.cloned.1.call-done, bf16[2048,1024]{0,1:T(8,128)(2,1)} %bitcast.6), kind=kOutput, calls=%fused_computation.29 | convolution fusion | flops 16852547584 | bytes 45326336 | tf_op jit(solution)/shard_map/dot_general | solution.py:21
  219.0 17.5 %pmax.7 = f32[2048]{0:T(1024)S(1)} all-reduce(f32[2048]{0:T(1024)S(1)} %get-tuple-element.10), channel_id=1, replica_groups=mesh['vocab'=8,'width'=4] {'vocab'}, use_global_device_ids=true, to_apply=%region_6.7 | all-reduce | flops 2048 | bytes 16384 | tf_op jit(solution)/shard_map/pmax | solution.py:31
  236.4 15.9 %fusion = (f32[2048]{0:T(1024)S(1)}, f32[2048]{0:T(1024)S(1)}, f32[2048]{0:T(1024)S(1)}) fusion(f32[2048,4016]{0,1:T(8,128)} %get-tuple-element.11, f32[2048]{0:T(1024)S(1)} %pmax.7, s32[2048]{0:T(1024)S(1)} %broadcast_subtract_fusion), kind=kLoop, calls=%fused_computation.2 | loop fusion | flops 57567232 | bytes 32940032 | tf_op jit(solution)/shard_map/reduce_sum | solution.py:35
  252.3 34.8 %all-reduce = (f32[2048]{0:T(1024)S(1)}, f32[2048]{0:T(1024)S(1)}, f32[2048]{0:T(1024)S(1)}) all-reduce(f32[2048]{0:T(1024)S(1)} %get-tuple-element.4, f32[2048]{0:T(1024)S(1)} %get-tuple-element.3, f32[2048]{0:T(1024)S(1)} %get-tuple-element.2), channel_id=1, replica_groups=mesh['vocab'=8,'width'=4] {'vocab'}, use_global_device_ids=true, to_apply=%region_4.5 | all-reduce | flops 6144 | bytes 49152 | tf_op jit(solution)/shard_map/psum | solution.py:34
  287.1 0.6 subtract_select_fusion
  (3 shorter events, 0.0 us)
Async XLA Ops:
  7.2 90.5 %copy-start.1 = (s32[4]{0:T(128)S(1)}, s32[4]{0:T(128)}, u32[]{:S(2)}) copy-start(s32[4]{0:T(128)} %param.9) | copy-start | bytes 52
  7.2 90.6 %copy-start = (s32[2048]{0:T(1024)S(1)}, s32[2048]{0:T(1024)}, u32[]{:S(2)}) copy-start(s32[2048]{0:T(1024)} %param.8) | copy-start | bytes 24580
  7.2 85.6 %all-gather.3.cloned.1.call-start = ((), (), s32[]{:S(2)}) async-start(), calls=%async_computation.1 | async-start | bytes 4718592 | tf_op jit(solution)/shard_map/all_gather | solution.py:17
  18.9 175.2 %all-gather.5.cloned.1.call-start = ((), (), s32[]{:S(2)}) async-start(), calls=%async_computation.2 | async-start | bytes 10280960 | tf_op jit(solution)/shard_map/all_gather | solution.py:23
  92.8 95.0 %all-to-all-start = ((bf16[4,2048,256]{2,1,0:T(8,128)(2,1)}), bf16[4,2048,256]{2,1,0:T(8,128)(2,1)}, u32[]{:S(2)}, u32[]{:S(2)}) async-start(bf16[4,2048,256]{2,1,0:T(8,128)(2,1)} %bitcast.5), calls=%async_computation | async-start | bytes 8388608 | tf_op jit(solution)/shard_map/all_to_all | solution.py:20
Sparse Core Ops, SparseCore 0:
  19.1 73.6 all-gather.2
  94.3 98.3 all-gather.4
where the time goes:
time: 295 us
  waiting for transfers between devices  164 us (56%)
  blocking collectives  60.6 us (21%)
  matrix products  24.8 us (8%)
  other arithmetic  19.9 us (7%)
  between operations  14.1 us (5%)
  local copies, waits for them, and re-layouts  6.34 us (2%)
  starting transfers between devices  4.92 us (2%)
    all_to_all x1, waiting for transfers between devices, on_device(): lax.all_to_all(gathered, 'width', split_axis=0, concat_axis=1, tiled=True)  90 us
    all_gather x1, waiting for transfers between devices, on_device(): gathered = lax.all_gather(normed, 'vocab', axis=0, tiled=True)  73.1 us
    psum x1, blocking collectives, on_device(): lax.psum((jnp.sum(exponent_terms, axis=1), jnp.sum(exponent_terms * shift...  34.8 us
    dot_general x1, matrix products, on_device(): jnp.dot(full_rows, lax.all_gather(head_weight, 'width', axis=0, tiled=Tru...  24.8 us
    pmax x1, blocking collectives, on_device(): largest = lax.pmax(jnp.max(logits, axis=1), 'vocab')  17.5 us
    reduce_sum x1, other arithmetic, on_device(): jnp.sum(exponent_terms * shifted, axis=1)  15.9 us
    psum x1, blocking collectives, on_device(): square_sum = lax.psum(square_part, 'width')  8.38 us
    all_to_all x1, local copies, waits for them, and re-layouts, on_device(): lax.all_to_all(gathered, 'width', split_axis=0, concat_axis=1, tiled=True)  6.33 us
  transfers between devices with their start and end apart: 3, of which 2 were waited for; matrix products, arithmetic and copies ran while one was open for 2% of the time, Pallas kernels for 0%

commit v1 on v0

v1 whole, which is shorter than its diff:
```python
import functools

import jax
import jax.numpy as jnp
from jax import lax
from jax.experimental import pallas as pl
from jax.experimental.pallas import tpu as pltpu
from jax.sharding import PartitionSpec as P

SEQ_LEN = 2048
EPS = 1e-06
LOW = -1e30
TILE = 256
EXTRA = 16
AXES = ("vocab", "width")
VMEM = pl.BlockSpec(memory_space=pltpu.VMEM)
SMEM = pl.BlockSpec(memory_space=pltpu.SMEM)


class Plan:
    def __init__(self, mesh, rows, columns):
        self.V, self.W = mesh.shape["vocab"], mesh.shape["width"]
        self.X = 1
        while 4 * self.X * self.X <= self.V:
            self.X *= 2
        self.Z = self.V // self.X
        self.rows = rows
        self.part = rows // self.W
        self.blocks = SEQ_LEN // rows
        self.columns = columns

    def perm(self, move):
        return [
            (v * self.W + w, t * self.W + u)
            for v in range(self.V)
            for w in range(self.W)
            for t, u in [move(v, w)]
        ]

    def width_xor(self, k):
        return self.perm(lambda v, w: (v, w ^ k))

    def vocab_xor(self, k):
        return self.perm(lambda v, w: (v ^ k, w))

    def z_ring(self):
        return self.perm(lambda v, w: ((v + self.X) % self.V, w))

    def x_ring(self):
        return self.perm(lambda v, w: (v - v % self.X + (v + 1) % self.X, w))


def quarter(plan, v, w):
    return lax.rem(w + v, plan.W)


def id_rows(plan, ids_ref, w, target):
    out = []
    for h in range(plan.blocks):
        q = quarter(plan, w * plan.blocks + h, target)
        out.append(ids_ref[pl.ds(h * plan.W + q, 1), :])
    return out


def send_kernel(plan, meta_ref, h_ref, gain_ref, ids_ref, *outs):
    v, w = meta_ref[0], meta_ref[1]
    part = plan.part
    gain = gain_ref[...]
    high = gain.astype(jnp.bfloat16).astype(jnp.float32)
    rest = gain - high
    middle = rest.astype(jnp.bfloat16).astype(jnp.float32)
    low = rest - middle
    width = gain.shape[1]
    for k in range(1, plan.W):
        target = w ^ k
        start = pl.multiple_of(quarter(plan, v, target) * part, part)
        outs[k - 1][:part, :] = h_ref[pl.ds(start, part), :]
        rows = [high, middle, low]
        for line in id_rows(plan, ids_ref, w, target):
            upper = line // 256
            for piece in (upper, line - upper * 256):
                piece = piece.astype(jnp.float32)
                if part < width:
                    piece = jnp.concatenate([piece, jnp.zeros((1, width - part), jnp.float32)], axis=1)
                rows.append(piece[:, :width])
        rows.append(jnp.zeros((EXTRA - len(rows), width), jnp.float32))
        outs[k - 1][part:, :] = jnp.concatenate(rows, axis=0).astype(jnp.bfloat16)


def norm_kernel(plan, depth, meta_ref, h_ref, gain_ref, ids_ref, *refs):
    pieces, (out_ref, out_ids) = refs[: plan.W - 1], refs[plan.W - 1 :]
    v, w = meta_ref[0], meta_ref[1]
    part, width = plan.part, gain_ref.shape[1]
    start = pl.multiple_of(quarter(plan, v, w) * part, part)
    wide = [h_ref[pl.ds(start, part), :].astype(jnp.float32)]
    gains = [gain_ref[...]]
    for h, line in enumerate(id_rows(plan, ids_ref, w, w)):
        out_ids[h : h + 1, :] = line
    for k in range(1, plan.W):
        wide.append(pieces[k - 1][:part, :].astype(jnp.float32))
        extra = pieces[k - 1][part:, :].astype(jnp.float32)
        gains.append((extra[0:1] + extra[1:2]) + extra[2:3])
        for h in range(plan.blocks):
            upper = extra[3 + 2 * h : 4 + 2 * h].astype(jnp.int32)
            under = extra[4 + 2 * h : 5 + 2 * h].astype(jnp.int32)
            row = k * plan.blocks + h
            out_ids[row : row + 1, :] = (upper * 256 + under)[:, :part]
    total = sum(jnp.sum(x * x, axis=1, keepdims=True) for x in wide)
    scale = lax.rsqrt(total / depth + EPS)
    for k in range(plan.W):
        normed = (wide[k] * scale * gains[k]).T
        out_ref[k * width : (k + 1) * width, :] = normed.astype(jnp.bfloat16)


def main_kernel(plan, jobs, sizes, bases, have, last, places, meta_ref, seq_ref, ids_ref, *refs):
    refs = list(refs)
    take = lambda n: [refs.pop(0) for _ in range(n)]
    W, part = plan.W, plan.part
    groups = take(len(jobs))
    chunks = [take(W) for _ in sizes]
    offsets = chunk_offsets(plan, sizes, bases, chunks)
    states = [take(1)[0] if h else None for h in have]
    outs = take(4 if last else len(jobs))
    buffers = take(2)
    v, w = meta_ref[0], meta_ref[1]
    z, x = v // plan.X, lax.rem(v, plan.X)
    lane = (8, part)
    for g, mine in enumerate(jobs):
        dz, dx = places[g]
        source = lax.rem(z - dz + plan.Z, plan.Z) * plan.X + lax.rem(x - dx + plan.X, plan.X)
        s, h = source // plan.blocks, lax.rem(source, plan.blocks)
        first = h * plan.rows + quarter(plan, source, w) * part
        live = seq_ref[s] > first
        rank = (s ^ w) * plan.blocks + h

        def run(state):
            ids = jnp.broadcast_to(ids_ref[pl.ds(rank, 1), :], lane)
            ids = ids - lax.broadcasted_iota(jnp.int32, lane, 0) - v * plan.columns

            def dot(c, start, size):
                left = jnp.concatenate(
                    [ref[pl.ds(off + start, size), :] for ref, off in zip(chunks[c], offsets[c])], axis=1
                )
                return jnp.dot(left, groups[g][...], preferred_element_type=jnp.float32)

            def fold(state, buffer, size, base):
                m, e_sum, l_sum, target = state
                n = size // 8
                logits = buffer[:size, :].reshape((n,) + lane)
                top = jnp.maximum(m, jnp.max(logits, axis=0))
                scale = jnp.exp(m - top)
                terms = jnp.exp(logits - top[None])
                e_sum = e_sum * scale + jnp.sum(terms, axis=0)
                l_sum = l_sum * scale + jnp.sum(terms * logits, axis=0)
                there = ids - base
                for i in range(n):
                    target = jnp.where(there == 8 * i, logits[i], target)
                return top, e_sum, l_sum, target

            for c in mine:
                size, base = sizes[c], bases[c]
                full, rest = size // TILE, size % TILE
                if full:
                    buffers[0][...] = dot(c, 0, TILE)

                    def pair(i, state):
                        for j in range(2):
                            at = 2 * i + j
                            buffers[1 - j][...] = dot(c, pl.multiple_of((at + 1) * TILE, TILE), TILE)
                            state = fold(state, buffers[j], TILE, base + at * TILE)
                        return state

                    pairs = (full - 1) // 2
                    state = lax.fori_loop(0, pairs, pair, state)
                    done = 2 * pairs
                    tail = [(a * TILE, TILE) for a in range(done + 1, full)]
                else:
                    done, tail = 0, []
                if rest:
                    tail.append((full * TILE, rest))
                if not full:
                    buffers[0][:rest, :] = dot(c, *tail.pop(0))
                spans = [(done * TILE, TILE if full else rest)] + tail
                for i, (start, count) in enumerate(spans):
                    if i + 1 < len(spans):
                        buffers[1 - i % 2][: spans[i + 1][1], :] = dot(c, *spans[i + 1])
                    state = fold(state, buffers[i % 2], count, base + start)
            return state

        def start_state():
            if have[g]:
                return tuple(states[g][i] for i in range(4))
            zero = jnp.zeros(lane, jnp.float32)
            return jnp.full(lane, LOW, jnp.float32), zero, zero, zero

        state = lax.cond(live, lambda: run(start_state()), start_state)
        if not last:
            for i in range(4):
                outs[g][i] = state[i]
            continue
        m, e_sum, l_sum, target = state
        top = jnp.max(m, axis=0, keepdims=True)
        scale = jnp.exp(m - top)
        lines = [top] + [jnp.sum(a, axis=0, keepdims=True) for a in (e_sum * scale, l_sum * scale, target)]
        for i, line in enumerate(lines):
            outs[i][pl.ds(source, 1), :] = line


def merge(parts):
    top = functools.reduce(jnp.maximum, [p[0] for p in parts])
    scales = [jnp.exp(p[0] - top) for p in parts]
    e_sum = sum(p[1] * c for p, c in zip(parts, scales))
    l_sum = sum(p[2] * c for p, c in zip(parts, scales))
    return top, e_sum, l_sum, sum(p[3] for p in parts)


def merge_kernel(count, *refs):
    parts = [[ref[i] for i in range(4)] for ref in refs[:count]]
    for i, value in enumerate(merge(parts)):
        refs[count][i] = value


def close_kernel(plan, count, meta_ref, *refs):
    parts = [[ref[i] for i in range(4)] for ref in refs[:count]]
    outs, held = refs[count:-1], refs[-1]
    w = meta_ref[1]
    top, e_sum, l_sum, target = merge(parts)
    logsum = top + jnp.log(e_sum)
    held[0] = target - logsum
    held[1] = logsum - l_sum / e_sum
    for k in range(plan.W):
        for h in range(plan.blocks):
            for i in range(2):
                row = i * plan.blocks + h
                outs[k][row : row + 1, :] = held[i, pl.ds((w ^ k) * plan.blocks + h, 1), :]


def place_kernel(plan, meta_ref, seq_ref, *refs):
    pieces, outs = refs[: plan.W], refs[plan.W :]
    w = meta_ref[1]
    length = seq_ref[w]
    column = lax.broadcasted_iota(jnp.int32, (1, plan.part), 1)
    for k in range(plan.W):
        for h in range(plan.blocks):
            q = quarter(plan, w * plan.blocks + h, w ^ k)
            live = column + (h * plan.rows + q * plan.part) < length
            for i in range(2):
                row = i * plan.blocks + h
                outs[i][pl.ds(h * plan.W + q, 1), :] = jnp.where(live, pieces[k][row : row + 1, :], 0.0)


def chunk_offsets(plan, sizes, bases, chunks):
    return [
        [base if ref.shape[0] == plan.columns and size < plan.columns else 0 for ref in refs]
        for size, base, refs in zip(sizes, bases, chunks)
    ]


def call(kernel, out_shape, args, smem, scratch=(), flops=0, name=None):
    return pl.pallas_call(
        kernel,
        out_shape=out_shape,
        in_specs=[SMEM] * smem + [VMEM] * (len(args) - smem),
        out_specs=jax.tree.map(lambda _: VMEM, out_shape),
        scratch_shapes=list(scratch),
        compiler_params=pltpu.CompilerParams(vmem_limit_bytes=24 * 2**20),
        cost_estimate=pl.CostEstimate(flops=flops, bytes_accessed=2**20, transcendentals=0),
        name=name,
    )(*args)


def chunk_spans(columns):
    step = -(-columns // (4 * TILE)) * TILE
    starts = list(range(0, columns, step))
    return [(a, min(step, columns - a)) for a in starts]


def on_device(mesh, hidden, norm_gain, head_weight, token_ids, seq_lengths):
    rows, width = hidden.shape
    columns = head_weight.shape[1]
    plan = Plan(mesh, rows, columns)
    W, part, blocks = plan.W, plan.part, plan.blocks
    depth = width * W
    v = lax.axis_index("vocab").astype(jnp.int32)
    w = lax.axis_index("width").astype(jnp.int32)
    meta = jnp.stack([v, w])
    gain = norm_gain.reshape(1, width)
    ids = token_ids.reshape(blocks * W, part)
    shape = jax.ShapeDtypeStruct
    move = lambda value, perm: lax.ppermute(value, AXES, perm)

    sent = call(
        functools.partial(send_kernel, plan),
        [shape((part + EXTRA, width), jnp.bfloat16)] * (W - 1),
        (meta, hidden, gain, ids),
        1,
        name="send",
    )
    pieces = [move(sent[k - 1], plan.width_xor(k)) for k in range(1, W)]

    spans = chunk_spans(columns)
    weight = head_weight.T
    bits = [1 << i for i in range(W.bit_length() - 1)]
    whole = {0: weight}
    for bit in bits[:1]:
        whole[bit] = move(weight, plan.width_xor(bit))
    chunks = []
    for a, n in spans:
        held = {0: weight[a : a + n]}
        for bit in reversed(bits):
            for k in list(held):
                if (k, bit) != (0, 1):
                    held[k | bit] = move(held[k], plan.width_xor(bit))
        held[0], held[1] = whole[0], whole[1]
        chunks.append([held[k] for k in range(W)])

    normed, all_ids = call(
        functools.partial(norm_kernel, plan, depth),
        [shape((depth, part), jnp.bfloat16), shape((W * blocks, part), jnp.int32)],
        (meta, hidden, gain, ids, *pieces),
        1,
        name="norm",
    )
    groups = {}
    ring = normed
    for dz in range(plan.Z):
        if dz:
            ring = move(ring, plan.z_ring())
        groups[dz, 0] = ring
        for dx in range(1, plan.X):
            groups[dz, dx] = move(groups[dz, dx - 1], plan.x_ring())

    states = {}

    def stage(jobs, last=False):
        keys = list(jobs)
        used = sorted({c for mine in jobs.values() for c in mine})
        have = [key in states for key in keys]
        sizes, bases = [spans[c][1] for c in used], [spans[c][0] for c in used]
        args = [meta, seq_lengths, all_ids] + [groups[key] for key in keys]
        for c in used:
            args += chunks[c]
        args += [states[key] for key in keys if key in states]
        if last:
            out = [shape((plan.V, part), jnp.float32)] * 4
        else:
            out = [shape((4, 8, part), jnp.float32)] * len(keys)
        work = sum(spans[c][1] for mine in jobs.values() for c in mine)
        got = call(
            functools.partial(
                main_kernel, plan, [[used.index(c) for c in jobs[key]] for key in keys], sizes, bases, have, last, keys
            ),
            out,
            args,
            2,
            scratch=[pltpu.VMEM((TILE, part), jnp.float32)] * 2,
            flops=2 * work * part * depth,
            name="logits",
        )
        if last:
            return jnp.stack(got)
        states.update(zip(keys, got))

    stats = stage({key: list(range(len(spans))) for key in groups}, last=True)

    levels = [1 << i for i in range(plan.V.bit_length() - 1)]
    rounds = [levels[i : i + 2] for i in range(0, len(levels), 2)]
    for i, level in enumerate(rounds):
        others = [level[0]] if len(level) == 1 else [level[0], level[1], level[0] | level[1]]
        parts = [stats] + [move(stats, plan.vocab_xor(k)) for k in others]
        if i + 1 < len(rounds):
            stats = call(
                functools.partial(merge_kernel, len(parts)), shape(stats.shape, jnp.float32), parts, 0, name="merge"
            )
    closed = call(
        functools.partial(close_kernel, plan, len(parts)),
        [shape((2 * blocks, part), jnp.float32)] * W,
        (meta, *parts),
        1,
        scratch=[pltpu.VMEM((2, plan.V, part), jnp.float32)],
        name="close",
    )
    closed = [closed[0]] + [move(closed[k], plan.width_xor(k)) for k in range(1, W)]
    log_probs, entropies = call(
        functools.partial(place_kernel, plan),
        [shape((blocks * W, part), jnp.float32)] * 2,
        (meta, seq_lengths, *closed),
        2,
        name="place",
    )
    return log_probs.reshape(-1), entropies.reshape(-1)


def solution(mesh):
    in_specs = (P("vocab", "width"), P("width"), P("width", "vocab"), P("width"), P())
    out_specs = (P("width"), P("width"))
    return jax.shard_map(
        functools.partial(on_device, mesh), mesh=mesh, in_specs=in_specs, out_specs=out_specs, check_vma=False
    )
```

time: 295 us -> 139 us (0.47)
  waiting for transfers between devices: 164 us -> 89.1 us
  blocking collectives: 60.6 us -> 0 us
  matrix products: 24.8 us -> 0 us
  starting transfers between devices: 4.92 us -> 26 us
  other arithmetic: 19.9 us -> 0.08 us
  Pallas kernels: 0 us -> 17.3 us
  between operations: 14.1 us -> 0.73 us
    all_to_all x1 -> x0, waiting for transfers between devices: 90 us -> none  [on_device(): lax.all_to_all(gathered, 'width', split_axis=0, concat_axis=1, tiled=True)]
    ppermute x0 -> x26, waiting for transfers between devices: none -> 89.1 us  [on_device(): move = lambda value, perm: lax.ppermute(value, AXES, perm)]
    all_gather x2 -> x0, waiting for transfers between devices: 73.1 us -> none  [the longest x1 73.1 us: on_device(): gathered = lax.all_gather(normed, 'vocab', axis=0, tiled=True)]
    psum x2 -> x0, blocking collectives: 43.2 us -> none  [the longest x1 34.8 us: on_device(): lax.psum((jnp.sum(exponent_terms, axis=1), jnp.sum(exponent_terms * shift...]
    ppermute x0 -> x26, starting transfers between devices: none -> 26 us  [on_device(): move = lambda value, perm: lax.ppermute(value, AXES, perm)]
    dot_general x1 -> x0, matrix products: 24.8 us -> none  [on_device(): jnp.dot(full_rows, lax.all_gather(head_weight, 'width', axis=0, tiled=Tru...]
    pmax x1 -> x0, blocking collectives: 17.5 us -> none  [on_device(): largest = lax.pmax(jnp.max(logits, axis=1), 'vocab')]
    pallas_call x0 -> x6, Pallas kernels: none -> 17.3 us  [call(): pl.pallas_call(kernel, out_shape=out_shape, in_specs=[SMEM] * smem + [VME...]
  transfers between devices with their start and end apart: 3 -> 26, of which waited for: 2 -> 16; matrix products, arithmetic and copies ran while one was open for 2% -> 1% of each run, Pallas kernels for 0% -> 0%
where the time goes in v1:
time: 139 us; the launch traced here: 138 us
  waiting for transfers between devices  89.1 us (64%)
  starting transfers between devices  26 us (19%)
  Pallas kernels  17.3 us (12%)
  local copies, waits for them, and re-layouts  5.14 us (4%)
    ppermute x26, waiting for transfers between devices, on_device(): move = lambda value, perm: lax.ppermute(value, AXES, perm)  89.1 us
    ppermute x26, starting transfers between devices, on_device(): move = lambda value, perm: lax.ppermute(value, AXES, perm)  26 us
    pallas_call x6, Pallas kernels, call(): pl.pallas_call(kernel, out_shape=out_shape, in_specs=[SMEM] * smem + [VME...  17.3 us
    unnamed x10, local copies, waits for them, and re-layouts  2.94 us
  transfers between devices with their start and end apart: 26, of which 16 were waited for; matrix products, arithmetic and copies ran while one was open for 1% of the time, Pallas kernels for 0%

profile of v1, /device:TPU:0, one launch (start us, length us, event | category | flops | bytes accessed | tf_op | source)
XLA Modules:
  0.0 138.4 jit_solution(3358743824243914690)
XLA Ops:
  0.6 0.7 reshape.17.ids_ref
  1.4 1.0 copy-done
  2.5 0.7 copy-done.2
  3.1 0.6 send.1
  3.7 0.5 collective-permute-start
  4.3 2.6 %collective-permute-start.1 = (bf16[272,256]{1,0:T(8,128)(2,1)S(1)}, bf16[272,256]{1,0:T(8,128)(2,1)S(1)}, u32[]{:S(2)}, u32[]{:S(2)}) collective-permute-start(bf16[272,256]{1,0:T(8,128)(2,1)S(1)} %get-tuple-element.18), channel_id=1, source_target_pairs={{0,2},{1,3},{2,0},{3,1},{4,6},{5,7},{6,4},{7,5},{8,10},{9,11},{10,... | collective-permute-start | bytes 417800 | tf_op jit(solution)/shard_map/ppermute | solution.py:290
  6.9 4.5 %collective-permute-done.1.refs_1_ = bf16[272,256]{1,0:T(8,128)(2,1)S(1)} collective-permute-done((bf16[272,256]{1,0:T(8,128)(2,1)S(1)}, bf16[272,256]{1,0:T(8,128)(2,1)S(1)}, u32[]{:S(2)}, u32[]{:S(2)}) %collective-permute-start.1) | collective-permute-done | bytes 139296 | tf_op jit(solution)/shard_map/ppermute | solution.py:290
  11.4 2.5 %collective-permute-done.2.refs_2_ = bf16[272,256]{1,0:T(8,128)(2,1)S(1)} collective-permute-done((bf16[272,256]{1,0:T(8,128)(2,1)S(1)}, bf16[272,256]{1,0:T(8,128)(2,1)S(1)}, u32[]{:S(2)}, u32[]{:S(2)}) %collective-permute-start.2) | collective-permute-done | bytes 139296 | tf_op jit(solution)/shard_map/ppermute | solution.py:290
  13.8 1.0 norm.1
  14.8 1.7 %collective-permute-start.4 = (bf16[1024,256]{1,0:T(8,128)(2,1)S(1)}, bf16[1024,256]{1,0:T(8,128)(2,1)S(1)}, u32[]{:S(2)}, u32[]{:S(2)}) collective-permute-start(bf16[1024,256]{1,0:T(8,128)(2,1)S(1)} %get-tuple-element.21.refs_0_), channel_id=1, source_target_pairs={{0,8},{1,9},{2,10},{3,11},{4,12},{5,13},{6,14},{7,15},{8,16},{9,17... | collective-permute-start | bytes 1572872 | tf_op jit(solution)/shard_map/ppermute | solution.py:290
  16.5 1.5 %fusion = (bf16[1024,256]{1,0:T(8,128)(2,1)S(1)}, bf16[1024,256]{1,0:T(8,128)(2,1)S(1)}, bf16[1024,256]{1,0:T(8,128)(2,1)S(1)}) fusion(bf16[4016,256]{1,0:T(8,128)(2,1)} %bitcast.12), kind=kLoop, calls=%fused_computation.2 | loop fusion | bytes 3145728 | tf_op jit(solution)/shard_map/slice | solution.py:309
  18.0 1.6 %collective-permute-start.15 = (bf16[1024,256]{1,0:T(8,128)(2,1)S(1)}, bf16[1024,256]{1,0:T(8,128)(2,1)S(1)}, u32[]{:S(2)}, u32[]{:S(2)}) collective-permute-start(bf16[1024,256]{1,0:T(8,128)(2,1)S(1)} %get-tuple-element.32), channel_id=1, source_target_pairs={{0,2},{1,3},{2,0},{3,1},{4,6},{5,7},{6,4},{7,5},{8,10},{9,11},{10,... | collective-permute-start | bytes 1572872 | tf_op jit(solution)/shard_map/ppermute | solution.py:290
  19.6 0.6 collective-permute-start.17
  20.2 1.5 %collective-permute-start.13 = (bf16[1024,256]{1,0:T(8,128)(2,1)S(1)}, bf16[1024,256]{1,0:T(8,128)(2,1)S(1)}, u32[]{:S(2)}, u32[]{:S(2)}) collective-permute-start(bf16[1024,256]{1,0:T(8,128)(2,1)S(1)} %get-tuple-element.33), channel_id=1, source_target_pairs={{0,2},{1,3},{2,0},{3,1},{4,6},{5,7},{6,4},{7,5},{8,10},{9,11},{10,... | collective-permute-start | bytes 1572872 | tf_op jit(solution)/shard_map/ppermute | solution.py:290
  21.7 21.5 %collective-permute-done.17.refs_22_ = bf16[944,256]{1,0:T(8,128)(2,1)S(1)} collective-permute-done((bf16[944,256]{1,0:T(8,128)(2,1)S(1)}, bf16[944,256]{1,0:T(8,128)(2,1)S(1)}, u32[]{:S(2)}, u32[]{:S(2)}) %collective-permute-start.17) | collective-permute-done | bytes 483360 | tf_op jit(solution)/shard_map/ppermute | solution.py:290
  43.2 1.5 %collective-permute-start.11 = (bf16[1024,256]{1,0:T(8,128)(2,1)S(1)}, bf16[1024,256]{1,0:T(8,128)(2,1)S(1)}, u32[]{:S(2)}, u32[]{:S(2)}) collective-permute-start(bf16[1024,256]{1,0:T(8,128)(2,1)S(1)} %get-tuple-element.34), channel_id=1, source_target_pairs={{0,2},{1,3},{2,0},{3,1},{4,6},{5,7},{6,4},{7,5},{8,10},{9,11},{10,... | collective-permute-start | bytes 1572872 | tf_op jit(solution)/shard_map/ppermute | solution.py:290
  44.7 1.6 %collective-permute-start.6 = (bf16[1024,256]{1,0:T(8,128)(2,1)S(1)}, bf16[1024,256]{1,0:T(8,128)(2,1)S(1)}, u32[]{:S(2)}, u32[]{:S(2)}) collective-permute-start(bf16[1024,256]{1,0:T(8,128)(2,1)S(1)} %collective-permute-done.4.refs_2_), channel_id=1, source_target_pairs={{0,8},{1,9},{2,10},{3,11},{4,12},{5,13},{6,14},{7,15},{8,16},{9,17... | collective-permute-start | bytes 1572872 | tf_op jit(solution)/shard_map/ppermute | solution.py:290
  46.3 1.5 %collective-permute-start.3 = (bf16[1024,256]{1,0:T(8,128)(2,1)S(1)}, bf16[1024,256]{1,0:T(8,128)(2,1)S(1)}, u32[]{:S(2)}, u32[]{:S(2)}) collective-permute-start(bf16[1024,256]{1,0:T(8,128)(2,1)S(1)} %get-tuple-element.21.refs_0_), channel_id=1, source_target_pairs={{0,4},{1,5},{2,6},{3,7},{4,0},{5,1},{6,2},{7,3},{8,12},{9,13},{10,... | collective-permute-start | bytes 1572872 | tf_op jit(solution)/shard_map/ppermute | solution.py:290
  47.8 6.6 %collective-permute-done.13.refs_14_ = bf16[1024,256]{1,0:T(8,128)(2,1)S(1)} collective-permute-done((bf16[1024,256]{1,0:T(8,128)(2,1)S(1)}, bf16[1024,256]{1,0:T(8,128)(2,1)S(1)}, u32[]{:S(2)}, u32[]{:S(2)}) %collective-permute-start.13) | collective-permute-done | bytes 524320 | tf_op jit(solution)/shard_map/ppermute | solution.py:290
  54.4 10.3 %collective-permute-done.11.refs_10_ = bf16[1024,256]{1,0:T(8,128)(2,1)S(1)} collective-permute-done((bf16[1024,256]{1,0:T(8,128)(2,1)S(1)}, bf16[1024,256]{1,0:T(8,128)(2,1)S(1)}, u32[]{:S(2)}, u32[]{:S(2)}) %collective-permute-start.11) | collective-permute-done | bytes 524320 | tf_op jit(solution)/shard_map/ppermute | solution.py:290
  64.7 1.6 %collective-permute-start.8 = (bf16[1024,256]{1,0:T(8,128)(2,1)S(1)}, bf16[1024,256]{1,0:T(8,128)(2,1)S(1)}, u32[]{:S(2)}, u32[]{:S(2)}) collective-permute-start(bf16[1024,256]{1,0:T(8,128)(2,1)S(1)} %collective-permute-done.6.refs_4_), channel_id=1, source_target_pairs={{0,8},{1,9},{2,10},{3,11},{4,12},{5,13},{6,14},{7,15},{8,16},{9,17... | collective-permute-start | bytes 1572872 | tf_op jit(solution)/shard_map/ppermute | solution.py:290
  66.3 0.2 collective-permute-start.18
  66.5 1.6 %collective-permute-done.18.refs_23_ = bf16[944,256]{1,0:T(8,128)(2,1)S(1)} collective-permute-done((bf16[944,256]{1,0:T(8,128)(2,1)S(1)}, bf16[944,256]{1,0:T(8,128)(2,1)S(1)}, u32[]{:S(2)}, u32[]{:S(2)}) %collective-permute-start.18) | collective-permute-done | bytes 483360 | tf_op jit(solution)/shard_map/ppermute | solution.py:290
  68.1 0.2 collective-permute-start.12
  68.3 1.5 %collective-permute-start.5 = (bf16[1024,256]{1,0:T(8,128)(2,1)S(1)}, bf16[1024,256]{1,0:T(8,128)(2,1)S(1)}, u32[]{:S(2)}, u32[]{:S(2)}) collective-permute-start(bf16[1024,256]{1,0:T(8,128)(2,1)S(1)} %collective-permute-done.4.refs_2_), channel_id=1, source_target_pairs={{0,4},{1,5},{2,6},{3,7},{4,0},{5,1},{6,2},{7,3},{8,12},{9,13},{10,... | collective-permute-start | bytes 1572872 | tf_op jit(solution)/shard_map/ppermute | solution.py:290
  69.8 0.5 collective-permute-start.7
  70.4 10.4 %collective-permute-done.8.refs_6_ = bf16[1024,256]{1,0:T(8,128)(2,1)S(1)} collective-permute-done((bf16[1024,256]{1,0:T(8,128)(2,1)S(1)}, bf16[1024,256]{1,0:T(8,128)(2,1)S(1)}, u32[]{:S(2)}, u32[]{:S(2)}) %collective-permute-start.8) | collective-permute-done | bytes 524320 | tf_op jit(solution)/shard_map/ppermute | solution.py:290
  80.8 1.5 %collective-permute-start.9 = (bf16[1024,256]{1,0:T(8,128)(2,1)S(1)}, bf16[1024,256]{1,0:T(8,128)(2,1)S(1)}, u32[]{:S(2)}, u32[]{:S(2)}) collective-permute-start(bf16[1024,256]{1,0:T(8,128)(2,1)S(1)} %collective-permute-done.8.refs_6_), channel_id=1, source_target_pairs={{0,4},{1,5},{2,6},{3,7},{4,0},{5,1},{6,2},{7,3},{8,12},{9,13},{10,... | collective-permute-start | bytes 1572872 | tf_op jit(solution)/shard_map/ppermute | solution.py:290
  82.3 0.8 collective-permute-done.5.refs_3_
  83.1 11.2 %collective-permute-done.7.refs_5_ = bf16[1024,256]{1,0:T(8,128)(2,1)S(1)} collective-permute-done((bf16[1024,256]{1,0:T(8,128)(2,1)S(1)}, bf16[1024,256]{1,0:T(8,128)(2,1)S(1)}, u32[]{:S(2)}, u32[]{:S(2)}) %collective-permute-start.7) | collective-permute-done | bytes 524320 | tf_op jit(solution)/shard_map/ppermute | solution.py:290
  94.3 10.6 %collective-permute-done.9.refs_7_ = bf16[1024,256]{1,0:T(8,128)(2,1)S(1)} collective-permute-done((bf16[1024,256]{1,0:T(8,128)(2,1)S(1)}, bf16[1024,256]{1,0:T(8,128)(2,1)S(1)}, u32[]{:S(2)}, u32[]{:S(2)}) %collective-permute-start.9) | collective-permute-done | bytes 524320 | tf_op jit(solution)/shard_map/ppermute | solution.py:290
  104.9 14.6 %logits.1 = (f32[8,256]{1,0:T(8,128)S(1)}, f32[8,256]{1,0:T(8,128)S(1)}, f32[8,256]{1,0:T(8,128)S(1)}, f32[8,256]{1,0:T(8,128)S(1)}) custom-call(s32[2]{0:T(128)S(1)} %pad_add_fusion.meta_ref, s32[4]{0:T(128)S(1)} %copy-done.3, s32[8,256]{1,0:T(8,128)S(1)} %get-tuple-element.20.ids_ref, bf16[1024,256]{1,0:T(8,128)(2,1)S(1)} %get-tuple-element.21.refs_0_, ...), custom_call_target="tpu_custom_call" | custom-call | flops 16844324864 | bytes 1048576 | tf_op jit(solution)/shard_map/logits/pallas_call | solution.py:260
  119.5 2.6 %collective-permute-start.21 = (f32[4,8,256]{2,1,0:T(8,128)S(1)}, f32[4,8,256]{2,1,0:T(8,128)S(1)}, u32[]{:S(2)}, u32[]{:S(2)}) collective-permute-start(f32[4,8,256]{2,1,0:T(8,128)S(1)} %pad_maximum_fusion.refs_0_), channel_id=1, source_target_pairs={{0,12},{1,13},{2,14},{3,15},{4,8},{5,9},{6,10},{7,11},{8,4},{9,5},... | collective-permute-start | bytes 98312 | tf_op jit(solution)/shard_map/ppermute | solution.py:290
  122.1 0.4 collective-permute-start.20
  122.5 0.6 collective-permute-start.19
  123.1 1.6 %collective-permute-done.21.refs_3_ = f32[4,8,256]{2,1,0:T(8,128)S(1)} collective-permute-done((f32[4,8,256]{2,1,0:T(8,128)S(1)}, f32[4,8,256]{2,1,0:T(8,128)S(1)}, u32[]{:S(2)}, u32[]{:S(2)}) %collective-permute-start.21) | collective-permute-done | bytes 32800 | tf_op jit(solution)/shard_map/ppermute | solution.py:290
  124.6 1.4 collective-permute-done.20.refs_2_
  126.0 0.4 collective-permute-done.19.refs_1_
  126.4 1.8 %collective-permute-start.22 = (f32[4,8,256]{2,1,0:T(8,128)S(1)}, f32[4,8,256]{2,1,0:T(8,128)S(1)}, u32[]{:S(2)}, u32[]{:S(2)}) collective-permute-start(f32[4,8,256]{2,1,0:T(8,128)S(1)} %merge.1.refs_0_), channel_id=1, source_target_pairs={{0,16},{1,17},{2,18},{3,19},{4,20},{5,21},{6,22},{7,23},{8,24},{9,... | collective-permute-start | bytes 98312 | tf_op jit(solution)/shard_map/ppermute | solution.py:290
  128.2 3.1 %collective-permute-done.22.refs_1_ = f32[4,8,256]{2,1,0:T(8,128)S(1)} collective-permute-done((f32[4,8,256]{2,1,0:T(8,128)S(1)}, f32[4,8,256]{2,1,0:T(8,128)S(1)}, u32[]{:S(2)}, u32[]{:S(2)}) %collective-permute-start.22) | collective-permute-done | bytes 32800 | tf_op jit(solution)/shard_map/ppermute | solution.py:290
  131.3 0.6 close.1
  131.9 1.6 %collective-permute-start.24 = (f32[4,256]{1,0:T(4,128)S(1)}, f32[4,256]{1,0:T(4,128)S(1)}, u32[]{:S(2)}, u32[]{:S(2)}) collective-permute-start(f32[4,256]{1,0:T(4,128)S(1)} %get-tuple-element.28), channel_id=1, source_target_pairs={{0,2},{1,3},{2,0},{3,1},{4,6},{5,7},{6,4},{7,5},{8,10},{9,11},{10,... | collective-permute-start | bytes 12296 | tf_op jit(solution)/shard_map/ppermute | solution.py:290
  133.5 0.3 collective-permute-start.25
  133.8 1.8 %collective-permute-done.24.refs_2_ = f32[4,256]{1,0:T(4,128)S(1)} collective-permute-done((f32[4,256]{1,0:T(4,128)S(1)}, f32[4,256]{1,0:T(4,128)S(1)}, u32[]{:S(2)}, u32[]{:S(2)}) %collective-permute-start.24) | collective-permute-done | bytes 4128 | tf_op jit(solution)/shard_map/ppermute | solution.py:290
  135.6 0.9 collective-permute-done.25.refs_3_
  136.6 0.6 place.1
  137.2 0.6 copy.7
  137.8 0.6 copy.8
  (25 shorter events, 0.3 us)
Async XLA Ops:
  1.4 1.0 copy-start
  2.5 0.7 copy-start.2
  3.7 15.8 %copy-start.1 = (bf16[256,4016]{0,1:T(8,128)(2,1)S(1)}, bf16[256,4016]{0,1:T(8,128)(2,1)}, u32[]{:S(2)}) copy-start(bf16[256,4016]{0,1:T(8,128)(2,1)} %param.7) | copy-start | bytes 6168580
  3.7 3.2 %collective-permute-start = (bf16[272,256]{1,0:T(8,128)(2,1)S(1)}, bf16[272,256]{1,0:T(8,128)(2,1)S(1)}, u32[]{:S(2)}, u32[]{:S(2)}) collective-permute-start(bf16[272,256]{1,0:T(8,128)(2,1)S(1)} %get-tuple-element.17), channel_id=1, source_target_pairs={{0,1},{1,0},{2,3},{3,2},{4,5},{5,4},{6,7},{7,6},{8,9},{9,8},{10,11... | collective-permute-start | bytes 417800 | tf_op jit(solution)/shard_map/ppermute | solution.py:290
  4.3 7.1 %collective-permute-start.1 = (bf16[272,256]{1,0:T(8,128)(2,1)S(1)}, bf16[272,256]{1,0:T(8,128)(2,1)S(1)}, u32[]{:S(2)}, u32[]{:S(2)}) collective-permute-start(bf16[272,256]{1,0:T(8,128)(2,1)S(1)} %get-tuple-element.18), channel_id=1, source_target_pairs={{0,2},{1,3},{2,0},{3,1},{4,6},{5,7},{6,4},{7,5},{8,10},{9,11},{10,... | collective-permute-start | bytes 417800 | tf_op jit(solution)/shard_map/ppermute | solution.py:290
  6.9 7.0 %collective-permute-start.2 = (bf16[272,256]{1,0:T(8,128)(2,1)S(1)}, bf16[272,256]{1,0:T(8,128)(2,1)S(1)}, u32[]{:S(2)}, u32[]{:S(2)}) collective-permute-start(bf16[272,256]{1,0:T(8,128)(2,1)S(1)} %get-tuple-element.19), channel_id=1, source_target_pairs={{0,3},{1,2},{2,1},{3,0},{4,7},{5,6},{6,5},{7,4},{8,11},{9,10},{10,... | collective-permute-start | bytes 417800 | tf_op jit(solution)/shard_map/ppermute | solution.py:290
  14.8 29.9 %collective-permute-start.4 = (bf16[1024,256]{1,0:T(8,128)(2,1)S(1)}, bf16[1024,256]{1,0:T(8,128)(2,1)S(1)}, u32[]{:S(2)}, u32[]{:S(2)}) collective-permute-start(bf16[1024,256]{1,0:T(8,128)(2,1)S(1)} %get-tuple-element.21.refs_0_), channel_id=1, source_target_pairs={{0,8},{1,9},{2,10},{3,11},{4,12},{5,13},{6,14},{7,15},{8,16},{9,17... | collective-permute-start | bytes 1572872 | tf_op jit(solution)/shard_map/ppermute | solution.py:290
  16.5 88.5 %copy-start.3 = (s32[4]{0:T(128)S(1)}, s32[4]{0:T(128)}, u32[]{:S(2)}) copy-start(s32[4]{0:T(128)} %seq_ref.3) | copy-start | bytes 52
  18.0 28.3 %collective-permute-start.15 = (bf16[1024,256]{1,0:T(8,128)(2,1)S(1)}, bf16[1024,256]{1,0:T(8,128)(2,1)S(1)}, u32[]{:S(2)}, u32[]{:S(2)}) collective-permute-start(bf16[1024,256]{1,0:T(8,128)(2,1)S(1)} %get-tuple-element.32), channel_id=1, source_target_pairs={{0,2},{1,3},{2,0},{3,1},{4,6},{5,7},{6,4},{7,5},{8,10},{9,11},{10,... | collective-permute-start | bytes 1572872 | tf_op jit(solution)/shard_map/ppermute | solution.py:290
  19.6 23.6 %collective-permute-start.17 = (bf16[944,256]{1,0:T(8,128)(2,1)S(1)}, bf16[944,256]{1,0:T(8,128)(2,1)S(1)}, u32[]{:S(2)}, u32[]{:S(2)}) collective-permute-start(bf16[944,256]{1,0:T(8,128)(2,1)S(1)} %slice.19), channel_id=1, source_target_pairs={{0,2},{1,3},{2,0},{3,1},{4,6},{5,7},{6,4},{7,5},{8,10},{9,11},{10,... | collective-permute-start | bytes 1449992 | tf_op jit(solution)/shard_map/ppermute | solution.py:290
  20.2 74.2 %collective-permute-start.10 = (bf16[4016,256]{1,0:T(8,128)(2,1)S(1)}, bf16[4016,256]{1,0:T(8,128)(2,1)S(1)}, u32[]{:S(2)}, u32[]{:S(2)}) collective-permute-start(bf16[4016,256]{1,0:T(8,128)(2,1)S(1)} %bitcast.14), channel_id=1, source_target_pairs={{0,1},{1,0},{2,3},{3,2},{4,5},{5,4},{6,7},{7,6},{8,9},{9,8},{10,11... | collective-permute-start | bytes 6168584 | tf_op jit(solution)/shard_map/ppermute | solution.py:290
  20.2 34.2 %collective-permute-start.13 = (bf16[1024,256]{1,0:T(8,128)(2,1)S(1)}, bf16[1024,256]{1,0:T(8,128)(2,1)S(1)}, u32[]{:S(2)}, u32[]{:S(2)}) collective-permute-start(bf16[1024,256]{1,0:T(8,128)(2,1)S(1)} %get-tuple-element.33), channel_id=1, source_target_pairs={{0,2},{1,3},{2,0},{3,1},{4,6},{5,7},{6,4},{7,5},{8,10},{9,11},{10,... | collective-permute-start | bytes 1572872 | tf_op jit(solution)/shard_map/ppermute | solution.py:290
  43.2 21.5 %collective-permute-start.11 = (bf16[1024,256]{1,0:T(8,128)(2,1)S(1)}, bf16[1024,256]{1,0:T(8,128)(2,1)S(1)}, u32[]{:S(2)}, u32[]{:S(2)}) collective-permute-start(bf16[1024,256]{1,0:T(8,128)(2,1)S(1)} %get-tuple-element.34), channel_id=1, source_target_pairs={{0,2},{1,3},{2,0},{3,1},{4,6},{5,7},{6,4},{7,5},{8,10},{9,11},{10,... | collective-permute-start | bytes 1572872 | tf_op jit(solution)/shard_map/ppermute | solution.py:290
  44.7 20.0 %collective-permute-start.6 = (bf16[1024,256]{1,0:T(8,128)(2,1)S(1)}, bf16[1024,256]{1,0:T(8,128)(2,1)S(1)}, u32[]{:S(2)}, u32[]{:S(2)}) collective-permute-start(bf16[1024,256]{1,0:T(8,128)(2,1)S(1)} %collective-permute-done.4.refs_2_), channel_id=1, source_target_pairs={{0,8},{1,9},{2,10},{3,11},{4,12},{5,13},{6,14},{7,15},{8,16},{9,17... | collective-permute-start | bytes 1572872 | tf_op jit(solution)/shard_map/ppermute | solution.py:290
  46.3 20.0 %collective-permute-start.3 = (bf16[1024,256]{1,0:T(8,128)(2,1)S(1)}, bf16[1024,256]{1,0:T(8,128)(2,1)S(1)}, u32[]{:S(2)}, u32[]{:S(2)}) collective-permute-start(bf16[1024,256]{1,0:T(8,128)(2,1)S(1)} %get-tuple-element.21.refs_0_), channel_id=1, source_target_pairs={{0,4},{1,5},{2,6},{3,7},{4,0},{5,1},{6,2},{7,3},{8,12},{9,13},{10,... | collective-permute-start | bytes 1572872 | tf_op jit(solution)/shard_map/ppermute | solution.py:290
  54.4 13.9 %collective-permute-start.16 = (bf16[1024,256]{1,0:T(8,128)(2,1)S(1)}, bf16[1024,256]{1,0:T(8,128)(2,1)S(1)}, u32[]{:S(2)}, u32[]{:S(2)}) collective-permute-start(bf16[1024,256]{1,0:T(8,128)(2,1)S(1)} %collective-permute-done.15.refs_18_), channel_id=1, source_target_pairs={{0,1},{1,0},{2,3},{3,2},{4,5},{5,4},{6,7},{7,6},{8,9},{9,8},{10,11... | collective-permute-start | bytes 1572872 | tf_op jit(solution)/shard_map/ppermute | solution.py:290
  64.7 5.2 %collective-permute-start.14 = (bf16[1024,256]{1,0:T(8,128)(2,1)S(1)}, bf16[1024,256]{1,0:T(8,128)(2,1)S(1)}, u32[]{:S(2)}, u32[]{:S(2)}) collective-permute-start(bf16[1024,256]{1,0:T(8,128)(2,1)S(1)} %collective-permute-done.13.refs_14_), channel_id=1, source_target_pairs={{0,1},{1,0},{2,3},{3,2},{4,5},{5,4},{6,7},{7,6},{8,9},{9,8},{10,11... | collective-permute-start | bytes 1572872 | tf_op jit(solution)/shard_map/ppermute | solution.py:290
  64.7 16.1 %collective-permute-start.8 = (bf16[1024,256]{1,0:T(8,128)(2,1)S(1)}, bf16[1024,256]{1,0:T(8,128)(2,1)S(1)}, u32[]{:S(2)}, u32[]{:S(2)}) collective-permute-start(bf16[1024,256]{1,0:T(8,128)(2,1)S(1)} %collective-permute-done.6.refs_4_), channel_id=1, source_target_pairs={{0,8},{1,9},{2,10},{3,11},{4,12},{5,13},{6,14},{7,15},{8,16},{9,17... | collective-permute-start | bytes 1572872 | tf_op jit(solution)/shard_map/ppermute | solution.py:290
  66.3 1.9 %collective-permute-start.18 = (bf16[944,256]{1,0:T(8,128)(2,1)S(1)}, bf16[944,256]{1,0:T(8,128)(2,1)S(1)}, u32[]{:S(2)}, u32[]{:S(2)}) collective-permute-start(bf16[944,256]{1,0:T(8,128)(2,1)S(1)} %collective-permute-done.17.refs_22_), channel_id=1, source_target_pairs={{0,1},{1,0},{2,3},{3,2},{4,5},{5,4},{6,7},{7,6},{8,9},{9,8},{10,11... | collective-permute-start | bytes 1449992 | tf_op jit(solution)/shard_map/ppermute | solution.py:290
  68.1 14.2 %collective-permute-start.12 = (bf16[1024,256]{1,0:T(8,128)(2,1)S(1)}, bf16[1024,256]{1,0:T(8,128)(2,1)S(1)}, u32[]{:S(2)}, u32[]{:S(2)}) collective-permute-start(bf16[1024,256]{1,0:T(8,128)(2,1)S(1)} %collective-permute-done.11.refs_10_), channel_id=1, source_target_pairs={{0,1},{1,0},{2,3},{3,2},{4,5},{5,4},{6,7},{7,6},{8,9},{9,8},{10,11... | collective-permute-start | bytes 1572872 | tf_op jit(solution)/shard_map/ppermute | solution.py:290
  68.3 14.8 %collective-permute-start.5 = (bf16[1024,256]{1,0:T(8,128)(2,1)S(1)}, bf16[1024,256]{1,0:T(8,128)(2,1)S(1)}, u32[]{:S(2)}, u32[]{:S(2)}) collective-permute-start(bf16[1024,256]{1,0:T(8,128)(2,1)S(1)} %collective-permute-done.4.refs_2_), channel_id=1, source_target_pairs={{0,4},{1,5},{2,6},{3,7},{4,0},{5,1},{6,2},{7,3},{8,12},{9,13},{10,... | collective-permute-start | bytes 1572872 | tf_op jit(solution)/shard_map/ppermute | solution.py:290
  69.8 24.5 %collective-permute-start.7 = (bf16[1024,256]{1,0:T(8,128)(2,1)S(1)}, bf16[1024,256]{1,0:T(8,128)(2,1)S(1)}, u32[]{:S(2)}, u32[]{:S(2)}) collective-permute-start(bf16[1024,256]{1,0:T(8,128)(2,1)S(1)} %collective-permute-done.6.refs_4_), channel_id=1, source_target_pairs={{0,4},{1,5},{2,6},{3,7},{4,0},{5,1},{6,2},{7,3},{8,12},{9,13},{10,... | collective-permute-start | bytes 1572872 | tf_op jit(solution)/shard_map/ppermute | solution.py:290
  80.8 24.1 %collective-permute-start.9 = (bf16[1024,256]{1,0:T(8,128)(2,1)S(1)}, bf16[1024,256]{1,0:T(8,128)(2,1)S(1)}, u32[]{:S(2)}, u32[]{:S(2)}) collective-permute-start(bf16[1024,256]{1,0:T(8,128)(2,1)S(1)} %collective-permute-done.8.refs_6_), channel_id=1, source_target_pairs={{0,4},{1,5},{2,6},{3,7},{4,0},{5,1},{6,2},{7,3},{8,12},{9,13},{10,... | collective-permute-start | bytes 1572872 | tf_op jit(solution)/shard_map/ppermute | solution.py:290
  119.5 5.1 %collective-permute-start.21 = (f32[4,8,256]{2,1,0:T(8,128)S(1)}, f32[4,8,256]{2,1,0:T(8,128)S(1)}, u32[]{:S(2)}, u32[]{:S(2)}) collective-permute-start(f32[4,8,256]{2,1,0:T(8,128)S(1)} %pad_maximum_fusion.refs_0_), channel_id=1, source_target_pairs={{0,12},{1,13},{2,14},{3,15},{4,8},{5,9},{6,10},{7,11},{8,4},{9,5},... | collective-permute-start | bytes 98312 | tf_op jit(solution)/shard_map/ppermute | solution.py:290
  122.1 3.9 %collective-permute-start.20 = (f32[4,8,256]{2,1,0:T(8,128)S(1)}, f32[4,8,256]{2,1,0:T(8,128)S(1)}, u32[]{:S(2)}, u32[]{:S(2)}) collective-permute-start(f32[4,8,256]{2,1,0:T(8,128)S(1)} %pad_maximum_fusion.refs_0_), channel_id=1, source_target_pairs={{0,8},{1,9},{2,10},{3,11},{4,12},{5,13},{6,14},{7,15},{8,0},{9,1},... | collective-permute-start | bytes 98312 | tf_op jit(solution)/shard_map/ppermute | solution.py:290
  122.5 3.9 %collective-permute-start.19 = (f32[4,8,256]{2,1,0:T(8,128)S(1)}, f32[4,8,256]{2,1,0:T(8,128)S(1)}, u32[]{:S(2)}, u32[]{:S(2)}) collective-permute-start(f32[4,8,256]{2,1,0:T(8,128)S(1)} %pad_maximum_fusion.refs_0_), channel_id=1, source_target_pairs={{0,4},{1,5},{2,6},{3,7},{4,0},{5,1},{6,2},{7,3},{8,12},{9,13},{10,... | collective-permute-start | bytes 98312 | tf_op jit(solution)/shard_map/ppermute | solution.py:290
  126.4 4.9 %collective-permute-start.22 = (f32[4,8,256]{2,1,0:T(8,128)S(1)}, f32[4,8,256]{2,1,0:T(8,128)S(1)}, u32[]{:S(2)}, u32[]{:S(2)}) collective-permute-start(f32[4,8,256]{2,1,0:T(8,128)S(1)} %merge.1.refs_0_), channel_id=1, source_target_pairs={{0,16},{1,17},{2,18},{3,19},{4,20},{5,21},{6,22},{7,23},{8,24},{9,... | collective-permute-start | bytes 98312 | tf_op jit(solution)/shard_map/ppermute | solution.py:290
  131.9 1.9 %collective-permute-start.23 = (f32[4,256]{1,0:T(4,128)S(1)}, f32[4,256]{1,0:T(4,128)S(1)}, u32[]{:S(2)}, u32[]{:S(2)}) collective-permute-start(f32[4,256]{1,0:T(4,128)S(1)} %get-tuple-element.27), channel_id=1, source_target_pairs={{0,1},{1,0},{2,3},{3,2},{4,5},{5,4},{6,7},{7,6},{8,9},{9,8},{10,11... | collective-permute-start | bytes 12296 | tf_op jit(solution)/shard_map/ppermute | solution.py:290
  131.9 3.7 %collective-permute-start.24 = (f32[4,256]{1,0:T(4,128)S(1)}, f32[4,256]{1,0:T(4,128)S(1)}, u32[]{:S(2)}, u32[]{:S(2)}) collective-permute-start(f32[4,256]{1,0:T(4,128)S(1)} %get-tuple-element.28), channel_id=1, source_target_pairs={{0,2},{1,3},{2,0},{3,1},{4,6},{5,7},{6,4},{7,5},{8,10},{9,11},{10,... | collective-permute-start | bytes 12296 | tf_op jit(solution)/shard_map/ppermute | solution.py:290
  133.5 3.0 %collective-permute-start.25 = (f32[4,256]{1,0:T(4,128)S(1)}, f32[4,256]{1,0:T(4,128)S(1)}, u32[]{:S(2)}, u32[]{:S(2)}) collective-permute-start(f32[4,256]{1,0:T(4,128)S(1)} %get-tuple-element.29), channel_id=1, source_target_pairs={{0,3},{1,2},{2,1},{3,0},{4,7},{5,6},{6,5},{7,4},{8,11},{9,10},{10,... | collective-permute-start | bytes 12296 | tf_op jit(solution)/shard_map/ppermute | solution.py:290

commit v2 on v1

v2 whole, which is shorter than its diff:
```python
import functools

import jax
import jax.numpy as jnp
from jax import lax
from jax.experimental import pallas as pl
from jax.experimental.pallas import tpu as pltpu
from jax.sharding import PartitionSpec as P

SEQ_LEN = 2048
EPS = 1e-06
LOW = -1e30
TILE = 256
EXTRA = 16
AXES = ("vocab", "width")
VMEM = pl.BlockSpec(memory_space=pltpu.VMEM)
SMEM = pl.BlockSpec(memory_space=pltpu.SMEM)
HBM = pl.BlockSpec(memory_space=pltpu.HBM)


class Plan:
    def __init__(self, mesh, rows, columns):
        self.V, self.W = mesh.shape["vocab"], mesh.shape["width"]
        self.X = 1
        while 4 * self.X * self.X <= self.V:
            self.X *= 2
        self.Z = self.V // self.X
        self.rows = rows
        self.part = rows // self.W
        self.blocks = SEQ_LEN // rows
        self.columns = columns

    def perm(self, move):
        return [
            (v * self.W + w, t * self.W + u)
            for v in range(self.V)
            for w in range(self.W)
            for t, u in [move(v, w)]
        ]

    def width_xor(self, k):
        return self.perm(lambda v, w: (v, w ^ k))

    def vocab_xor(self, k):
        return self.perm(lambda v, w: (v ^ k, w))

    def z_ring(self):
        return self.perm(lambda v, w: ((v + self.X) % self.V, w))

    def x_ring(self):
        return self.perm(lambda v, w: (v - v % self.X + (v + 1) % self.X, w))


def quarter(plan, v, w):
    return lax.rem(w + v, plan.W)


def id_rows(plan, ids_ref, w, target):
    out = []
    for h in range(plan.blocks):
        q = quarter(plan, w * plan.blocks + h, target)
        start = pl.multiple_of((h * plan.W + q) * plan.part, plan.part)
        out.append(ids_ref[pl.ds(start, plan.part)].reshape(1, plan.part))
    return out


def send_kernel(plan, h_ref, gain_hbm, ids_hbm, *refs):
    outs, (gain_ref, ids_ref, sems) = refs[: plan.W], refs[plan.W :]
    v, w = lax.axis_index("vocab"), lax.axis_index("width")
    part = plan.part
    small = [
        pltpu.make_async_copy(gain_hbm, gain_ref, sems.at[0]),
        pltpu.make_async_copy(ids_hbm, ids_ref, sems.at[1]),
    ]
    for copy in small:
        copy.start()
    large = []
    for k in range(plan.W):
        start = pl.multiple_of(quarter(plan, v, w ^ k) * part, part)
        large.append(pltpu.make_async_copy(h_ref.at[pl.ds(start, part)], outs[k].at[pl.ds(0, part)], sems.at[2 + k]))
        large[-1].start()
    for copy in small:
        copy.wait()
    gain = gain_ref[...].reshape(1, gain_ref.shape[0])
    high = gain.astype(jnp.bfloat16).astype(jnp.float32)
    rest = gain - high
    middle = rest.astype(jnp.bfloat16).astype(jnp.float32)
    low = rest - middle
    width = gain.shape[1]
    for k in range(plan.W):
        rows = [high, middle, low]
        for line in id_rows(plan, ids_ref, w, w ^ k):
            upper = line // 256
            for piece in (upper, line - upper * 256):
                piece = piece.astype(jnp.float32)
                if part < width:
                    piece = jnp.concatenate([piece, jnp.zeros((1, width - part), jnp.float32)], axis=1)
                rows.append(piece[:, :width])
        rows.append(jnp.zeros((EXTRA - len(rows), width), jnp.float32))
        outs[k][part:, :] = jnp.concatenate(rows, axis=0).astype(jnp.bfloat16)
    for copy in large:
        copy.wait()


def norm_kernel(plan, depth, *refs):
    pieces, (out_ref, out_ids) = refs[: plan.W], refs[plan.W :]
    part, width = plan.part, depth // plan.W
    wide, gains = [], []
    for k in range(plan.W):
        wide.append(pieces[k][:part, :].astype(jnp.float32))
        extra = pieces[k][part:, :].astype(jnp.float32)
        gains.append((extra[0:1] + extra[1:2]) + extra[2:3])
        for h in range(plan.blocks):
            upper = extra[3 + 2 * h : 4 + 2 * h].astype(jnp.int32)
            under = extra[4 + 2 * h : 5 + 2 * h].astype(jnp.int32)
            row = k * plan.blocks + h
            out_ids[row : row + 1, :] = (upper * 256 + under)[:, :part]
    total = sum(jnp.sum(x * x, axis=1, keepdims=True) for x in wide)
    scale = lax.rsqrt(total / depth + EPS)
    for k in range(plan.W):
        normed = (wide[k] * scale * gains[k]).T
        out_ref[k * width : (k + 1) * width, :] = normed.astype(jnp.bfloat16)


def main_kernel(plan, jobs, sizes, bases, have, last, places, halves, where, offsets, seq_ref, ids_ref, *refs):
    refs = list(refs)
    take = lambda n: [refs.pop(0) for _ in range(n)]
    W, part = plan.W, plan.part
    groups = [take(n) for n in halves]
    held = take(max(where) + 1)
    chunks = [[held[i] for i in where[c * W : (c + 1) * W]] for c in range(len(sizes))]
    states = [take(1)[0] if h else None for h in have]
    outs = take(1 if last else len(jobs))
    buffers = take(2)
    v, w = lax.axis_index("vocab"), lax.axis_index("width")
    z, x = v // plan.X, lax.rem(v, plan.X)
    lane = (8, part)
    for g, mine in enumerate(jobs):
        dz, dx = places[g]
        source = lax.rem(z - dz + plan.Z, plan.Z) * plan.X + lax.rem(x - dx + plan.X, plan.X)
        s, h = source // plan.blocks, lax.rem(source, plan.blocks)
        first = h * plan.rows + quarter(plan, source, w) * part
        live = seq_ref[s] > first
        rank = (s ^ w) * plan.blocks + h

        def run(state):
            ids = jnp.broadcast_to(ids_ref[pl.ds(rank, 1), :], lane)
            ids = ids - lax.broadcasted_iota(jnp.int32, lane, 0) - v * plan.columns

            def right():
                held = [ref[...] for ref in groups[g]]
                return held[0] if len(held) == 1 else jnp.concatenate(held, axis=0)

            def dot(c, start, size):
                left = jnp.concatenate(
                    [ref[off + start : off + start + size, :] for ref, off in zip(chunks[c], offsets[c])], axis=1
                )
                return jnp.dot(left, right(), preferred_element_type=jnp.float32)

            def fold(state, buffer, size, base):
                m, e_sum, l_sum, target = state
                n = size // 8
                logits = buffer[:size, :].reshape((n,) + lane)
                top = jnp.maximum(m, jnp.max(logits, axis=0))
                scale = jnp.exp(m - top)
                terms = jnp.exp(logits - top[None])
                e_sum = e_sum * scale + jnp.sum(terms, axis=0)
                l_sum = l_sum * scale + jnp.sum(terms * logits, axis=0)
                there = ids - base
                for i in range(n):
                    target = jnp.where(there == 8 * i, logits[i], target)
                return top, e_sum, l_sum, target

            tiles = [(c, at, min(TILE, sizes[c] - at)) for c in mine for at in range(0, sizes[c], TILE)]
            buffers[0][: tiles[0][2], :] = dot(*tiles[0])
            for i, (c, at, size) in enumerate(tiles):
                if i + 1 < len(tiles):
                    buffers[1 - i % 2][: tiles[i + 1][2], :] = dot(*tiles[i + 1])
                state = fold(state, buffers[i % 2], size, bases[c] + at)
            return state

        def start_state():
            if have[g]:
                return tuple(states[g][i] for i in range(4))
            zero = jnp.zeros(lane, jnp.float32)
            return jnp.full(lane, LOW, jnp.float32), zero, zero, zero

        state = lax.cond(live, lambda: run(start_state()), start_state) if mine else start_state()
        if not last:
            for i in range(4):
                outs[g][i] = state[i]
            continue
        m, e_sum, l_sum, target = state
        top = jnp.max(m, axis=0, keepdims=True)
        scale = jnp.exp(m - top)
        lines = [top] + [jnp.sum(a, axis=0, keepdims=True) for a in (e_sum * scale, l_sum * scale, target)]
        for i, line in enumerate(lines):
            outs[0][i, pl.ds(source, 1), :] = line


def merge(parts):
    top = functools.reduce(jnp.maximum, [p[0] for p in parts])
    scales = [jnp.exp(p[0] - top) for p in parts]
    e_sum = sum(p[1] * c for p, c in zip(parts, scales))
    l_sum = sum(p[2] * c for p, c in zip(parts, scales))
    return top, e_sum, l_sum, sum(p[3] for p in parts)


def read(ref):
    return [ref[i] for i in range(4)]


def results(stats):
    top, e_sum, l_sum, target = stats
    logsum = top + jnp.log(e_sum)
    return target - logsum, logsum - l_sum / e_sum


def merge_kernel(count, *refs):
    for i, value in enumerate(merge([read(ref) for ref in refs[:count]])):
        refs[count][i] = value


def split_kernel(plan, count, *refs):
    mine, other = refs[count:]
    upper = lax.axis_index("width") // 2 == 1
    half = plan.V // 2
    for i, value in enumerate(merge([read(ref) for ref in refs[:count]])):
        mine[i] = jnp.where(upper, value[half:], value[:half])
        other[i] = jnp.where(upper, value[:half], value[half:])


def pair_kernel(plan, a_ref, b_ref, c_ref, d_ref, keep_ref, pass_ref):
    odd = lax.rem(lax.axis_index("width"), 2) == 1
    blocks = plan.blocks
    for n, (one, two) in enumerate(((a_ref, b_ref), (c_ref, d_ref))):
        for i, value in enumerate(results(merge([read(one), read(two)]))):
            rows = slice((2 * n + i) * blocks, (2 * n + i + 1) * blocks)
            keep_ref[rows, :] = jnp.where(odd, value[blocks:], value[:blocks])
            pass_ref[rows, :] = jnp.where(odd, value[:blocks], value[blocks:])


def close_kernel(plan, count, *refs):
    outs, held = refs[count:-1], refs[-1]
    w = lax.axis_index("width")
    for i, value in enumerate(results(merge([read(ref) for ref in refs[:count]]))):
        held[i] = value
    for k in range(plan.W):
        for h in range(plan.blocks):
            for i in range(2):
                row = i * plan.blocks + h
                outs[k][row : row + 1, :] = held[i, pl.ds((w ^ k) * plan.blocks + h, 1), :]


def place_kernel(plan, count, order, seq_ref, *refs):
    pieces, outs = refs[:count], refs[count:]
    w = lax.axis_index("width")
    length = seq_ref[w]
    column = lax.broadcasted_iota(jnp.int32, (1, plan.part), 1)
    sets = len(order) // count
    for n, k in enumerate(order):
        for h in range(plan.blocks):
            q = quarter(plan, w * plan.blocks + h, w ^ k)
            live = column + (h * plan.rows + q * plan.part) < length
            start = pl.multiple_of((h * plan.W + q) * plan.part, plan.part)
            for i in range(2):
                row = (2 * (n % sets) + i) * plan.blocks + h
                value = jnp.where(live, pieces[n // sets][row : row + 1, :], 0.0)
                outs[i][pl.ds(start, plan.part)] = value.reshape(plan.part)


def call(kernel, out_shape, args, smem, scratch=(), flops=0, name=None, far=0, limit=12):
    return pl.pallas_call(
        kernel,
        out_shape=out_shape,
        in_specs=[SMEM] * smem + [HBM] * far + [VMEM] * (len(args) - smem - far),
        out_specs=jax.tree.map(lambda _: VMEM, out_shape),
        scratch_shapes=list(scratch),
        compiler_params=pltpu.CompilerParams(vmem_limit_bytes=limit * 2**20),
        cost_estimate=pl.CostEstimate(flops=flops, bytes_accessed=2**20, transcendentals=0),
        name=name,
    )(*args)


def chunk_spans(columns, shares=(0.32, 0.64)):
    ends = [0] + [TILE * round(columns * share / TILE) for share in shares] + [columns]
    return [(a, b - a) for a, b in zip(ends, ends[1:])]


def tie(*values):
    return lax.optimization_barrier(values)


def on_device(mesh, hidden, norm_gain, head_weight, token_ids, seq_lengths):
    rows, width = hidden.shape
    columns = head_weight.shape[1]
    plan = Plan(mesh, rows, columns)
    W, part, blocks = plan.W, plan.part, plan.blocks
    depth = width * W
    shape = jax.ShapeDtypeStruct
    move = lambda value, perm: lax.ppermute(value, AXES, perm)

    sent = call(
        functools.partial(send_kernel, plan),
        [shape((part + EXTRA, width), jnp.bfloat16)] * W,
        (hidden, norm_gain, token_ids),
        0,
        scratch=[
            pltpu.VMEM((width,), jnp.float32),
            pltpu.VMEM(token_ids.shape, jnp.int32),
            pltpu.SemaphoreType.DMA((2 + W,)),
        ],
        name="send",
        far=3,
        limit=56,
    )
    pieces = {k: move(sent[k], plan.width_xor(k)) for k in sorted(range(1, W), key=lambda k: (k != 1, -k))}
    pieces = [sent[0]] + [pieces[k] for k in range(1, W)]
    normed, all_ids = call(
        functools.partial(norm_kernel, plan, depth),
        [shape((depth, part), jnp.bfloat16), shape((W * blocks, part), jnp.int32)],
        pieces,
        0,
        name="norm",
    )

    spans = chunk_spans(columns)
    weight = head_weight.T
    bits = [1 << i for i in range(W.bit_length() - 1)]
    near = move(weight, plan.width_xor(1))

    def far_chunk(c, after):
        a, n = spans[c]
        held = {0: tie(weight[a : a + n], *after)[0]}
        for bit in reversed(bits[1:]):
            for k in list(held):
                held[k | bit] = move(held[k], plan.width_xor(bit))
        return held

    def near_chunk(c, held):
        start, size = spans[c]
        cut = size // 32 * 16
        for at, count in ((0, cut), (cut, size - cut)):
            refs = {0: (weight, start + at), 1: (near, start + at)}
            for k in held:
                if k:
                    refs[k] = (held[k], at)
                    refs[k | 1] = (move(held[k][at : at + count], plan.width_xor(1)), 0)
            chunks.append([refs[k] for k in range(W)])
            parts.append((start + at, count))

    states, groups, chunks, parts, done = {}, {}, [], [], {}

    def stage(wanted, last=False):
        jobs = {key: [c for c in mine if c not in done.get(key, [])] for key, mine in wanted.items()}
        done.update(wanted)
        keys = list(jobs)
        used = sorted({c for mine in jobs.values() for c in mine})
        have = [key in states for key in keys]
        sizes, bases = [parts[c][1] for c in used], [parts[c][0] for c in used]
        args = [seq_lengths, all_ids] + [part for key in keys if jobs[key] for part in groups[key]]
        halves = [len(groups[key]) if jobs[key] else 0 for key in keys]
        held = [chunks[c][k][0] for c in used for k in range(W)]
        offsets = [[chunks[c][k][1] for k in range(W)] for c in used]
        unique = [held[i] for i in range(len(held)) if all(held[i] is not held[j] for j in range(i))]
        where = [next(j for j in range(len(unique)) if unique[j] is one) for one in held]
        args += unique
        args += [states[key] for key in keys if key in states]
        if last:
            out = [shape((4, plan.V, part), jnp.float32)]
        else:
            out = [shape((4, 8, part), jnp.float32)] * len(keys)
        work = sum(parts[c][1] for mine in jobs.values() for c in mine)
        got = call(
            functools.partial(
                main_kernel, plan, [[used.index(c) for c in jobs[key]] for key in keys], sizes, bases, have, last, keys,
                halves, where,
                offsets
            ),
            out,
            args,
            1,
            scratch=[pltpu.VMEM((TILE, part), jnp.float32)] * 2,
            flops=2 * work * part * depth,
            name="logits",
        )
        if last:
            return got[0]
        states.update(zip(keys, got))

    groups[0, 0] = [normed]
    ring, far = normed, {}
    fast = plan.X == 2 and plan.Z == 4
    for dz in range(plan.Z):
        end = dz == plan.Z - 1
        onward, arrived, tied = [], {}, {}
        if not end:
            onward = [move(ring, plan.z_ring())]
        if end and plan.X == 2:
            half = depth // 2
            arrived[dz, 1] = [
                move(ring[:half], plan.x_ring()),
                move(groups[dz - 1, 1][0][half:], plan.z_ring()),
            ]
        else:
            passed = ring
            for dx in range(1, plan.X):
                passed = move(passed, plan.x_ring())
                arrived[dz, dx] = [passed]
        if dz < len(spans):
            tied["far"] = far_chunk(dz, pieces[-1:])
        if far:
            near_chunk(dz - 1, far)
            if fast:
                stage({key: list(range(len(chunks))) for key in groups})
                tied["states"] = states
        onward, arrived, tied = lax.optimization_barrier((onward, arrived, tied))
        states = tied.get("states", states)
        far = tied.get("far", {})
        groups.update(arrived)
        if not end:
            ring = onward[0]
            groups[dz + 1, 0] = onward
    stats = stage({key: list(range(len(chunks))) for key in groups}, last=True)

    levels = [1 << i for i in range(plan.V.bit_length() - 1)]
    if W == 4 and plan.V == 8:
        parts = [stats] + [move(stats, plan.vocab_xor(k)) for k in (1, 2, 3)]
        mine, other = call(
            functools.partial(split_kernel, plan, 4),
            [shape((4, plan.V // 2, part), jnp.float32)] * 2,
            parts,
            0,
            name="split",
        )
        arrived = [
            move(other, plan.width_xor(2)),
            move(mine, plan.vocab_xor(4)),
            move(other, plan.perm(lambda v, w: (v ^ 4, w ^ 2))),
        ]
        keep, passed = call(
            functools.partial(pair_kernel, plan),
            [shape((4 * blocks, part), jnp.float32)] * 2,
            (mine, arrived[1], arrived[0], arrived[2]),
            0,
            name="pair",
        )
        closed, order = [keep, move(passed, plan.width_xor(1))], (0, 2, 1, 3)
    else:
        rounds = [levels[i : i + 2] for i in range(0, len(levels), 2)]
        for i, level in enumerate(rounds):
            others = [level[0]] if len(level) == 1 else [level[0], level[1], level[0] | level[1]]
            parts = [stats] + [move(stats, plan.vocab_xor(k)) for k in others]
            if i + 1 < len(rounds):
                stats = call(
                    functools.partial(merge_kernel, len(parts)), shape(stats.shape, jnp.float32), parts, 0, name="merge"
                )
        closed = call(
            functools.partial(close_kernel, plan, len(parts)),
            [shape((2 * blocks, part), jnp.float32)] * W,
            parts,
            0,
            scratch=[pltpu.VMEM((2, plan.V, part), jnp.float32)],
            name="close",
        )
        closed = [closed[0]] + [move(closed[k], plan.width_xor(k)) for k in range(1, W)]
        order = tuple(range(W))
    return tuple(
        call(
            functools.partial(place_kernel, plan, len(closed), order),
            [shape(token_ids.shape, jnp.float32)] * 2,
            (seq_lengths, *closed),
            1,
            name="place",
        )
    )


def solution(mesh):
    in_specs = (P("vocab", "width"), P("width"), P("width", "vocab"), P("width"), P())
    out_specs = (P("width"), P("width"))
    return jax.shard_map(
        functools.partial(on_device, mesh), mesh=mesh, in_specs=in_specs, out_specs=out_specs, check_vma=False
    )
```

time: 139 us -> 101 us (0.73); the launches traced: 138 us -> 102 us
  waiting for transfers between devices: 89.1 us -> 41.9 us
  Pallas kernels: 17.3 us -> 25.2 us
  starting transfers between devices: 26 us -> 32.2 us
  local copies, waits for them, and re-layouts: 5.14 us -> 1.72 us
    ppermute x26 -> x28, waiting for transfers between devices: 89.1 us -> 41.9 us  [on_device(): move = lambda value, perm: lax.ppermute(value, AXES, perm)]
    pallas_call x6 -> x9, Pallas kernels: 17.3 us -> 25.2 us  [call(): pl.pallas_call(kernel, out_shape=out_shape, in_specs=[SMEM] * smem + [HBM...]
    ppermute x26 -> x28, starting transfers between devices: 26 us -> 32.2 us  [on_device(): move = lambda value, perm: lax.ppermute(value, AXES, perm)]
    unnamed x10 -> x6, local copies, waits for them, and re-layouts: 2.94 us -> 0.01 us
  transfers between devices with their start and end apart: 26 -> 28, of which waited for: 16 -> 13; matrix products, arithmetic and copies ran while one was open for 1% -> 2% of each run, Pallas kernels for 0% -> 21%
where the time goes in v2:
time: 101 us; the launch traced here: 102 us
  waiting for transfers between devices  41.9 us (41%)
  starting transfers between devices  32.2 us (32%)
  Pallas kernels  25.2 us (25%)
  local copies, waits for them, and re-layouts  1.72 us (2%)
    ppermute x28, waiting for transfers between devices, on_device(): move = lambda value, perm: lax.ppermute(value, AXES, perm)  41.9 us
    ppermute x28, starting transfers between devices, on_device(): move = lambda value, perm: lax.ppermute(value, AXES, perm)  32.2 us
    pallas_call x9, Pallas kernels, call(): pl.pallas_call(kernel, out_shape=out_shape, in_specs=[SMEM] * smem + [HBM...  25.2 us
  transfers between devices with their start and end apart: 28, of which 13 were waited for; matrix products, arithmetic and copies ran while one was open for 2% of the time, Pallas kernels for 21%

profile of v2, /device:TPU:0, one launch (start us, length us, event | category | flops | bytes accessed | tf_op | source)
XLA Modules:
  0.0 101.8 jit_solution(7087739941919177108)
XLA Ops:
  0.6 2.0 %send.1 = (bf16[272,256]{1,0:T(8,128)(2,1)}, bf16[272,256]{1,0:T(8,128)(2,1)}, bf16[272,256]{1,0:T(8,128)(2,1)}, bf16[272,256]{1,0:T(8,128)(2,1)}) custom-call(bf16[1024,256]{1,0:T(8,128)(2,1)} %h_ref.1, f32[256]{0:T(256)} %gain_hbm.1, s32[2048]{0:T(1024)} %ids_hbm.1), custom_call_target="tpu_custom_call" | custom-call | bytes 1048576 | tf_op jit(solution)/shard_map/send/pallas_call | solution.py:273
  2.7 2.5 %collective-permute-start.2 = (bf16[272,256]{1,0:T(8,128)(2,1)}, bf16[272,256]{1,0:T(8,128)(2,1)S(1)}, u32[]{:S(2)}, u32[]{:S(2)}) collective-permute-start(bf16[272,256]{1,0:T(8,128)(2,1)} %get-tuple-element.59), channel_id=1, source_target_pairs={{0,3},{1,2},{2,1},{3,0},{4,7},{5,6},{6,5},{7,4},{8,11},{9,10},{10,... | collective-permute-start | bytes 417800 | tf_op jit(solution)/shard_map/ppermute | solution.py:301
  5.1 0.7 collective-permute-start
  5.8 0.0 collective-permute-start.1
  5.9 0.2 collective-permute-start.9
  6.0 1.5 %fusion = (bf16[1280,256]{1,0:T(8,128)(2,1)S(1)}, bf16[1280,256]{1,0:T(8,128)(2,1)S(1)}) fusion(bf16[4016,256]{1,0:T(8,128)(2,1)} %bitcast.2), kind=kLoop, calls=%fused_computation | loop fusion | bytes 2621440 | tf_op jit(solution)/shard_map/slice | solution.py:334
  7.5 2.0 %collective-permute-done.2.refs_3_ = bf16[272,256]{1,0:T(8,128)(2,1)S(1)} collective-permute-done((bf16[272,256]{1,0:T(8,128)(2,1)}, bf16[272,256]{1,0:T(8,128)(2,1)S(1)}, u32[]{:S(2)}, u32[]{:S(2)}) %collective-permute-start.2) | collective-permute-done | bytes 139296 | tf_op jit(solution)/shard_map/ppermute | solution.py:301
  9.5 2.3 %collective-permute-start.5 = (bf16[1280,256]{1,0:T(8,128)(2,1)S(1)}, bf16[1280,256]{1,0:T(8,128)(2,1)S(1)}, u32[]{:S(2)}, u32[]{:S(2)}) collective-permute-start(bf16[1280,256]{1,0:T(8,128)(2,1)S(1)} %get-tuple-element.62), channel_id=1, source_target_pairs={{0,2},{1,3},{2,0},{3,1},{4,6},{5,7},{6,4},{7,5},{8,10},{9,11},{10,... | collective-permute-start | bytes 1966088 | tf_op jit(solution)/shard_map/ppermute | solution.py:301
  11.9 0.7 collective-permute-done.1.refs_2_
  12.6 0.4 norm.1
  13.0 2.5 %collective-permute-start.3 = (bf16[1024,256]{1,0:T(8,128)(2,1)S(1)}, bf16[1024,256]{1,0:T(8,128)(2,1)S(1)}, u32[]{:S(2)}, u32[]{:S(2)}) collective-permute-start(bf16[1024,256]{1,0:T(8,128)(2,1)S(1)} %get-tuple-element.61.refs_0_), channel_id=1, source_target_pairs={{0,8},{1,9},{2,10},{3,11},{4,12},{5,13},{6,14},{7,15},{8,16},{9,17... | collective-permute-start | bytes 1572872 | tf_op jit(solution)/shard_map/ppermute | solution.py:301
  15.5 1.5 %collective-permute-start.4 = (bf16[1024,256]{1,0:T(8,128)(2,1)S(1)}, bf16[1024,256]{1,0:T(8,128)(2,1)S(1)}, u32[]{:S(2)}, u32[]{:S(2)}) collective-permute-start(bf16[1024,256]{1,0:T(8,128)(2,1)S(1)} %get-tuple-element.61.refs_0_), channel_id=1, source_target_pairs={{0,4},{1,5},{2,6},{3,7},{4,0},{5,1},{6,2},{7,3},{8,12},{9,13},{10,... | collective-permute-start | bytes 1572872 | tf_op jit(solution)/shard_map/ppermute | solution.py:301
  17.0 12.6 %collective-permute-done.3.refs_2_ = bf16[1024,256]{1,0:T(8,128)(2,1)S(1)} collective-permute-done((bf16[1024,256]{1,0:T(8,128)(2,1)S(1)}, bf16[1024,256]{1,0:T(8,128)(2,1)S(1)}, u32[]{:S(2)}, u32[]{:S(2)}) %collective-permute-start.3) | collective-permute-done | bytes 524320 | tf_op jit(solution)/shard_map/ppermute | solution.py:301
  29.6 0.1 collective-permute-start.10
  29.7 1.6 %collective-permute-start.8 = (bf16[1280,256]{1,0:T(8,128)(2,1)S(1)}, bf16[1280,256]{1,0:T(8,128)(2,1)S(1)}, u32[]{:S(2)}, u32[]{:S(2)}) collective-permute-start(bf16[1280,256]{1,0:T(8,128)(2,1)S(1)} %get-tuple-element.64), channel_id=1, source_target_pairs={{0,2},{1,3},{2,0},{3,1},{4,6},{5,7},{6,4},{7,5},{8,10},{9,11},{10,... | collective-permute-start | bytes 1966088 | tf_op jit(solution)/shard_map/ppermute | solution.py:301
  31.3 1.0 collective-permute-start.6
  32.3 1.5 %collective-permute-start.7 = (bf16[1024,256]{1,0:T(8,128)(2,1)S(1)}, bf16[1024,256]{1,0:T(8,128)(2,1)S(1)}, u32[]{:S(2)}, u32[]{:S(2)}) collective-permute-start(bf16[1024,256]{1,0:T(8,128)(2,1)S(1)} %collective-permute-done.3.refs_2_), channel_id=1, source_target_pairs={{0,4},{1,5},{2,6},{3,7},{4,0},{5,1},{6,2},{7,3},{8,12},{9,13},{10,... | collective-permute-start | bytes 1572872 | tf_op jit(solution)/shard_map/ppermute | solution.py:301
  33.8 1.6 %collective-permute-done.11.refs_7_.refs_9_.refs_11_.refs_6_ = bf16[640,256]{1,0:T(8,128)(2,1)S(1)} collective-permute-done((bf16[640,256]{1,0:T(8,128)(2,1)S(1)}, bf16[640,256]{1,0:T(8,128)(2,1)S(1)}, u32[]{:S(2)}, u32[]{:S(2)}) %collective-permute-start.11) | collective-permute-done | bytes 327712 | tf_op jit(solution)/shard_map/ppermute | solution.py:301
  35.5 3.6 %logits.4 = (f32[4,8,256]{2,1,0:T(8,128)S(1)}, f32[4,8,256]{2,1,0:T(8,128)S(1)}, f32[4,8,256]{2,1,0:T(8,128)S(1)}) custom-call(s32[4]{0:T(128)S(1)} %copy-done.2, s32[8,256]{1,0:T(8,128)S(1)} %get-tuple-element.60.ids_ref, bf16[1024,256]{1,0:T(8,128)(2,1)S(1)} %get-tuple-element.61.refs_0_, bf16[1024,256]{1,0:T(8,128)(2,1)S(1)} %collective-permute-done.4.refs_1_, ...), custom_call_target="tpu_custom_call" | custom-call | flops 2013265920 | bytes 1048576 | tf_op jit(solution)/shard_map/logits/pallas_call | solution.py:273
  39.1 7.7 %collective-permute-done.8.refs_10_.refs_12_.refs_7_ = bf16[1280,256]{1,0:T(8,128)(2,1)S(1)} collective-permute-done((bf16[1280,256]{1,0:T(8,128)(2,1)S(1)}, bf16[1280,256]{1,0:T(8,128)(2,1)S(1)}, u32[]{:S(2)}, u32[]{:S(2)}) %collective-permute-start.8) | collective-permute-done | bytes 655392 | tf_op jit(solution)/shard_map/ppermute | solution.py:301
  46.8 0.3 collective-permute-done.6.refs_4_
  47.2 0.1 collective-permute-start.15
  47.2 0.5 collective-permute-start.16
  47.8 1.4 %collective-permute-start.14 = (bf16[1456,256]{1,0:T(8,128)(2,1)S(1)}, bf16[1456,256]{1,0:T(8,128)(2,1)S(1)}, u32[]{:S(2)}, u32[]{:S(2)}) collective-permute-start(bf16[1456,256]{1,0:T(8,128)(2,1)S(1)} %slice.46), channel_id=1, source_target_pairs={{0,2},{1,3},{2,0},{3,1},{4,6},{5,7},{6,4},{7,5},{8,10},{9,11},{10,... | collective-permute-start | bytes 2236424 | tf_op jit(solution)/shard_map/ppermute | solution.py:301
  49.2 1.0 collective-permute-start.12
  50.2 1.5 %collective-permute-start.13 = (bf16[1024,256]{1,0:T(8,128)(2,1)S(1)}, bf16[1024,256]{1,0:T(8,128)(2,1)S(1)}, u32[]{:S(2)}, u32[]{:S(2)}) collective-permute-start(bf16[1024,256]{1,0:T(8,128)(2,1)S(1)} %collective-permute-done.6.refs_4_), channel_id=1, source_target_pairs={{0,4},{1,5},{2,6},{3,7},{4,0},{5,1},{6,2},{7,3},{8,12},{9,13},{10,... | collective-permute-start | bytes 1572872 | tf_op jit(solution)/shard_map/ppermute | solution.py:301
  51.7 7.5 %logits.5 = (f32[4,8,256]{2,1,0:T(8,128)S(1)}, f32[4,8,256]{2,1,0:T(8,128)S(1)}, f32[4,8,256]{2,1,0:T(8,128)S(1)}, f32[4,8,256]{2,1,0:T(8,128)S(1)}, f32[4,8,256]{2,1,0:T(8,128)S(1)}) custom-call(s32[4]{0:T(128)S(1)} %copy-done.2, s32[8,256]{1,0:T(8,128)S(1)} %get-tuple-element.60.ids_ref, bf16[1024,256]{1,0:T(8,128)(2,1)S(1)} %get-tuple-element.61.refs_0_, ...), custom_call_target="tpu_custom_call" | custom-call | flops 4697620480 | bytes 1048576 | tf_op jit(solution)/shard_map/logits/pallas_call | solution.py:273
  59.1 7.4 %collective-permute-done.14.refs_15_.refs_10_ = bf16[1456,256]{1,0:T(8,128)(2,1)S(1)} collective-permute-done((bf16[1456,256]{1,0:T(8,128)(2,1)S(1)}, bf16[1456,256]{1,0:T(8,128)(2,1)S(1)}, u32[]{:S(2)}, u32[]{:S(2)}) %collective-permute-start.14) | collective-permute-done | bytes 745504 | tf_op jit(solution)/shard_map/ppermute | solution.py:301
  66.5 0.1 collective-permute-start.20
  66.7 0.6 collective-permute-start.19
  67.2 1.6 %collective-permute-start.17 = (bf16[512,256]{1,0:T(8,128)(2,1)S(1)}, bf16[512,256]{1,0:T(8,128)(2,1)S(1)}, u32[]{:S(2)}, u32[]{:S(2)}) collective-permute-start(bf16[512,256]{1,0:T(8,128)(2,1)S(1)} %slice.40), channel_id=1, source_target_pairs={{0,4},{1,5},{2,6},{3,7},{4,0},{5,1},{6,2},{7,3},{8,12},{9,13},{10,... | collective-permute-start | bytes 786440 | tf_op jit(solution)/shard_map/ppermute | solution.py:301
  68.8 0.8 collective-permute-start.18
  69.6 9.6 %logits.6 = (f32[4,8,256]{2,1,0:T(8,128)S(1)}, f32[4,8,256]{2,1,0:T(8,128)S(1)}, f32[4,8,256]{2,1,0:T(8,128)S(1)}, f32[4,8,256]{2,1,0:T(8,128)S(1)}, f32[4,8,256...) custom-call(s32[4]{0:T(128)S(1)} %copy-done.2, s32[8,256]{1,0:T(8,128)S(1)} %get-tuple-element.60.ids_ref, ...), custom_call_target="tpu_custom_call" | custom-call | flops 8027897856 | bytes 1048576 | tf_op jit(solution)/shard_map/logits/pallas_call | solution.py:273
  79.2 0.9 logits.7.refs_0_
  80.1 0.8 collective-permute-start.21
  80.9 4.7 %collective-permute-start.22 = (f32[4,8,256]{2,1,0:T(8,128)S(1)}, f32[4,8,256]{2,1,0:T(8,128)S(1)}, u32[]{:S(2)}, u32[]{:S(2)}) collective-permute-start(f32[4,8,256]{2,1,0:T(8,128)S(1)} %logits.7.refs_0_), channel_id=1, source_target_pairs={{0,8},{1,9},{2,10},{3,11},{4,12},{5,13},{6,14},{7,15},{8,0},{9,1},... | collective-permute-start | bytes 98312 | tf_op jit(solution)/shard_map/ppermute | solution.py:301
  85.5 0.9 collective-permute-start.23
  86.5 1.0 collective-permute-done.22.refs_2_
  87.4 2.9 %collective-permute-done.23.refs_3_ = f32[4,8,256]{2,1,0:T(8,128)S(1)} collective-permute-done((f32[4,8,256]{2,1,0:T(8,128)S(1)}, f32[4,8,256]{2,1,0:T(8,128)S(1)}, u32[]{:S(2)}, u32[]{:S(2)}) %collective-permute-start.23) | collective-permute-done | bytes 32800 | tf_op jit(solution)/shard_map/ppermute | solution.py:301
  90.4 0.5 collective-permute-start.24
  90.8 3.0 %collective-permute-start.25 = (f32[4,4,256]{2,1,0:T(4,128)S(1)}, f32[4,4,256]{2,1,0:T(4,128)S(1)}, u32[]{:S(2)}, u32[]{:S(2)}) collective-permute-start(f32[4,4,256]{2,1,0:T(4,128)S(1)} %get-tuple-element.107), channel_id=1, source_target_pairs={{0,2},{1,3},{2,0},{3,1},{4,6},{5,7},{6,4},{7,5},{8,10},{9,11},{10,... | collective-permute-start | bytes 49160 | tf_op jit(solution)/shard_map/ppermute | solution.py:301
  93.8 1.0 collective-permute-start.26
  94.8 0.2 collective-permute-done.24.b_ref
  95.1 0.5 collective-permute-done.25.c_ref
  95.6 3.8 %collective-permute-done.26.d_ref = f32[4,4,256]{2,1,0:T(4,128)S(1)} collective-permute-done((f32[4,4,256]{2,1,0:T(4,128)S(1)}, f32[4,4,256]{2,1,0:T(4,128)S(1)}, u32[]{:S(2)}, u32[]{:S(2)}) %collective-permute-start.26) | collective-permute-done | bytes 16416 | tf_op jit(solution)/shard_map/ppermute | solution.py:301
  99.4 0.1 collective-permute-start.27
  99.5 1.2 %collective-permute-done.27.refs_1_ = f32[8,256]{1,0:T(8,128)S(1)} collective-permute-done((f32[8,256]{1,0:T(8,128)S(1)}, f32[8,256]{1,0:T(8,128)S(1)}, u32[]{:S(2)}, u32[]{:S(2)}) %collective-permute-start.27) | collective-permute-done | bytes 8224 | tf_op jit(solution)/shard_map/ppermute | solution.py:301
  100.7 1.2 %place.1 = (f32[2048]{0:T(1024)}, f32[2048]{0:T(1024)}) custom-call(s32[4]{0:T(128)S(1)} %copy-done.2, f32[8,256]{1,0:T(8,128)S(1)} %get-tuple-element.108.refs_0_, f32[8,256]{1,0:T(8,128)S(1)} %collective-permute-done.27.refs_1_), custom_call_target="tpu_custom_call" | custom-call | bytes 1048576 | tf_op jit(solution)/shard_map/place/pallas_call | solution.py:273
  (31 shorter events, 0.3 us)
Async XLA Ops:
  2.7 9.9 %copy-start.1 = (bf16[272,256]{1,0:T(8,128)(2,1)S(1)}, bf16[272,256]{1,0:T(8,128)(2,1)}, u32[]{:S(2)}) copy-start(bf16[272,256]{1,0:T(8,128)(2,1)} %get-tuple-element.56.refs_0_) | copy-start | bytes 417796
  2.7 6.9 %collective-permute-start.2 = (bf16[272,256]{1,0:T(8,128)(2,1)}, bf16[272,256]{1,0:T(8,128)(2,1)S(1)}, u32[]{:S(2)}, u32[]{:S(2)}) collective-permute-start(bf16[272,256]{1,0:T(8,128)(2,1)} %get-tuple-element.59), channel_id=1, source_target_pairs={{0,3},{1,2},{2,1},{3,0},{4,7},{5,6},{6,5},{7,4},{8,11},{9,10},{10,... | collective-permute-start | bytes 417800 | tf_op jit(solution)/shard_map/ppermute | solution.py:301
  5.1 6.7 %collective-permute-start = (bf16[272,256]{1,0:T(8,128)(2,1)}, bf16[272,256]{1,0:T(8,128)(2,1)S(1)}, u32[]{:S(2)}, u32[]{:S(2)}) collective-permute-start(bf16[272,256]{1,0:T(8,128)(2,1)} %get-tuple-element.57), channel_id=1, source_target_pairs={{0,1},{1,0},{2,3},{3,2},{4,5},{5,4},{6,7},{7,6},{8,9},{9,8},{10,11... | collective-permute-start | bytes 417800 | tf_op jit(solution)/shard_map/ppermute | solution.py:301
  5.8 6.8 %collective-permute-start.1 = (bf16[272,256]{1,0:T(8,128)(2,1)}, bf16[272,256]{1,0:T(8,128)(2,1)S(1)}, u32[]{:S(2)}, u32[]{:S(2)}) collective-permute-start(bf16[272,256]{1,0:T(8,128)(2,1)} %get-tuple-element.58), channel_id=1, source_target_pairs={{0,2},{1,3},{2,0},{3,1},{4,6},{5,7},{6,4},{7,5},{8,10},{9,11},{10,... | collective-permute-start | bytes 417800 | tf_op jit(solution)/shard_map/ppermute | solution.py:301
  5.9 29.6 %copy-start = (bf16[256,4016]{0,1:T(8,128)(2,1)S(1)}, bf16[256,4016]{0,1:T(8,128)(2,1)}, u32[]{:S(2)}) copy-start(bf16[256,4016]{0,1:T(8,128)(2,1)} %param.7) | copy-start | bytes 6168580
  5.9 29.6 %copy-start.2 = (s32[4]{0:T(128)S(1)}, s32[4]{0:T(128)}, u32[]{:S(2)}) copy-start(s32[4]{0:T(128)} %seq_ref.9) | copy-start | bytes 52
  5.9 29.6 %collective-permute-start.9 = (bf16[4016,256]{1,0:T(8,128)(2,1)}, bf16[4016,256]{1,0:T(8,128)(2,1)S(1)}, u32[]{:S(2)}, u32[]{:S(2)}) collective-permute-start(bf16[4016,256]{1,0:T(8,128)(2,1)} %bitcast.1), channel_id=1, source_target_pairs={{0,1},{1,0},{2,3},{3,2},{4,5},{5,4},{6,7},{7,6},{8,9},{9,8},{10,11... | collective-permute-start | bytes 6168584 | tf_op jit(solution)/shard_map/ppermute | solution.py:301
  9.5 20.0 %collective-permute-start.5 = (bf16[1280,256]{1,0:T(8,128)(2,1)S(1)}, bf16[1280,256]{1,0:T(8,128)(2,1)S(1)}, u32[]{:S(2)}, u32[]{:S(2)}) collective-permute-start(bf16[1280,256]{1,0:T(8,128)(2,1)S(1)} %get-tuple-element.62), channel_id=1, source_target_pairs={{0,2},{1,3},{2,0},{3,1},{4,6},{5,7},{6,4},{7,5},{8,10},{9,11},{10,... | collective-permute-start | bytes 1966088 | tf_op jit(solution)/shard_map/ppermute | solution.py:301
  13.0 16.6 %collective-permute-start.3 = (bf16[1024,256]{1,0:T(8,128)(2,1)S(1)}, bf16[1024,256]{1,0:T(8,128)(2,1)S(1)}, u32[]{:S(2)}, u32[]{:S(2)}) collective-permute-start(bf16[1024,256]{1,0:T(8,128)(2,1)S(1)} %get-tuple-element.61.refs_0_), channel_id=1, source_target_pairs={{0,8},{1,9},{2,10},{3,11},{4,12},{5,13},{6,14},{7,15},{8,16},{9,17... | collective-permute-start | bytes 1572872 | tf_op jit(solution)/shard_map/ppermute | solution.py:301
  15.5 14.1 %collective-permute-start.4 = (bf16[1024,256]{1,0:T(8,128)(2,1)S(1)}, bf16[1024,256]{1,0:T(8,128)(2,1)S(1)}, u32[]{:S(2)}, u32[]{:S(2)}) collective-permute-start(bf16[1024,256]{1,0:T(8,128)(2,1)S(1)} %get-tuple-element.61.refs_0_), channel_id=1, source_target_pairs={{0,4},{1,5},{2,6},{3,7},{4,0},{5,1},{6,2},{7,3},{8,12},{9,13},{10,... | collective-permute-start | bytes 1572872 | tf_op jit(solution)/shard_map/ppermute | solution.py:301
  29.6 4.2 %collective-permute-start.10 = (bf16[640,256]{1,0:T(8,128)(2,1)S(1)}, bf16[640,256]{1,0:T(8,128)(2,1)S(1)}, u32[]{:S(2)}, u32[]{:S(2)}) collective-permute-start(bf16[640,256]{1,0:T(8,128)(2,1)S(1)} %get-tuple-element.115), channel_id=1, source_target_pairs={{0,1},{1,0},{2,3},{3,2},{4,5},{5,4},{6,7},{7,6},{8,9},{9,8},{10,11... | collective-permute-start | bytes 983048 | tf_op jit(solution)/shard_map/ppermute | solution.py:301
  29.7 17.1 %collective-permute-start.8 = (bf16[1280,256]{1,0:T(8,128)(2,1)S(1)}, bf16[1280,256]{1,0:T(8,128)(2,1)S(1)}, u32[]{:S(2)}, u32[]{:S(2)}) collective-permute-start(bf16[1280,256]{1,0:T(8,128)(2,1)S(1)} %get-tuple-element.64), channel_id=1, source_target_pairs={{0,2},{1,3},{2,0},{3,1},{4,6},{5,7},{6,4},{7,5},{8,10},{9,11},{10,... | collective-permute-start | bytes 1966088 | tf_op jit(solution)/shard_map/ppermute | solution.py:301
  31.3 15.8 %collective-permute-start.6 = (bf16[1024,256]{1,0:T(8,128)(2,1)S(1)}, bf16[1024,256]{1,0:T(8,128)(2,1)S(1)}, u32[]{:S(2)}, u32[]{:S(2)}) collective-permute-start(bf16[1024,256]{1,0:T(8,128)(2,1)S(1)} %collective-permute-done.3.refs_2_), channel_id=1, source_target_pairs={{0,8},{1,9},{2,10},{3,11},{4,12},{5,13},{6,14},{7,15},{8,16},{9,17... | collective-permute-start | bytes 1572872 | tf_op jit(solution)/shard_map/ppermute | solution.py:301
  32.3 14.8 %collective-permute-start.7 = (bf16[1024,256]{1,0:T(8,128)(2,1)S(1)}, bf16[1024,256]{1,0:T(8,128)(2,1)S(1)}, u32[]{:S(2)}, u32[]{:S(2)}) collective-permute-start(bf16[1024,256]{1,0:T(8,128)(2,1)S(1)} %collective-permute-done.3.refs_2_), channel_id=1, source_target_pairs={{0,4},{1,5},{2,6},{3,7},{4,0},{5,1},{6,2},{7,3},{8,12},{9,13},{10,... | collective-permute-start | bytes 1572872 | tf_op jit(solution)/shard_map/ppermute | solution.py:301
  33.8 1.6 %collective-permute-start.11 = (bf16[640,256]{1,0:T(8,128)(2,1)S(1)}, bf16[640,256]{1,0:T(8,128)(2,1)S(1)}, u32[]{:S(2)}, u32[]{:S(2)}) collective-permute-start(bf16[640,256]{1,0:T(8,128)(2,1)S(1)} %get-tuple-element.114), channel_id=1, source_target_pairs={{0,1},{1,0},{2,3},{3,2},{4,5},{5,4},{6,7},{7,6},{8,9},{9,8},{10,11... | collective-permute-start | bytes 983048 | tf_op jit(solution)/shard_map/ppermute | solution.py:301
  47.2 4.5 %collective-permute-start.15 = (bf16[640,256]{1,0:T(8,128)(2,1)S(1)}, bf16[640,256]{1,0:T(8,128)(2,1)S(1)}, u32[]{:S(2)}, u32[]{:S(2)}) collective-permute-start(bf16[640,256]{1,0:T(8,128)(2,1)S(1)} %get-tuple-element.113), channel_id=1, source_target_pairs={{0,1},{1,0},{2,3},{3,2},{4,5},{5,4},{6,7},{7,6},{8,9},{9,8},{10,11... | collective-permute-start | bytes 983048 | tf_op jit(solution)/shard_map/ppermute | solution.py:301
  47.2 4.4 %collective-permute-start.16 = (bf16[640,256]{1,0:T(8,128)(2,1)S(1)}, bf16[640,256]{1,0:T(8,128)(2,1)S(1)}, u32[]{:S(2)}, u32[]{:S(2)}) collective-permute-start(bf16[640,256]{1,0:T(8,128)(2,1)S(1)} %get-tuple-element.112), channel_id=1, source_target_pairs={{0,1},{1,0},{2,3},{3,2},{4,5},{5,4},{6,7},{7,6},{8,9},{9,8},{10,11... | collective-permute-start | bytes 983048 | tf_op jit(solution)/shard_map/ppermute | solution.py:301
  47.8 18.7 %collective-permute-start.14 = (bf16[1456,256]{1,0:T(8,128)(2,1)S(1)}, bf16[1456,256]{1,0:T(8,128)(2,1)S(1)}, u32[]{:S(2)}, u32[]{:S(2)}) collective-permute-start(bf16[1456,256]{1,0:T(8,128)(2,1)S(1)} %slice.46), channel_id=1, source_target_pairs={{0,2},{1,3},{2,0},{3,1},{4,6},{5,7},{6,4},{7,5},{8,10},{9,11},{10,... | collective-permute-start | bytes 2236424 | tf_op jit(solution)/shard_map/ppermute | solution.py:301
  49.2 17.4 %collective-permute-start.12 = (bf16[1024,256]{1,0:T(8,128)(2,1)S(1)}, bf16[1024,256]{1,0:T(8,128)(2,1)S(1)}, u32[]{:S(2)}, u32[]{:S(2)}) collective-permute-start(bf16[1024,256]{1,0:T(8,128)(2,1)S(1)} %collective-permute-done.6.refs_4_), channel_id=1, source_target_pairs={{0,8},{1,9},{2,10},{3,11},{4,12},{5,13},{6,14},{7,15},{8,16},{9,17... | collective-permute-start | bytes 1572872 | tf_op jit(solution)/shard_map/ppermute | solution.py:301
  50.2 16.4 %collective-permute-start.13 = (bf16[1024,256]{1,0:T(8,128)(2,1)S(1)}, bf16[1024,256]{1,0:T(8,128)(2,1)S(1)}, u32[]{:S(2)}, u32[]{:S(2)}) collective-permute-start(bf16[1024,256]{1,0:T(8,128)(2,1)S(1)} %collective-permute-done.6.refs_4_), channel_id=1, source_target_pairs={{0,4},{1,5},{2,6},{3,7},{4,0},{5,1},{6,2},{7,3},{8,12},{9,13},{10,... | collective-permute-start | bytes 1572872 | tf_op jit(solution)/shard_map/ppermute | solution.py:301
  66.5 3.0 %collective-permute-start.20 = (bf16[736,256]{1,0:T(8,128)(2,1)S(1)}, bf16[736,256]{1,0:T(8,128)(2,1)S(1)}, u32[]{:S(2)}, u32[]{:S(2)}) collective-permute-start(bf16[736,256]{1,0:T(8,128)(2,1)S(1)} %slice.43), channel_id=1, source_target_pairs={{0,1},{1,0},{2,3},{3,2},{4,5},{5,4},{6,7},{7,6},{8,9},{9,8},{10,11... | collective-permute-start | bytes 1130504 | tf_op jit(solution)/shard_map/ppermute | solution.py:301
  66.7 2.9 %collective-permute-start.19 = (bf16[720,256]{1,0:T(8,128)(2,1)S(1)}, bf16[720,256]{1,0:T(8,128)(2,1)S(1)}, u32[]{:S(2)}, u32[]{:S(2)}) collective-permute-start(bf16[720,256]{1,0:T(8,128)(2,1)S(1)} %slice.42), channel_id=1, source_target_pairs={{0,1},{1,0},{2,3},{3,2},{4,5},{5,4},{6,7},{7,6},{8,9},{9,8},{10,11... | collective-permute-start | bytes 1105928 | tf_op jit(solution)/shard_map/ppermute | solution.py:301
  67.2 11.9 %collective-permute-start.17 = (bf16[512,256]{1,0:T(8,128)(2,1)S(1)}, bf16[512,256]{1,0:T(8,128)(2,1)S(1)}, u32[]{:S(2)}, u32[]{:S(2)}) collective-permute-start(bf16[512,256]{1,0:T(8,128)(2,1)S(1)} %slice.40), channel_id=1, source_target_pairs={{0,4},{1,5},{2,6},{3,7},{4,0},{5,1},{6,2},{7,3},{8,12},{9,13},{10,... | collective-permute-start | bytes 786440 | tf_op jit(solution)/shard_map/ppermute | solution.py:301
  68.8 10.4 %collective-permute-start.18 = (bf16[512,256]{1,0:T(8,128)(2,1)S(1)}, bf16[512,256]{1,0:T(8,128)(2,1)S(1)}, u32[]{:S(2)}, u32[]{:S(2)}) collective-permute-start(bf16[512,256]{1,0:T(8,128)(2,1)S(1)} %slice.41), channel_id=1, source_target_pairs={{0,8},{1,9},{2,10},{3,11},{4,12},{5,13},{6,14},{7,15},{8,16},{9,17... | collective-permute-start | bytes 786440 | tf_op jit(solution)/shard_map/ppermute | solution.py:301
  80.1 6.4 %collective-permute-start.21 = (f32[4,8,256]{2,1,0:T(8,128)S(1)}, f32[4,8,256]{2,1,0:T(8,128)S(1)}, u32[]{:S(2)}, u32[]{:S(2)}) collective-permute-start(f32[4,8,256]{2,1,0:T(8,128)S(1)} %logits.7.refs_0_), channel_id=1, source_target_pairs={{0,4},{1,5},{2,6},{3,7},{4,0},{5,1},{6,2},{7,3},{8,12},{9,13},{10,... | collective-permute-start | bytes 98312 | tf_op jit(solution)/shard_map/ppermute | solution.py:301
  80.9 6.6 %collective-permute-start.22 = (f32[4,8,256]{2,1,0:T(8,128)S(1)}, f32[4,8,256]{2,1,0:T(8,128)S(1)}, u32[]{:S(2)}, u32[]{:S(2)}) collective-permute-start(f32[4,8,256]{2,1,0:T(8,128)S(1)} %logits.7.refs_0_), channel_id=1, source_target_pairs={{0,8},{1,9},{2,10},{3,11},{4,12},{5,13},{6,14},{7,15},{8,0},{9,1},... | collective-permute-start | bytes 98312 | tf_op jit(solution)/shard_map/ppermute | solution.py:301
  85.5 4.8 %collective-permute-start.23 = (f32[4,8,256]{2,1,0:T(8,128)S(1)}, f32[4,8,256]{2,1,0:T(8,128)S(1)}, u32[]{:S(2)}, u32[]{:S(2)}) collective-permute-start(f32[4,8,256]{2,1,0:T(8,128)S(1)} %logits.7.refs_0_), channel_id=1, source_target_pairs={{0,12},{1,13},{2,14},{3,15},{4,8},{5,9},{6,10},{7,11},{8,4},{9,5},... | collective-permute-start | bytes 98312 | tf_op jit(solution)/shard_map/ppermute | solution.py:301
  90.4 4.7 %collective-permute-start.24 = (f32[4,4,256]{2,1,0:T(4,128)S(1)}, f32[4,4,256]{2,1,0:T(4,128)S(1)}, u32[]{:S(2)}, u32[]{:S(2)}) collective-permute-start(f32[4,4,256]{2,1,0:T(4,128)S(1)} %get-tuple-element.106.a_ref), channel_id=1, source_target_pairs={{0,16},{1,17},{2,18},{3,19},{4,20},{5,21},{6,22},{7,23},{8,24},{9,... | collective-permute-start | bytes 49160 | tf_op jit(solution)/shard_map/ppermute | solution.py:301
  90.8 4.7 %collective-permute-start.25 = (f32[4,4,256]{2,1,0:T(4,128)S(1)}, f32[4,4,256]{2,1,0:T(4,128)S(1)}, u32[]{:S(2)}, u32[]{:S(2)}) collective-permute-start(f32[4,4,256]{2,1,0:T(4,128)S(1)} %get-tuple-element.107), channel_id=1, source_target_pairs={{0,2},{1,3},{2,0},{3,1},{4,6},{5,7},{6,4},{7,5},{8,10},{9,11},{10,... | collective-permute-start | bytes 49160 | tf_op jit(solution)/shard_map/ppermute | solution.py:301
  93.8 5.5 %collective-permute-start.26 = (f32[4,4,256]{2,1,0:T(4,128)S(1)}, f32[4,4,256]{2,1,0:T(4,128)S(1)}, u32[]{:S(2)}, u32[]{:S(2)}) collective-permute-start(f32[4,4,256]{2,1,0:T(4,128)S(1)} %get-tuple-element.107), channel_id=1, source_target_pairs={{0,18},{1,19},{2,16},{3,17},{4,22},{5,23},{6,20},{7,21},{8,26},{9,... | collective-permute-start | bytes 49160 | tf_op jit(solution)/shard_map/ppermute | solution.py:301
  99.4 1.2 %collective-permute-start.27 = (f32[8,256]{1,0:T(8,128)S(1)}, f32[8,256]{1,0:T(8,128)S(1)}, u32[]{:S(2)}, u32[]{:S(2)}) collective-permute-start(f32[8,256]{1,0:T(8,128)S(1)} %get-tuple-element.109), channel_id=1, source_target_pairs={{0,1},{1,0},{2,3},{3,2},{4,5},{5,4},{6,7},{7,6},{8,9},{9,8},{10,11... | collective-permute-start | bytes 24584 | tf_op jit(solution)/shard_map/ppermute | solution.py:301

commit v3 on v2

--- a/solution.py
+++ b/solution.py
@@ -12,6 +12,7 @@
 LOW = -1e30
 TILE = 256
 EXTRA = 16
+NEAR = 1024
 AXES = ("vocab", "width")
 VMEM = pl.BlockSpec(memory_space=pltpu.VMEM)
 SMEM = pl.BlockSpec(memory_space=pltpu.SMEM)
@@ -171,7 +172,7 @@
                     target = jnp.where(there == 8 * i, logits[i], target)
                 return top, e_sum, l_sum, target
 
-            tiles = [(c, at, min(TILE, sizes[c] - at)) for c in mine for at in range(0, sizes[c], TILE)]
+            tiles = [(c, at, size) for c in mine for at, size in even(sizes[c], TILE)]
             buffers[0][: tiles[0][2], :] = dot(*tiles[0])
             for i, (c, at, size) in enumerate(tiles):
                 if i + 1 < len(tiles):
@@ -230,7 +231,7 @@
         other[i] = jnp.where(upper, value[:half], value[half:])
 
 
-def pair_kernel(plan, a_ref, b_ref, c_ref, d_ref, keep_ref, pass_ref):
+def pair_kernel(plan, d_ref, b_ref, c_ref, a_ref, keep_ref, pass_ref):
     odd = lax.rem(lax.axis_index("width"), 2) == 1
     blocks = plan.blocks
     for n, (one, two) in enumerate(((a_ref, b_ref), (c_ref, d_ref))):
@@ -282,9 +283,14 @@
     )(*args)
 
 
-def chunk_spans(columns, shares=(0.32, 0.64)):
-    ends = [0] + [TILE * round(columns * share / TILE) for share in shares] + [columns]
+def chunk_spans(columns, shares=(0.32, 0.733)):
+    ends = [0] + [64 * round(columns * share / 64) for share in shares] + [columns]
     return [(a, b - a) for a, b in zip(ends, ends[1:])]
+
+
+def even(size, most):
+    step = -(-size // (16 * -(-size // most))) * 16
+    return [(at, min(step, size - at)) for at in range(0, size, step)]
 
 
 def tie(*values):
@@ -303,7 +309,7 @@
     sent = call(
         functools.partial(send_kernel, plan),
         [shape((part + EXTRA, width), jnp.bfloat16)] * W,
-        (hidden, norm_gain, token_ids),
+        [pltpu.with_memory_space_constraint(x, pltpu.HBM) for x in (hidden, norm_gain, token_ids)],
         0,
         scratch=[
             pltpu.VMEM((width,), jnp.float32),
@@ -312,7 +318,6 @@
         ],
         name="send",
         far=3,
-        limit=56,
     )
     pieces = {k: move(sent[k], plan.width_xor(k)) for k in sorted(range(1, W), key=lambda k: (k != 1, -k))}
     pieces = [sent[0]] + [pieces[k] for k in range(1, W)]
@@ -339,8 +344,7 @@
 
     def near_chunk(c, held):
         start, size = spans[c]
-        cut = size // 32 * 16
-        for at, count in ((0, cut), (cut, size - cut)):
+        for at, count in even(size, NEAR):
             refs = {0: (weight, start + at), 1: (near, start + at)}
             for k in held:
                 if k:
@@ -425,7 +429,7 @@
 
     levels = [1 << i for i in range(plan.V.bit_length() - 1)]
     if W == 4 and plan.V == 8:
-        parts = [stats] + [move(stats, plan.vocab_xor(k)) for k in (1, 2, 3)]
+        parts = [stats] + [move(stats, plan.vocab_xor(k)) for k in (3, 2, 1)]
         mine, other = call(
             functools.partial(split_kernel, plan, 4),
             [shape((4, plan.V // 2, part), jnp.float32)] * 2,
@@ -434,14 +438,14 @@
             name="split",
         )
         arrived = [
+            move(other, plan.perm(lambda v, w: (v ^ 4, w ^ 2))),
+            move(mine, plan.vocab_xor(4)),
             move(other, plan.width_xor(2)),
-            move(mine, plan.vocab_xor(4)),
-            move(other, plan.perm(lambda v, w: (v ^ 4, w ^ 2))),
         ]
         keep, passed = call(
             functools.partial(pair_kernel, plan),
             [shape((4 * blocks, part), jnp.float32)] * 2,
-            (mine, arrived[1], arrived[0], arrived[2]),
+            (*arrived, mine),
             0,
             name="pair",
         )

time: 101 us -> 93.5 us (0.926); the launches traced: 102 us -> 93.3 us
  waiting for transfers between devices: 41.9 us -> 33.7 us
  starting transfers between devices: 32.2 us -> 31.1 us
    ppermute x28, waiting for transfers between devices: 41.9 us -> 33.7 us  [on_device(): move = lambda value, perm: lax.ppermute(value, AXES, perm)]
    ppermute x28, starting transfers between devices: 32.2 us -> 31.1 us  [on_device(): move = lambda value, perm: lax.ppermute(value, AXES, perm)]
    pallas_call x9, Pallas kernels: 25.2 us -> 26.2 us  [call(): pl.pallas_call(kernel, out_shape=out_shape, in_specs=[SMEM] * smem + [HBM...]
  transfers between devices with their start and end apart: 28 -> 28, of which waited for: 13 -> 14; matrix products, arithmetic and copies ran while one was open for 2% -> 1% of each run, Pallas kernels for 21% -> 25%
where the time goes in v3:
time: 93.5 us; the launch traced here: 93.3 us
  waiting for transfers between devices  33.7 us (36%)
  starting transfers between devices  31.1 us (33%)
  Pallas kernels  26.2 us (28%)
  local copies, waits for them, and re-layouts  1.41 us (2%)
    ppermute x28, waiting for transfers between devices, on_device(): move = lambda value, perm: lax.ppermute(value, AXES, perm)  33.7 us
    ppermute x28, starting transfers between devices, on_device(): move = lambda value, perm: lax.ppermute(value, AXES, perm)  31.1 us
    pallas_call x9, Pallas kernels, call(): pl.pallas_call(kernel, out_shape=out_shape, in_specs=[SMEM] * smem + [HBM...  26.2 us
  transfers between devices with their start and end apart: 28, of which 14 were waited for; matrix products, arithmetic and copies ran while one was open for 1% of the time, Pallas kernels for 25%

profile of v3, /device:TPU:0, one launch (start us, length us, event | category | flops | bytes accessed | tf_op | source)
XLA Modules:
  0.0 93.3 jit_solution(13414980020658600786)
XLA Ops:
  0.6 0.5 collective-permute-start.9
  1.2 1.3 %send.1 = (bf16[272,256]{1,0:T(8,128)(2,1)S(1)}, bf16[272,256]{1,0:T(8,128)(2,1)S(1)}, bf16[272,256]{1,0:T(8,128)(2,1)S(1)}, bf16[272,256]{1,0:T(8,128)(2,1)S(1)}) custom-call(bf16[1024,256]{1,0:T(8,128)(2,1)} %h_ref.1, f32[256]{0:T(256)} %gain_hbm.1, s32[2048]{0:T(1024)} %ids_hbm.1), custom_call_target="tpu_custom_call" | custom-call | bytes 1048576 | tf_op jit(solution)/shard_map/send/pallas_call | solution.py:274
  2.4 2.6 %collective-permute-start.2 = (bf16[272,256]{1,0:T(8,128)(2,1)S(1)}, bf16[272,256]{1,0:T(8,128)(2,1)S(1)}, u32[]{:S(2)}, u32[]{:S(2)}) collective-permute-start(bf16[272,256]{1,0:T(8,128)(2,1)S(1)} %get-tuple-element.59), channel_id=1, source_target_pairs={{0,3},{1,2},{2,1},{3,0},{4,7},{5,6},{6,5},{7,4},{8,11},{9,10},{10,... | collective-permute-start | bytes 417800 | tf_op jit(solution)/shard_map/ppermute | solution.py:307
  5.0 0.2 collective-permute-start
  5.2 0.3 collective-permute-start.1
  5.5 1.1 %slice.44 = bf16[1280,256]{1,0:T(8,128)(2,1)S(1)} slice(bf16[4016,256]{1,0:T(8,128)(2,1)} %bitcast.2), slice={[0:1280], [0:256]} | slice | bytes 1310720 | tf_op jit(solution)/shard_map/slice | solution.py:339
  6.7 2.4 %collective-permute-done.2.refs_3_ = bf16[272,256]{1,0:T(8,128)(2,1)S(1)} collective-permute-done((bf16[272,256]{1,0:T(8,128)(2,1)S(1)}, bf16[272,256]{1,0:T(8,128)(2,1)S(1)}, u32[]{:S(2)}, u32[]{:S(2)}) %collective-permute-start.2) | collective-permute-done | bytes 139296 | tf_op jit(solution)/shard_map/ppermute | solution.py:307
  9.0 1.6 %collective-permute-start.5 = (bf16[1280,256]{1,0:T(8,128)(2,1)S(1)}, bf16[1280,256]{1,0:T(8,128)(2,1)S(1)}, u32[]{:S(2)}, u32[]{:S(2)}) collective-permute-start(bf16[1280,256]{1,0:T(8,128)(2,1)S(1)} %slice.44), channel_id=1, source_target_pairs={{0,2},{1,3},{2,0},{3,1},{4,6},{5,7},{6,4},{7,5},{8,10},{9,11},{10,... | collective-permute-start | bytes 1966088 | tf_op jit(solution)/shard_map/ppermute | solution.py:307
  10.6 1.7 %collective-permute-done.1.refs_2_ = bf16[272,256]{1,0:T(8,128)(2,1)S(1)} collective-permute-done((bf16[272,256]{1,0:T(8,128)(2,1)S(1)}, bf16[272,256]{1,0:T(8,128)(2,1)S(1)}, u32[]{:S(2)}, u32[]{:S(2)}) %collective-permute-start.1) | collective-permute-done | bytes 139296 | tf_op jit(solution)/shard_map/ppermute | solution.py:307
  12.3 0.4 norm.1
  12.7 1.9 %collective-permute-start.3 = (bf16[1024,256]{1,0:T(8,128)(2,1)S(1)}, bf16[1024,256]{1,0:T(8,128)(2,1)S(1)}, u32[]{:S(2)}, u32[]{:S(2)}) collective-permute-start(bf16[1024,256]{1,0:T(8,128)(2,1)S(1)} %get-tuple-element.61.refs_0_), channel_id=1, source_target_pairs={{0,8},{1,9},{2,10},{3,11},{4,12},{5,13},{6,14},{7,15},{8,16},{9,17... | collective-permute-start | bytes 1572872 | tf_op jit(solution)/shard_map/ppermute | solution.py:307
  14.6 1.5 %collective-permute-start.4 = (bf16[1024,256]{1,0:T(8,128)(2,1)S(1)}, bf16[1024,256]{1,0:T(8,128)(2,1)S(1)}, u32[]{:S(2)}, u32[]{:S(2)}) collective-permute-start(bf16[1024,256]{1,0:T(8,128)(2,1)S(1)} %get-tuple-element.61.refs_0_), channel_id=1, source_target_pairs={{0,4},{1,5},{2,6},{3,7},{4,0},{5,1},{6,2},{7,3},{8,12},{9,13},{10,... | collective-permute-start | bytes 1572872 | tf_op jit(solution)/shard_map/ppermute | solution.py:307
  16.2 1.6 %collective-permute-start.8 = (bf16[1664,256]{1,0:T(8,128)(2,1)S(1)}, bf16[1664,256]{1,0:T(8,128)(2,1)S(1)}, u32[]{:S(2)}, u32[]{:S(2)}) collective-permute-start(bf16[1664,256]{1,0:T(8,128)(2,1)S(1)} %slice.45), channel_id=1, source_target_pairs={{0,2},{1,3},{2,0},{3,1},{4,6},{5,7},{6,4},{7,5},{8,10},{9,11},{10,... | collective-permute-start | bytes 2555912 | tf_op jit(solution)/shard_map/ppermute | solution.py:307
  17.7 10.6 %collective-permute-done.3.refs_2_ = bf16[1024,256]{1,0:T(8,128)(2,1)S(1)} collective-permute-done((bf16[1024,256]{1,0:T(8,128)(2,1)S(1)}, bf16[1024,256]{1,0:T(8,128)(2,1)S(1)}, u32[]{:S(2)}, u32[]{:S(2)}) %collective-permute-start.3) | collective-permute-done | bytes 524320 | tf_op jit(solution)/shard_map/ppermute | solution.py:307
  28.4 0.1 collective-permute-start.10
  28.5 1.1 %collective-permute-start.6 = (bf16[1024,256]{1,0:T(8,128)(2,1)S(1)}, bf16[1024,256]{1,0:T(8,128)(2,1)S(1)}, u32[]{:S(2)}, u32[]{:S(2)}) collective-permute-start(bf16[1024,256]{1,0:T(8,128)(2,1)S(1)} %collective-permute-done.3.refs_2_), channel_id=1, source_target_pairs={{0,8},{1,9},{2,10},{3,11},{4,12},{5,13},{6,14},{7,15},{8,16},{9,17... | collective-permute-start | bytes 1572872 | tf_op jit(solution)/shard_map/ppermute | solution.py:307
  29.5 1.5 %collective-permute-start.7 = (bf16[1024,256]{1,0:T(8,128)(2,1)S(1)}, bf16[1024,256]{1,0:T(8,128)(2,1)S(1)}, u32[]{:S(2)}, u32[]{:S(2)}) collective-permute-start(bf16[1024,256]{1,0:T(8,128)(2,1)S(1)} %collective-permute-done.3.refs_2_), channel_id=1, source_target_pairs={{0,4},{1,5},{2,6},{3,7},{4,0},{5,1},{6,2},{7,3},{8,12},{9,13},{10,... | collective-permute-start | bytes 1572872 | tf_op jit(solution)/shard_map/ppermute | solution.py:307
  31.0 1.6 %collective-permute-done.11.refs_7_.refs_9_.refs_11_.refs_6_ = bf16[640,256]{1,0:T(8,128)(2,1)S(1)} collective-permute-done((bf16[640,256]{1,0:T(8,128)(2,1)S(1)}, bf16[640,256]{1,0:T(8,128)(2,1)S(1)}, u32[]{:S(2)}, u32[]{:S(2)}) %collective-permute-start.11) | collective-permute-done | bytes 327712 | tf_op jit(solution)/shard_map/ppermute | solution.py:307
  32.7 3.7 %logits.4 = (f32[4,8,256]{2,1,0:T(8,128)S(1)}, f32[4,8,256]{2,1,0:T(8,128)S(1)}, f32[4,8,256]{2,1,0:T(8,128)S(1)}) custom-call(s32[4]{0:T(128)S(1)} %copy-done.1, s32[8,256]{1,0:T(8,128)S(1)} %get-tuple-element.60.ids_ref, bf16[1024,256]{1,0:T(8,128)(2,1)S(1)} %get-tuple-element.61.refs_0_, bf16[1024,256]{1,0:T(8,128)(2,1)S(1)} %collective-permute-done.4.refs_1_, ...), custom_call_target="tpu_custom_call" | custom-call | flops 2013265920 | bytes 1048576 | tf_op jit(solution)/shard_map/logits/pallas_call | solution.py:274
  36.3 8.2 %collective-permute-done.8.refs_10_.refs_12_.refs_7_ = bf16[1664,256]{1,0:T(8,128)(2,1)S(1)} collective-permute-done((bf16[1664,256]{1,0:T(8,128)(2,1)S(1)}, bf16[1664,256]{1,0:T(8,128)(2,1)S(1)}, u32[]{:S(2)}, u32[]{:S(2)}) %collective-permute-start.8) | collective-permute-done | bytes 852000 | tf_op jit(solution)/shard_map/ppermute | solution.py:307
  44.7 0.1 collective-permute-start.15
  44.7 0.5 collective-permute-start.16
  45.3 1.8 %collective-permute-start.14 = (bf16[1072,256]{1,0:T(8,128)(2,1)S(1)}, bf16[1072,256]{1,0:T(8,128)(2,1)S(1)}, u32[]{:S(2)}, u32[]{:S(2)}) collective-permute-start(bf16[1072,256]{1,0:T(8,128)(2,1)S(1)} %slice.46), channel_id=1, source_target_pairs={{0,2},{1,3},{2,0},{3,1},{4,6},{5,7},{6,4},{7,5},{8,10},{9,11},{10,... | collective-permute-start | bytes 1646600 | tf_op jit(solution)/shard_map/ppermute | solution.py:307
  47.1 1.6 %collective-permute-start.12 = (bf16[1024,256]{1,0:T(8,128)(2,1)S(1)}, bf16[1024,256]{1,0:T(8,128)(2,1)S(1)}, u32[]{:S(2)}, u32[]{:S(2)}) collective-permute-start(bf16[1024,256]{1,0:T(8,128)(2,1)S(1)} %collective-permute-done.6.refs_4_), channel_id=1, source_target_pairs={{0,8},{1,9},{2,10},{3,11},{4,12},{5,13},{6,14},{7,15},{8,16},{9,17... | collective-permute-start | bytes 1572872 | tf_op jit(solution)/shard_map/ppermute | solution.py:307
  48.7 1.5 %collective-permute-start.13 = (bf16[1024,256]{1,0:T(8,128)(2,1)S(1)}, bf16[1024,256]{1,0:T(8,128)(2,1)S(1)}, u32[]{:S(2)}, u32[]{:S(2)}) collective-permute-start(bf16[1024,256]{1,0:T(8,128)(2,1)S(1)} %collective-permute-done.6.refs_4_), channel_id=1, source_target_pairs={{0,4},{1,5},{2,6},{3,7},{4,0},{5,1},{6,2},{7,3},{8,12},{9,13},{10,... | collective-permute-start | bytes 1572872 | tf_op jit(solution)/shard_map/ppermute | solution.py:307
  50.2 8.7 %logits.5 = (f32[4,8,256]{2,1,0:T(8,128)S(1)}, f32[4,8,256]{2,1,0:T(8,128)S(1)}, f32[4,8,256]{2,1,0:T(8,128)S(1)}, f32[4,8,256]{2,1,0:T(8,128)S(1)}, f32[4,8,256]{2,1,0:T(8,128)S(1)}) custom-call(s32[4]{0:T(128)S(1)} %copy-done.1, s32[8,256]{1,0:T(8,128)S(1)} %get-tuple-element.60.ids_ref, bf16[1024,256]{1,0:T(8,128)(2,1)S(1)} %get-tuple-element.61.refs_0_, ...), custom_call_target="tpu_custom_call" | custom-call | flops 5704253440 | bytes 1048576 | tf_op jit(solution)/shard_map/logits/pallas_call | solution.py:274
  58.8 0.9 %collective-permute-done.14.refs_15_.refs_10_ = bf16[1072,256]{1,0:T(8,128)(2,1)S(1)} collective-permute-done((bf16[1072,256]{1,0:T(8,128)(2,1)S(1)}, bf16[1072,256]{1,0:T(8,128)(2,1)S(1)}, u32[]{:S(2)}, u32[]{:S(2)}) %collective-permute-start.14) | collective-permute-done | bytes 548896 | tf_op jit(solution)/shard_map/ppermute | solution.py:307
  59.8 2.8 %collective-permute-done.12.refs_6_ = bf16[1024,256]{1,0:T(8,128)(2,1)S(1)} collective-permute-done((bf16[1024,256]{1,0:T(8,128)(2,1)S(1)}, bf16[1024,256]{1,0:T(8,128)(2,1)S(1)}, u32[]{:S(2)}, u32[]{:S(2)}) %collective-permute-start.12) | collective-permute-done | bytes 524320 | tf_op jit(solution)/shard_map/ppermute | solution.py:307
  62.6 0.1 collective-permute-start.19
  62.7 0.6 collective-permute-start.20
  63.3 1.6 %collective-permute-start.17 = (bf16[512,256]{1,0:T(8,128)(2,1)S(1)}, bf16[512,256]{1,0:T(8,128)(2,1)S(1)}, u32[]{:S(2)}, u32[]{:S(2)}) collective-permute-start(bf16[512,256]{1,0:T(8,128)(2,1)S(1)} %slice.40), channel_id=1, source_target_pairs={{0,4},{1,5},{2,6},{3,7},{4,0},{5,1},{6,2},{7,3},{8,12},{9,13},{10,... | collective-permute-start | bytes 786440 | tf_op jit(solution)/shard_map/ppermute | solution.py:307
  64.9 1.1 %collective-permute-start.18 = (bf16[512,256]{1,0:T(8,128)(2,1)S(1)}, bf16[512,256]{1,0:T(8,128)(2,1)S(1)}, u32[]{:S(2)}, u32[]{:S(2)}) collective-permute-start(bf16[512,256]{1,0:T(8,128)(2,1)S(1)} %slice.41), channel_id=1, source_target_pairs={{0,8},{1,9},{2,10},{3,11},{4,12},{5,13},{6,14},{7,15},{8,16},{9,17... | collective-permute-start | bytes 786440 | tf_op jit(solution)/shard_map/ppermute | solution.py:307
  65.9 10.4 %logits.6 = (f32[4,8,256]{2,1,0:T(8,128)S(1)}, f32[4,8,256]{2,1,0:T(8,128)S(1)}, f32[4,8,256]{2,1,0:T(8,128)S(1)}, f32[4,8,256]{2,1,0:T(8,128)S(1)}, f32[4,8,256...) custom-call(s32[4]{0:T(128)S(1)} %copy-done.1, s32[8,256]{1,0:T(8,128)S(1)} %get-tuple-element.60.ids_ref, ...), custom_call_target="tpu_custom_call" | custom-call | flops 7021264896 | bytes 1048576 | tf_op jit(solution)/shard_map/logits/pallas_call | solution.py:274
  76.3 0.7 logits.7.refs_0_
  77.0 3.6 %collective-permute-start.21 = (f32[4,8,256]{2,1,0:T(8,128)S(1)}, f32[4,8,256]{2,1,0:T(8,128)S(1)}, u32[]{:S(2)}, u32[]{:S(2)}) collective-permute-start(f32[4,8,256]{2,1,0:T(8,128)S(1)} %logits.7.refs_0_), channel_id=1, source_target_pairs={{0,12},{1,13},{2,14},{3,15},{4,8},{5,9},{6,10},{7,11},{8,4},{9,5},... | collective-permute-start | bytes 98312 | tf_op jit(solution)/shard_map/ppermute | solution.py:307
  80.6 0.1 collective-permute-start.22
  80.7 1.4 %collective-permute-start.23 = (f32[4,8,256]{2,1,0:T(8,128)S(1)}, f32[4,8,256]{2,1,0:T(8,128)S(1)}, u32[]{:S(2)}, u32[]{:S(2)}) collective-permute-start(f32[4,8,256]{2,1,0:T(8,128)S(1)} %logits.7.refs_0_), channel_id=1, source_target_pairs={{0,4},{1,5},{2,6},{3,7},{4,0},{5,1},{6,2},{7,3},{8,12},{9,13},{10,... | collective-permute-start | bytes 98312 | tf_op jit(solution)/shard_map/ppermute | solution.py:307
  82.1 0.4 collective-permute-done.21.refs_1_
  82.5 2.0 %collective-permute-done.22.refs_2_ = f32[4,8,256]{2,1,0:T(8,128)S(1)} collective-permute-done((f32[4,8,256]{2,1,0:T(8,128)S(1)}, f32[4,8,256]{2,1,0:T(8,128)S(1)}, u32[]{:S(2)}, u32[]{:S(2)}) %collective-permute-start.22) | collective-permute-done | bytes 32800 | tf_op jit(solution)/shard_map/ppermute | solution.py:307
  84.5 0.1 collective-permute-done.23.refs_3_
  84.6 1.2 %collective-permute-start.24 = (f32[4,4,256]{2,1,0:T(4,128)S(1)}, f32[4,4,256]{2,1,0:T(4,128)S(1)}, u32[]{:S(2)}, u32[]{:S(2)}) collective-permute-start(f32[4,4,256]{2,1,0:T(4,128)S(1)} %get-tuple-element.106), channel_id=1, source_target_pairs={{0,18},{1,19},{2,16},{3,17},{4,22},{5,23},{6,20},{7,21},{8,26},{9,... | collective-permute-start | bytes 49160 | tf_op jit(solution)/shard_map/ppermute | solution.py:307
  85.8 1.3 %collective-permute-start.25 = (f32[4,4,256]{2,1,0:T(4,128)S(1)}, f32[4,4,256]{2,1,0:T(4,128)S(1)}, u32[]{:S(2)}, u32[]{:S(2)}) collective-permute-start(f32[4,4,256]{2,1,0:T(4,128)S(1)} %get-tuple-element.107.a_ref), channel_id=1, source_target_pairs={{0,16},{1,17},{2,18},{3,19},{4,20},{5,21},{6,22},{7,23},{8,24},{9,... | collective-permute-start | bytes 49160 | tf_op jit(solution)/shard_map/ppermute | solution.py:307
  87.1 2.0 %collective-permute-start.26 = (f32[4,4,256]{2,1,0:T(4,128)S(1)}, f32[4,4,256]{2,1,0:T(4,128)S(1)}, u32[]{:S(2)}, u32[]{:S(2)}) collective-permute-start(f32[4,4,256]{2,1,0:T(4,128)S(1)} %get-tuple-element.106), channel_id=1, source_target_pairs={{0,2},{1,3},{2,0},{3,1},{4,6},{5,7},{6,4},{7,5},{8,10},{9,11},{10,... | collective-permute-start | bytes 49160 | tf_op jit(solution)/shard_map/ppermute | solution.py:307
  89.1 1.1 %collective-permute-done.24.d_ref = f32[4,4,256]{2,1,0:T(4,128)S(1)} collective-permute-done((f32[4,4,256]{2,1,0:T(4,128)S(1)}, f32[4,4,256]{2,1,0:T(4,128)S(1)}, u32[]{:S(2)}, u32[]{:S(2)}) %collective-permute-start.24) | collective-permute-done | bytes 16416 | tf_op jit(solution)/shard_map/ppermute | solution.py:307
  90.2 0.2 collective-permute-done.25.b_ref
  90.4 0.4 collective-permute-done.26.c_ref
  90.9 1.2 %collective-permute-done.27.refs_1_ = f32[8,256]{1,0:T(8,128)S(1)} collective-permute-done((f32[8,256]{1,0:T(8,128)S(1)}, f32[8,256]{1,0:T(8,128)S(1)}, u32[]{:S(2)}, u32[]{:S(2)}) %collective-permute-start.27) | collective-permute-done | bytes 8224 | tf_op jit(solution)/shard_map/ppermute | solution.py:307
  92.1 1.2 %place.1 = (f32[2048]{0:T(1024)}, f32[2048]{0:T(1024)}) custom-call(s32[4]{0:T(128)S(1)} %copy-done.1, f32[8,256]{1,0:T(8,128)S(1)} %get-tuple-element.108.refs_0_, f32[8,256]{1,0:T(8,128)S(1)} %collective-permute-done.27.refs_1_), custom_call_target="tpu_custom_call" | custom-call | bytes 1048576 | tf_op jit(solution)/shard_map/place/pallas_call | solution.py:274
  (30 shorter events, 0.5 us)
Async XLA Ops:
  0.6 15.5 %copy-start = (bf16[256,4016]{0,1:T(8,128)(2,1)S(1)}, bf16[256,4016]{0,1:T(8,128)(2,1)}, u32[]{:S(2)}) copy-start(bf16[256,4016]{0,1:T(8,128)(2,1)} %param.7) | copy-start | bytes 6168580
  0.6 32.0 %collective-permute-start.9 = (bf16[4016,256]{1,0:T(8,128)(2,1)}, bf16[4016,256]{1,0:T(8,128)(2,1)S(1)}, u32[]{:S(2)}, u32[]{:S(2)}) collective-permute-start(bf16[4016,256]{1,0:T(8,128)(2,1)} %bitcast.1), channel_id=1, source_target_pairs={{0,1},{1,0},{2,3},{3,2},{4,5},{5,4},{6,7},{7,6},{8,9},{9,8},{10,11... | collective-permute-start | bytes 6168584 | tf_op jit(solution)/shard_map/ppermute | solution.py:307
  2.4 6.6 %collective-permute-start.2 = (bf16[272,256]{1,0:T(8,128)(2,1)S(1)}, bf16[272,256]{1,0:T(8,128)(2,1)S(1)}, u32[]{:S(2)}, u32[]{:S(2)}) collective-permute-start(bf16[272,256]{1,0:T(8,128)(2,1)S(1)} %get-tuple-element.59), channel_id=1, source_target_pairs={{0,3},{1,2},{2,1},{3,0},{4,7},{5,6},{6,5},{7,4},{8,11},{9,10},{10,... | collective-permute-start | bytes 417800 | tf_op jit(solution)/shard_map/ppermute | solution.py:307
  5.0 5.6 %collective-permute-start = (bf16[272,256]{1,0:T(8,128)(2,1)S(1)}, bf16[272,256]{1,0:T(8,128)(2,1)S(1)}, u32[]{:S(2)}, u32[]{:S(2)}) collective-permute-start(bf16[272,256]{1,0:T(8,128)(2,1)S(1)} %get-tuple-element.57), channel_id=1, source_target_pairs={{0,1},{1,0},{2,3},{3,2},{4,5},{5,4},{6,7},{7,6},{8,9},{9,8},{10,11... | collective-permute-start | bytes 417800 | tf_op jit(solution)/shard_map/ppermute | solution.py:307
  5.2 7.1 %collective-permute-start.1 = (bf16[272,256]{1,0:T(8,128)(2,1)S(1)}, bf16[272,256]{1,0:T(8,128)(2,1)S(1)}, u32[]{:S(2)}, u32[]{:S(2)}) collective-permute-start(bf16[272,256]{1,0:T(8,128)(2,1)S(1)} %get-tuple-element.58), channel_id=1, source_target_pairs={{0,2},{1,3},{2,0},{3,1},{4,6},{5,7},{6,4},{7,5},{8,10},{9,11},{10,... | collective-permute-start | bytes 417800 | tf_op jit(solution)/shard_map/ppermute | solution.py:307
  6.6 26.0 %copy-start.1 = (s32[4]{0:T(128)S(1)}, s32[4]{0:T(128)}, u32[]{:S(2)}) copy-start(s32[4]{0:T(128)} %seq_ref.9) | copy-start | bytes 52
  9.0 19.3 %collective-permute-start.5 = (bf16[1280,256]{1,0:T(8,128)(2,1)S(1)}, bf16[1280,256]{1,0:T(8,128)(2,1)S(1)}, u32[]{:S(2)}, u32[]{:S(2)}) collective-permute-start(bf16[1280,256]{1,0:T(8,128)(2,1)S(1)} %slice.44), channel_id=1, source_target_pairs={{0,2},{1,3},{2,0},{3,1},{4,6},{5,7},{6,4},{7,5},{8,10},{9,11},{10,... | collective-permute-start | bytes 1966088 | tf_op jit(solution)/shard_map/ppermute | solution.py:307
  12.7 15.7 %collective-permute-start.3 = (bf16[1024,256]{1,0:T(8,128)(2,1)S(1)}, bf16[1024,256]{1,0:T(8,128)(2,1)S(1)}, u32[]{:S(2)}, u32[]{:S(2)}) collective-permute-start(bf16[1024,256]{1,0:T(8,128)(2,1)S(1)} %get-tuple-element.61.refs_0_), channel_id=1, source_target_pairs={{0,8},{1,9},{2,10},{3,11},{4,12},{5,13},{6,14},{7,15},{8,16},{9,17... | collective-permute-start | bytes 1572872 | tf_op jit(solution)/shard_map/ppermute | solution.py:307
  14.6 13.7 %collective-permute-start.4 = (bf16[1024,256]{1,0:T(8,128)(2,1)S(1)}, bf16[1024,256]{1,0:T(8,128)(2,1)S(1)}, u32[]{:S(2)}, u32[]{:S(2)}) collective-permute-start(bf16[1024,256]{1,0:T(8,128)(2,1)S(1)} %get-tuple-element.61.refs_0_), channel_id=1, source_target_pairs={{0,4},{1,5},{2,6},{3,7},{4,0},{5,1},{6,2},{7,3},{8,12},{9,13},{10,... | collective-permute-start | bytes 1572872 | tf_op jit(solution)/shard_map/ppermute | solution.py:307
  16.2 28.4 %collective-permute-start.8 = (bf16[1664,256]{1,0:T(8,128)(2,1)S(1)}, bf16[1664,256]{1,0:T(8,128)(2,1)S(1)}, u32[]{:S(2)}, u32[]{:S(2)}) collective-permute-start(bf16[1664,256]{1,0:T(8,128)(2,1)S(1)} %slice.45), channel_id=1, source_target_pairs={{0,2},{1,3},{2,0},{3,1},{4,6},{5,7},{6,4},{7,5},{8,10},{9,11},{10,... | collective-permute-start | bytes 2555912 | tf_op jit(solution)/shard_map/ppermute | solution.py:307
  28.4 2.6 %collective-permute-start.10 = (bf16[640,256]{1,0:T(8,128)(2,1)S(1)}, bf16[640,256]{1,0:T(8,128)(2,1)S(1)}, u32[]{:S(2)}, u32[]{:S(2)}) collective-permute-start(bf16[640,256]{1,0:T(8,128)(2,1)S(1)} %get-tuple-element.113), channel_id=1, source_target_pairs={{0,1},{1,0},{2,3},{3,2},{4,5},{5,4},{6,7},{7,6},{8,9},{9,8},{10,11... | collective-permute-start | bytes 983048 | tf_op jit(solution)/shard_map/ppermute | solution.py:307
  28.5 16.1 %collective-permute-start.6 = (bf16[1024,256]{1,0:T(8,128)(2,1)S(1)}, bf16[1024,256]{1,0:T(8,128)(2,1)S(1)}, u32[]{:S(2)}, u32[]{:S(2)}) collective-permute-start(bf16[1024,256]{1,0:T(8,128)(2,1)S(1)} %collective-permute-done.3.refs_2_), channel_id=1, source_target_pairs={{0,8},{1,9},{2,10},{3,11},{4,12},{5,13},{6,14},{7,15},{8,16},{9,17... | collective-permute-start | bytes 1572872 | tf_op jit(solution)/shard_map/ppermute | solution.py:307
  29.5 15.1 %collective-permute-start.7 = (bf16[1024,256]{1,0:T(8,128)(2,1)S(1)}, bf16[1024,256]{1,0:T(8,128)(2,1)S(1)}, u32[]{:S(2)}, u32[]{:S(2)}) collective-permute-start(bf16[1024,256]{1,0:T(8,128)(2,1)S(1)} %collective-permute-done.3.refs_2_), channel_id=1, source_target_pairs={{0,4},{1,5},{2,6},{3,7},{4,0},{5,1},{6,2},{7,3},{8,12},{9,13},{10,... | collective-permute-start | bytes 1572872 | tf_op jit(solution)/shard_map/ppermute | solution.py:307
  31.0 1.6 %collective-permute-start.11 = (bf16[640,256]{1,0:T(8,128)(2,1)S(1)}, bf16[640,256]{1,0:T(8,128)(2,1)S(1)}, u32[]{:S(2)}, u32[]{:S(2)}) collective-permute-start(bf16[640,256]{1,0:T(8,128)(2,1)S(1)} %get-tuple-element.112), channel_id=1, source_target_pairs={{0,1},{1,0},{2,3},{3,2},{4,5},{5,4},{6,7},{7,6},{8,9},{9,8},{10,11... | collective-permute-start | bytes 983048 | tf_op jit(solution)/shard_map/ppermute | solution.py:307
  44.7 5.5 %collective-permute-start.15 = (bf16[832,256]{1,0:T(8,128)(2,1)S(1)}, bf16[832,256]{1,0:T(8,128)(2,1)S(1)}, u32[]{:S(2)}, u32[]{:S(2)}) collective-permute-start(bf16[832,256]{1,0:T(8,128)(2,1)S(1)} %get-tuple-element.111), channel_id=1, source_target_pairs={{0,1},{1,0},{2,3},{3,2},{4,5},{5,4},{6,7},{7,6},{8,9},{9,8},{10,11... | collective-permute-start | bytes 1277960 | tf_op jit(solution)/shard_map/ppermute | solution.py:307
  44.7 5.4 %collective-permute-start.16 = (bf16[832,256]{1,0:T(8,128)(2,1)S(1)}, bf16[832,256]{1,0:T(8,128)(2,1)S(1)}, u32[]{:S(2)}, u32[]{:S(2)}) collective-permute-start(bf16[832,256]{1,0:T(8,128)(2,1)S(1)} %get-tuple-element.110), channel_id=1, source_target_pairs={{0,1},{1,0},{2,3},{3,2},{4,5},{5,4},{6,7},{7,6},{8,9},{9,8},{10,11... | collective-permute-start | bytes 1277960 | tf_op jit(solution)/shard_map/ppermute | solution.py:307
  45.3 14.5 %collective-permute-start.14 = (bf16[1072,256]{1,0:T(8,128)(2,1)S(1)}, bf16[1072,256]{1,0:T(8,128)(2,1)S(1)}, u32[]{:S(2)}, u32[]{:S(2)}) collective-permute-start(bf16[1072,256]{1,0:T(8,128)(2,1)S(1)} %slice.46), channel_id=1, source_target_pairs={{0,2},{1,3},{2,0},{3,1},{4,6},{5,7},{6,4},{7,5},{8,10},{9,11},{10,... | collective-permute-start | bytes 1646600 | tf_op jit(solution)/shard_map/ppermute | solution.py:307
  47.1 15.5 %collective-permute-start.12 = (bf16[1024,256]{1,0:T(8,128)(2,1)S(1)}, bf16[1024,256]{1,0:T(8,128)(2,1)S(1)}, u32[]{:S(2)}, u32[]{:S(2)}) collective-permute-start(bf16[1024,256]{1,0:T(8,128)(2,1)S(1)} %collective-permute-done.6.refs_4_), channel_id=1, source_target_pairs={{0,8},{1,9},{2,10},{3,11},{4,12},{5,13},{6,14},{7,15},{8,16},{9,17... | collective-permute-start | bytes 1572872 | tf_op jit(solution)/shard_map/ppermute | solution.py:307
  48.7 13.9 %collective-permute-start.13 = (bf16[1024,256]{1,0:T(8,128)(2,1)S(1)}, bf16[1024,256]{1,0:T(8,128)(2,1)S(1)}, u32[]{:S(2)}, u32[]{:S(2)}) collective-permute-start(bf16[1024,256]{1,0:T(8,128)(2,1)S(1)} %collective-permute-done.6.refs_4_), channel_id=1, source_target_pairs={{0,4},{1,5},{2,6},{3,7},{4,0},{5,1},{6,2},{7,3},{8,12},{9,13},{10,... | collective-permute-start | bytes 1572872 | tf_op jit(solution)/shard_map/ppermute | solution.py:307
  62.6 3.3 %collective-permute-start.19 = (bf16[544,256]{1,0:T(8,128)(2,1)S(1)}, bf16[544,256]{1,0:T(8,128)(2,1)S(1)}, u32[]{:S(2)}, u32[]{:S(2)}) collective-permute-start(bf16[544,256]{1,0:T(8,128)(2,1)S(1)} %slice.42), channel_id=1, source_target_pairs={{0,1},{1,0},{2,3},{3,2},{4,5},{5,4},{6,7},{7,6},{8,9},{9,8},{10,11... | collective-permute-start | bytes 835592 | tf_op jit(solution)/shard_map/ppermute | solution.py:307
  62.7 3.2 %collective-permute-start.20 = (bf16[528,256]{1,0:T(8,128)(2,1)S(1)}, bf16[528,256]{1,0:T(8,128)(2,1)S(1)}, u32[]{:S(2)}, u32[]{:S(2)}) collective-permute-start(bf16[528,256]{1,0:T(8,128)(2,1)S(1)} %slice.43), channel_id=1, source_target_pairs={{0,1},{1,0},{2,3},{3,2},{4,5},{5,4},{6,7},{7,6},{8,9},{9,8},{10,11... | collective-permute-start | bytes 811016 | tf_op jit(solution)/shard_map/ppermute | solution.py:307
  63.3 13.0 %collective-permute-start.17 = (bf16[512,256]{1,0:T(8,128)(2,1)S(1)}, bf16[512,256]{1,0:T(8,128)(2,1)S(1)}, u32[]{:S(2)}, u32[]{:S(2)}) collective-permute-start(bf16[512,256]{1,0:T(8,128)(2,1)S(1)} %slice.40), channel_id=1, source_target_pairs={{0,4},{1,5},{2,6},{3,7},{4,0},{5,1},{6,2},{7,3},{8,12},{9,13},{10,... | collective-permute-start | bytes 786440 | tf_op jit(solution)/shard_map/ppermute | solution.py:307
  64.9 11.4 %collective-permute-start.18 = (bf16[512,256]{1,0:T(8,128)(2,1)S(1)}, bf16[512,256]{1,0:T(8,128)(2,1)S(1)}, u32[]{:S(2)}, u32[]{:S(2)}) collective-permute-start(bf16[512,256]{1,0:T(8,128)(2,1)S(1)} %slice.41), channel_id=1, source_target_pairs={{0,8},{1,9},{2,10},{3,11},{4,12},{5,13},{6,14},{7,15},{8,16},{9,17... | collective-permute-start | bytes 786440 | tf_op jit(solution)/shard_map/ppermute | solution.py:307
  77.0 5.5 %collective-permute-start.21 = (f32[4,8,256]{2,1,0:T(8,128)S(1)}, f32[4,8,256]{2,1,0:T(8,128)S(1)}, u32[]{:S(2)}, u32[]{:S(2)}) collective-permute-start(f32[4,8,256]{2,1,0:T(8,128)S(1)} %logits.7.refs_0_), channel_id=1, source_target_pairs={{0,12},{1,13},{2,14},{3,15},{4,8},{5,9},{6,10},{7,11},{8,4},{9,5},... | collective-permute-start | bytes 98312 | tf_op jit(solution)/shard_map/ppermute | solution.py:307
  80.6 3.9 %collective-permute-start.22 = (f32[4,8,256]{2,1,0:T(8,128)S(1)}, f32[4,8,256]{2,1,0:T(8,128)S(1)}, u32[]{:S(2)}, u32[]{:S(2)}) collective-permute-start(f32[4,8,256]{2,1,0:T(8,128)S(1)} %logits.7.refs_0_), channel_id=1, source_target_pairs={{0,8},{1,9},{2,10},{3,11},{4,12},{5,13},{6,14},{7,15},{8,0},{9,1},... | collective-permute-start | bytes 98312 | tf_op jit(solution)/shard_map/ppermute | solution.py:307
  80.7 3.9 %collective-permute-start.23 = (f32[4,8,256]{2,1,0:T(8,128)S(1)}, f32[4,8,256]{2,1,0:T(8,128)S(1)}, u32[]{:S(2)}, u32[]{:S(2)}) collective-permute-start(f32[4,8,256]{2,1,0:T(8,128)S(1)} %logits.7.refs_0_), channel_id=1, source_target_pairs={{0,4},{1,5},{2,6},{3,7},{4,0},{5,1},{6,2},{7,3},{8,12},{9,13},{10,... | collective-permute-start | bytes 98312 | tf_op jit(solution)/shard_map/ppermute | solution.py:307
  84.6 5.6 %collective-permute-start.24 = (f32[4,4,256]{2,1,0:T(4,128)S(1)}, f32[4,4,256]{2,1,0:T(4,128)S(1)}, u32[]{:S(2)}, u32[]{:S(2)}) collective-permute-start(f32[4,4,256]{2,1,0:T(4,128)S(1)} %get-tuple-element.106), channel_id=1, source_target_pairs={{0,18},{1,19},{2,16},{3,17},{4,22},{5,23},{6,20},{7,21},{8,26},{9,... | collective-permute-start | bytes 49160 | tf_op jit(solution)/shard_map/ppermute | solution.py:307
  85.8 4.6 %collective-permute-start.25 = (f32[4,4,256]{2,1,0:T(4,128)S(1)}, f32[4,4,256]{2,1,0:T(4,128)S(1)}, u32[]{:S(2)}, u32[]{:S(2)}) collective-permute-start(f32[4,4,256]{2,1,0:T(4,128)S(1)} %get-tuple-element.107.a_ref), channel_id=1, source_target_pairs={{0,16},{1,17},{2,18},{3,19},{4,20},{5,21},{6,22},{7,23},{8,24},{9,... | collective-permute-start | bytes 49160 | tf_op jit(solution)/shard_map/ppermute | solution.py:307
  87.1 3.7 %collective-permute-start.26 = (f32[4,4,256]{2,1,0:T(4,128)S(1)}, f32[4,4,256]{2,1,0:T(4,128)S(1)}, u32[]{:S(2)}, u32[]{:S(2)}) collective-permute-start(f32[4,4,256]{2,1,0:T(4,128)S(1)} %get-tuple-element.106), channel_id=1, source_target_pairs={{0,2},{1,3},{2,0},{3,1},{4,6},{5,7},{6,4},{7,5},{8,10},{9,11},{10,... | collective-permute-start | bytes 49160 | tf_op jit(solution)/shard_map/ppermute | solution.py:307
  90.9 1.2 %collective-permute-start.27 = (f32[8,256]{1,0:T(8,128)S(1)}, f32[8,256]{1,0:T(8,128)S(1)}, u32[]{:S(2)}, u32[]{:S(2)}) collective-permute-start(f32[8,256]{1,0:T(8,128)S(1)} %get-tuple-element.109), channel_id=1, source_target_pairs={{0,1},{1,0},{2,3},{3,2},{4,5},{5,4},{6,7},{7,6},{8,9},{9,8},{10,11... | collective-permute-start | bytes 24584 | tf_op jit(solution)/shard_map/ppermute | solution.py:307

commit v4 on v3

--- a/solution.py
+++ b/solution.py
@@ -278,12 +278,12 @@
         out_specs=jax.tree.map(lambda _: VMEM, out_shape),
         scratch_shapes=list(scratch),
         compiler_params=pltpu.CompilerParams(vmem_limit_bytes=limit * 2**20),
-        cost_estimate=pl.CostEstimate(flops=flops, bytes_accessed=2**20, transcendentals=0),
+        cost_estimate=pl.CostEstimate(flops=flops, bytes_accessed=0, transcendentals=0),
         name=name,
     )(*args)
 
 
-def chunk_spans(columns, shares=(0.32, 0.733)):
+def chunk_spans(columns, shares=(0.32, 0.701)):
     ends = [0] + [64 * round(columns * share / 64) for share in shares] + [columns]
     return [(a, b - a) for a, b in zip(ends, ends[1:])]
 
@@ -350,10 +350,11 @@
                 if k:
                     refs[k] = (held[k], at)
                     refs[k | 1] = (move(held[k][at : at + count], plan.width_xor(1)), 0)
-            chunks.append([refs[k] for k in range(W)])
+            chunks.append([refs[k][0] for k in range(W)])
+            firsts.append([refs[k][1] for k in range(W)])
             parts.append((start + at, count))
 
-    states, groups, chunks, parts, done = {}, {}, [], [], {}
+    states, groups, chunks, firsts, parts, done = {}, {}, [], [], [], {}
 
     def stage(wanted, last=False):
         jobs = {key: [c for c in mine if c not in done.get(key, [])] for key, mine in wanted.items()}
@@ -364,8 +365,8 @@
         sizes, bases = [parts[c][1] for c in used], [parts[c][0] for c in used]
         args = [seq_lengths, all_ids] + [part for key in keys if jobs[key] for part in groups[key]]
         halves = [len(groups[key]) if jobs[key] else 0 for key in keys]
-        held = [chunks[c][k][0] for c in used for k in range(W)]
-        offsets = [[chunks[c][k][1] for k in range(W)] for c in used]
+        held = [chunks[c][k] for c in used for k in range(W)]
+        offsets = [firsts[c] for c in used]
         unique = [held[i] for i in range(len(held)) if all(held[i] is not held[j] for j in range(i))]
         where = [next(j for j in range(len(unique)) if unique[j] is one) for one in held]
         args += unique
@@ -385,7 +386,7 @@
             args,
             1,
             scratch=[pltpu.VMEM((TILE, part), jnp.float32)] * 2,
-            flops=2 * work * part * depth,
+            flops=0,
             name="logits",
         )
         if last:
@@ -411,16 +412,24 @@
             for dx in range(1, plan.X):
                 passed = move(passed, plan.x_ring())
                 arrived[dz, dx] = [passed]
+        if far:
+            near_chunk(dz - 1, far)
+        whole = len(chunks)
         if dz < len(spans):
             tied["far"] = far_chunk(dz, pieces[-1:])
-        if far:
-            near_chunk(dz - 1, far)
+        if fast and dz:
+            stage({key: list(range(whole)) for key in groups})
+            tied["states"] = states
+        if dz == len(spans) - 1:
+            held, states = lax.optimization_barrier((tied.pop("far"), states))
+            near_chunk(dz, held)
+            tied["last"] = chunks[whole:]
             if fast:
-                stage({key: list(range(len(chunks))) for key in groups})
                 tied["states"] = states
         onward, arrived, tied = lax.optimization_barrier((onward, arrived, tied))
         states = tied.get("states", states)
         far = tied.get("far", {})
+        chunks[whole:] = tied.get("last", [])
         groups.update(arrived)
         if not end:
             ring = onward[0]

time: 93.5 us -> 91.4 us (0.978)
  waiting for transfers between devices: 33.7 us -> 36.8 us
  starting transfers between devices: 31.1 us -> 28.5 us
  Pallas kernels: 26.2 us -> 23.6 us
    ppermute x28, waiting for transfers between devices: 33.7 us -> 36.8 us  [on_device(): move = lambda value, perm: lax.ppermute(value, AXES, perm)]
    pallas_call x9, Pallas kernels: 26.2 us -> 23.6 us  [call(): pl.pallas_call(kernel, out_shape=out_shape, in_specs=[SMEM] * smem + [HBM...]
    ppermute x28, starting transfers between devices: 31.1 us -> 28.5 us  [on_device(): move = lambda value, perm: lax.ppermute(value, AXES, perm)]
  transfers between devices with their start and end apart: 28 -> 28, of which waited for: 14 -> 15; matrix products, arithmetic and copies ran while one was open for 1% -> 2% of each run, Pallas kernels for 25% -> 22%
where the time goes in v4:
time: 91.4 us; the launch traced here: 91.2 us
  waiting for transfers between devices  36.8 us (40%)
  starting transfers between devices  28.5 us (31%)
  Pallas kernels  23.6 us (26%)
  local copies, waits for them, and re-layouts  1.41 us (2%)
    ppermute x28, waiting for transfers between devices, on_device(): move = lambda value, perm: lax.ppermute(value, AXES, perm)  36.8 us
    ppermute x28, starting transfers between devices, on_device(): move = lambda value, perm: lax.ppermute(value, AXES, perm)  28.5 us
    pallas_call x9, Pallas kernels, call(): pl.pallas_call(kernel, out_shape=out_shape, in_specs=[SMEM] * smem + [HBM...  23.6 us
  transfers between devices with their start and end apart: 28, of which 15 were waited for; matrix products, arithmetic and copies ran while one was open for 2% of the time, Pallas kernels for 22%

profile of v4, /device:TPU:0, one launch (start us, length us, event | category | flops | bytes accessed | tf_op | source)
XLA Modules:
  0.0 91.2 jit_solution(3388444380456797261)
XLA Ops:
  0.6 0.5 collective-permute-start.9
  1.2 1.3 %send.1 = (bf16[272,256]{1,0:T(8,128)(2,1)S(1)}, bf16[272,256]{1,0:T(8,128)(2,1)S(1)}, bf16[272,256]{1,0:T(8,128)(2,1)S(1)}, bf16[272,256]{1,0:T(8,128)(2,1)S(1)}) custom-call(bf16[1024,256]{1,0:T(8,128)(2,1)} %h_ref.1, f32[256]{0:T(256)} %gain_hbm.1, s32[2048]{0:T(1024)} %ids_hbm.1), custom_call_target="tpu_custom_call" | custom-call | tf_op jit(solution)/shard_map/send/pallas_call | solution.py:274
  2.4 2.6 %collective-permute-start.2 = (bf16[272,256]{1,0:T(8,128)(2,1)S(1)}, bf16[272,256]{1,0:T(8,128)(2,1)S(1)}, u32[]{:S(2)}, u32[]{:S(2)}) collective-permute-start(bf16[272,256]{1,0:T(8,128)(2,1)S(1)} %get-tuple-element.72), channel_id=1, source_target_pairs={{0,3},{1,2},{2,1},{3,0},{4,7},{5,6},{6,5},{7,4},{8,11},{9,10},{10,... | collective-permute-start | bytes 417800 | tf_op jit(solution)/shard_map/ppermute | solution.py:307
  5.0 0.2 collective-permute-start
  5.2 0.3 collective-permute-start.1
  5.5 1.1 %slice.44 = bf16[1280,256]{1,0:T(8,128)(2,1)S(1)} slice(bf16[4016,256]{1,0:T(8,128)(2,1)} %bitcast.2), slice={[0:1280], [0:256]} | slice | bytes 1310720 | tf_op jit(solution)/shard_map/slice | solution.py:339
  6.6 2.4 %collective-permute-done.2.refs_3_ = bf16[272,256]{1,0:T(8,128)(2,1)S(1)} collective-permute-done((bf16[272,256]{1,0:T(8,128)(2,1)S(1)}, bf16[272,256]{1,0:T(8,128)(2,1)S(1)}, u32[]{:S(2)}, u32[]{:S(2)}) %collective-permute-start.2) | collective-permute-done | bytes 139296 | tf_op jit(solution)/shard_map/ppermute | solution.py:307
  9.0 1.6 %collective-permute-start.5 = (bf16[1280,256]{1,0:T(8,128)(2,1)S(1)}, bf16[1280,256]{1,0:T(8,128)(2,1)S(1)}, u32[]{:S(2)}, u32[]{:S(2)}) collective-permute-start(bf16[1280,256]{1,0:T(8,128)(2,1)S(1)} %slice.44), channel_id=1, source_target_pairs={{0,2},{1,3},{2,0},{3,1},{4,6},{5,7},{6,4},{7,5},{8,10},{9,11},{10,... | collective-permute-start | bytes 1966088 | tf_op jit(solution)/shard_map/ppermute | solution.py:307
  10.6 1.7 %collective-permute-done.1.refs_2_ = bf16[272,256]{1,0:T(8,128)(2,1)S(1)} collective-permute-done((bf16[272,256]{1,0:T(8,128)(2,1)S(1)}, bf16[272,256]{1,0:T(8,128)(2,1)S(1)}, u32[]{:S(2)}, u32[]{:S(2)}) %collective-permute-start.1) | collective-permute-done | bytes 139296 | tf_op jit(solution)/shard_map/ppermute | solution.py:307
  12.3 0.4 norm.1
  12.7 1.9 %collective-permute-start.3 = (bf16[1024,256]{1,0:T(8,128)(2,1)S(1)}, bf16[1024,256]{1,0:T(8,128)(2,1)S(1)}, u32[]{:S(2)}, u32[]{:S(2)}) collective-permute-start(bf16[1024,256]{1,0:T(8,128)(2,1)S(1)} %get-tuple-element.74.refs_0_), channel_id=1, source_target_pairs={{0,8},{1,9},{2,10},{3,11},{4,12},{5,13},{6,14},{7,15},{8,16},{9,17... | collective-permute-start | bytes 1572872 | tf_op jit(solution)/shard_map/ppermute | solution.py:307
  14.6 1.5 %collective-permute-start.4 = (bf16[1024,256]{1,0:T(8,128)(2,1)S(1)}, bf16[1024,256]{1,0:T(8,128)(2,1)S(1)}, u32[]{:S(2)}, u32[]{:S(2)}) collective-permute-start(bf16[1024,256]{1,0:T(8,128)(2,1)S(1)} %get-tuple-element.74.refs_0_), channel_id=1, source_target_pairs={{0,4},{1,5},{2,6},{3,7},{4,0},{5,1},{6,2},{7,3},{8,12},{9,13},{10,... | collective-permute-start | bytes 1572872 | tf_op jit(solution)/shard_map/ppermute | solution.py:307
  16.2 1.6 %collective-permute-start.8 = (bf16[1536,256]{1,0:T(8,128)(2,1)S(1)}, bf16[1536,256]{1,0:T(8,128)(2,1)S(1)}, u32[]{:S(2)}, u32[]{:S(2)}) collective-permute-start(bf16[1536,256]{1,0:T(8,128)(2,1)S(1)} %slice.45), channel_id=1, source_target_pairs={{0,2},{1,3},{2,0},{3,1},{4,6},{5,7},{6,4},{7,5},{8,10},{9,11},{10,... | collective-permute-start | bytes 2359304 | tf_op jit(solution)/shard_map/ppermute | solution.py:307
  17.8 10.6 %collective-permute-done.3.refs_2_ = bf16[1024,256]{1,0:T(8,128)(2,1)S(1)} collective-permute-done((bf16[1024,256]{1,0:T(8,128)(2,1)S(1)}, bf16[1024,256]{1,0:T(8,128)(2,1)S(1)}, u32[]{:S(2)}, u32[]{:S(2)}) %collective-permute-start.3) | collective-permute-done | bytes 524320 | tf_op jit(solution)/shard_map/ppermute | solution.py:307
  28.4 0.1 collective-permute-start.10
  28.5 1.1 %collective-permute-start.6 = (bf16[1024,256]{1,0:T(8,128)(2,1)S(1)}, bf16[1024,256]{1,0:T(8,128)(2,1)S(1)}, u32[]{:S(2)}, u32[]{:S(2)}) collective-permute-start(bf16[1024,256]{1,0:T(8,128)(2,1)S(1)} %collective-permute-done.3.refs_2_), channel_id=1, source_target_pairs={{0,8},{1,9},{2,10},{3,11},{4,12},{5,13},{6,14},{7,15},{8,16},{9,17... | collective-permute-start | bytes 1572872 | tf_op jit(solution)/shard_map/ppermute | solution.py:307
  29.5 1.5 %collective-permute-start.7 = (bf16[1024,256]{1,0:T(8,128)(2,1)S(1)}, bf16[1024,256]{1,0:T(8,128)(2,1)S(1)}, u32[]{:S(2)}, u32[]{:S(2)}) collective-permute-start(bf16[1024,256]{1,0:T(8,128)(2,1)S(1)} %collective-permute-done.3.refs_2_), channel_id=1, source_target_pairs={{0,4},{1,5},{2,6},{3,7},{4,0},{5,1},{6,2},{7,3},{8,12},{9,13},{10,... | collective-permute-start | bytes 1572872 | tf_op jit(solution)/shard_map/ppermute | solution.py:307
  31.1 1.6 %collective-permute-done.11.refs_7_.refs_9_.refs_11_.refs_6_ = bf16[640,256]{1,0:T(8,128)(2,1)S(1)} collective-permute-done((bf16[640,256]{1,0:T(8,128)(2,1)S(1)}, bf16[640,256]{1,0:T(8,128)(2,1)S(1)}, u32[]{:S(2)}, u32[]{:S(2)}) %collective-permute-start.11) | collective-permute-done | bytes 327712 | tf_op jit(solution)/shard_map/ppermute | solution.py:307
  32.7 1.5 %collective-permute-start.14 = (bf16[1200,256]{1,0:T(8,128)(2,1)S(1)}, bf16[1200,256]{1,0:T(8,128)(2,1)S(1)}, u32[]{:S(2)}, u32[]{:S(2)}) collective-permute-start(bf16[1200,256]{1,0:T(8,128)(2,1)S(1)} %slice.46), channel_id=1, source_target_pairs={{0,2},{1,3},{2,0},{3,1},{4,6},{5,7},{6,4},{7,5},{8,10},{9,11},{10,... | collective-permute-start | bytes 1843208 | tf_op jit(solution)/shard_map/ppermute | solution.py:307
  34.2 2.6 %logits.4 = (f32[4,8,256]{2,1,0:T(8,128)S(1)}, f32[4,8,256]{2,1,0:T(8,128)S(1)}, f32[4,8,256]{2,1,0:T(8,128)S(1)}) custom-call(s32[4]{0:T(128)S(1)} %copy-done.1, s32[8,256]{1,0:T(8,128)S(1)} %get-tuple-element.73.ids_ref, bf16[1024,256]{1,0:T(8,128)(2,1)S(1)} %get-tuple-element.74.refs_0_, bf16[1024,256]{1,0:T(8,128)(2,1)S(1)} %collective-permute-done.4.refs_1_, ...), custom_call_target="tpu_custom_call" | custom-call | tf_op jit(solution)/shard_map/logits/pallas_call | solution.py:274
  36.8 6.6 %collective-permute-done.8.refs_10_.refs_12_.refs_7_ = bf16[1536,256]{1,0:T(8,128)(2,1)S(1)} collective-permute-done((bf16[1536,256]{1,0:T(8,128)(2,1)S(1)}, bf16[1536,256]{1,0:T(8,128)(2,1)S(1)}, u32[]{:S(2)}, u32[]{:S(2)}) %collective-permute-start.8) | collective-permute-done | bytes 786464 | tf_op jit(solution)/shard_map/ppermute | solution.py:307
  43.4 1.2 %collective-permute-done.6.refs_4_ = bf16[1024,256]{1,0:T(8,128)(2,1)S(1)} collective-permute-done((bf16[1024,256]{1,0:T(8,128)(2,1)S(1)}, bf16[1024,256]{1,0:T(8,128)(2,1)S(1)}, u32[]{:S(2)}, u32[]{:S(2)}) %collective-permute-start.6) | collective-permute-done | bytes 524320 | tf_op jit(solution)/shard_map/ppermute | solution.py:307
  44.7 0.1 collective-permute-start.15
  44.7 0.5 collective-permute-start.16
  45.2 0.5 collective-permute-start.12
  45.7 1.5 %collective-permute-start.13 = (bf16[1024,256]{1,0:T(8,128)(2,1)S(1)}, bf16[1024,256]{1,0:T(8,128)(2,1)S(1)}, u32[]{:S(2)}, u32[]{:S(2)}) collective-permute-start(bf16[1024,256]{1,0:T(8,128)(2,1)S(1)} %collective-permute-done.6.refs_4_), channel_id=1, source_target_pairs={{0,4},{1,5},{2,6},{3,7},{4,0},{5,1},{6,2},{7,3},{8,12},{9,13},{10,... | collective-permute-start | bytes 1572872 | tf_op jit(solution)/shard_map/ppermute | solution.py:307
  47.2 7.2 %logits.5 = (f32[4,8,256]{2,1,0:T(8,128)S(1)}, f32[4,8,256]{2,1,0:T(8,128)S(1)}, f32[4,8,256]{2,1,0:T(8,128)S(1)}, f32[4,8,256]{2,1,0:T(8,128)S(1)}, f32[4,8,256]{2,1,0:T(8,128)S(1)}) custom-call(s32[4]{0:T(128)S(1)} %copy-done.1, s32[8,256]{1,0:T(8,128)S(1)} %get-tuple-element.73.ids_ref, bf16[1024,256]{1,0:T(8,128)(2,1)S(1)} %get-tuple-element.74.refs_0_, ...), custom_call_target="tpu_custom_call" | custom-call | tf_op jit(solution)/shard_map/logits/pallas_call | solution.py:274
  54.4 1.9 %collective-permute-done.14.refs_17_.refs_21_.refs_12_.refs_16_ = bf16[1200,256]{1,0:T(8,128)(2,1)S(1)} collective-permute-done((bf16[1200,256]{1,0:T(8,128)(2,1)S(1)}, bf16[1200,256]{1,0:T(8,128)(2,1)S(1)}, u32[]{:S(2)}, u32[]{:S(2)}) %collective-permute-start.14) | collective-permute-done | bytes 614432 | tf_op jit(solution)/shard_map/ppermute | solution.py:307
  56.3 0.1 collective-permute-start.17
  56.5 0.6 collective-permute-start.18
  57.0 3.9 %collective-permute-done.12.refs_6_ = bf16[1024,256]{1,0:T(8,128)(2,1)S(1)} collective-permute-done((bf16[1024,256]{1,0:T(8,128)(2,1)S(1)}, bf16[1024,256]{1,0:T(8,128)(2,1)S(1)}, u32[]{:S(2)}, u32[]{:S(2)}) %collective-permute-start.12) | collective-permute-done | bytes 524320 | tf_op jit(solution)/shard_map/ppermute | solution.py:307
  61.0 1.6 %collective-permute-start.19 = (bf16[512,256]{1,0:T(8,128)(2,1)S(1)}, bf16[512,256]{1,0:T(8,128)(2,1)S(1)}, u32[]{:S(2)}, u32[]{:S(2)}) collective-permute-start(bf16[512,256]{1,0:T(8,128)(2,1)S(1)} %slice.42), channel_id=1, source_target_pairs={{0,4},{1,5},{2,6},{3,7},{4,0},{5,1},{6,2},{7,3},{8,12},{9,13},{10,... | collective-permute-start | bytes 786440 | tf_op jit(solution)/shard_map/ppermute | solution.py:307
  62.6 10.3 %logits.6 = (f32[4,8,256]{2,1,0:T(8,128)S(1)}, f32[4,8,256]{2,1,0:T(8,128)S(1)}, f32[4,8,256]{2,1,0:T(8,128)S(1)}, f32[4,8,256]{2,1,0:T(8,128)S(1)}, f32[4,8,256...) custom-call(s32[4]{0:T(128)S(1)} %copy-done.1, s32[8,256]{1,0:T(8,128)S(1)} %get-tuple-element.73.ids_ref, ...), custom_call_target="tpu_custom_call" | custom-call | tf_op jit(solution)/shard_map/logits/pallas_call | solution.py:274
  72.9 0.7 logits.7.refs_0_
  73.6 3.4 %collective-permute-start.21 = (f32[4,8,256]{2,1,0:T(8,128)S(1)}, f32[4,8,256]{2,1,0:T(8,128)S(1)}, u32[]{:S(2)}, u32[]{:S(2)}) collective-permute-start(f32[4,8,256]{2,1,0:T(8,128)S(1)} %logits.7.refs_0_), channel_id=1, source_target_pairs={{0,12},{1,13},{2,14},{3,15},{4,8},{5,9},{6,10},{7,11},{8,4},{9,5},... | collective-permute-start | bytes 98312 | tf_op jit(solution)/shard_map/ppermute | solution.py:307
  77.0 0.2 collective-permute-start.22
  77.1 1.3 %collective-permute-start.23 = (f32[4,8,256]{2,1,0:T(8,128)S(1)}, f32[4,8,256]{2,1,0:T(8,128)S(1)}, u32[]{:S(2)}, u32[]{:S(2)}) collective-permute-start(f32[4,8,256]{2,1,0:T(8,128)S(1)} %logits.7.refs_0_), channel_id=1, source_target_pairs={{0,4},{1,5},{2,6},{3,7},{4,0},{5,1},{6,2},{7,3},{8,12},{9,13},{10,... | collective-permute-start | bytes 98312 | tf_op jit(solution)/shard_map/ppermute | solution.py:307
  78.5 0.4 collective-permute-done.21.refs_1_
  78.9 2.0 %collective-permute-done.22.refs_2_ = f32[4,8,256]{2,1,0:T(8,128)S(1)} collective-permute-done((f32[4,8,256]{2,1,0:T(8,128)S(1)}, f32[4,8,256]{2,1,0:T(8,128)S(1)}, u32[]{:S(2)}, u32[]{:S(2)}) %collective-permute-start.22) | collective-permute-done | bytes 32800 | tf_op jit(solution)/shard_map/ppermute | solution.py:307
  80.9 0.2 collective-permute-done.23.refs_3_
  81.1 2.7 %collective-permute-start.24 = (f32[4,4,256]{2,1,0:T(4,128)S(1)}, f32[4,4,256]{2,1,0:T(4,128)S(1)}, u32[]{:S(2)}, u32[]{:S(2)}) collective-permute-start(f32[4,4,256]{2,1,0:T(4,128)S(1)} %get-tuple-element.132), channel_id=1, source_target_pairs={{0,18},{1,19},{2,16},{3,17},{4,22},{5,23},{6,20},{7,21},{8,26},{9,... | collective-permute-start | bytes 49160 | tf_op jit(solution)/shard_map/ppermute | solution.py:307
  83.7 1.3 %collective-permute-start.25 = (f32[4,4,256]{2,1,0:T(4,128)S(1)}, f32[4,4,256]{2,1,0:T(4,128)S(1)}, u32[]{:S(2)}, u32[]{:S(2)}) collective-permute-start(f32[4,4,256]{2,1,0:T(4,128)S(1)} %get-tuple-element.133.a_ref), channel_id=1, source_target_pairs={{0,16},{1,17},{2,18},{3,19},{4,20},{5,21},{6,22},{7,23},{8,24},{9,... | collective-permute-start | bytes 49160 | tf_op jit(solution)/shard_map/ppermute | solution.py:307
  85.0 0.5 collective-permute-start.26
  85.5 1.1 %collective-permute-done.24.d_ref = f32[4,4,256]{2,1,0:T(4,128)S(1)} collective-permute-done((f32[4,4,256]{2,1,0:T(4,128)S(1)}, f32[4,4,256]{2,1,0:T(4,128)S(1)}, u32[]{:S(2)}, u32[]{:S(2)}) %collective-permute-start.24) | collective-permute-done | bytes 16416 | tf_op jit(solution)/shard_map/ppermute | solution.py:307
  86.7 1.7 %collective-permute-done.25.b_ref = f32[4,4,256]{2,1,0:T(4,128)S(1)} collective-permute-done((f32[4,4,256]{2,1,0:T(4,128)S(1)}, f32[4,4,256]{2,1,0:T(4,128)S(1)}, u32[]{:S(2)}, u32[]{:S(2)}) %collective-permute-start.25) | collective-permute-done | bytes 16416 | tf_op jit(solution)/shard_map/ppermute | solution.py:307
  88.4 0.4 collective-permute-done.26.c_ref
  88.9 1.2 %collective-permute-done.27.refs_1_ = f32[8,256]{1,0:T(8,128)S(1)} collective-permute-done((f32[8,256]{1,0:T(8,128)S(1)}, f32[8,256]{1,0:T(8,128)S(1)}, u32[]{:S(2)}, u32[]{:S(2)}) %collective-permute-start.27) | collective-permute-done | bytes 8224 | tf_op jit(solution)/shard_map/ppermute | solution.py:307
  90.0 1.2 %place.1 = (f32[2048]{0:T(1024)}, f32[2048]{0:T(1024)}) custom-call(s32[4]{0:T(128)S(1)} %copy-done.1, f32[8,256]{1,0:T(8,128)S(1)} %get-tuple-element.134.refs_0_, f32[8,256]{1,0:T(8,128)S(1)} %collective-permute-done.27.refs_1_), custom_call_target="tpu_custom_call" | custom-call | tf_op jit(solution)/shard_map/place/pallas_call | solution.py:274
  (30 shorter events, 0.5 us)
Async XLA Ops:
  0.6 15.5 %copy-start = (bf16[256,4016]{0,1:T(8,128)(2,1)S(1)}, bf16[256,4016]{0,1:T(8,128)(2,1)}, u32[]{:S(2)}) copy-start(bf16[256,4016]{0,1:T(8,128)(2,1)} %param.7) | copy-start | bytes 6168580
  0.6 33.5 %collective-permute-start.9 = (bf16[4016,256]{1,0:T(8,128)(2,1)}, bf16[4016,256]{1,0:T(8,128)(2,1)S(1)}, u32[]{:S(2)}, u32[]{:S(2)}) collective-permute-start(bf16[4016,256]{1,0:T(8,128)(2,1)} %bitcast.1), channel_id=1, source_target_pairs={{0,1},{1,0},{2,3},{3,2},{4,5},{5,4},{6,7},{7,6},{8,9},{9,8},{10,11... | collective-permute-start | bytes 6168584 | tf_op jit(solution)/shard_map/ppermute | solution.py:307
  2.4 6.6 %collective-permute-start.2 = (bf16[272,256]{1,0:T(8,128)(2,1)S(1)}, bf16[272,256]{1,0:T(8,128)(2,1)S(1)}, u32[]{:S(2)}, u32[]{:S(2)}) collective-permute-start(bf16[272,256]{1,0:T(8,128)(2,1)S(1)} %get-tuple-element.72), channel_id=1, source_target_pairs={{0,3},{1,2},{2,1},{3,0},{4,7},{5,6},{6,5},{7,4},{8,11},{9,10},{10,... | collective-permute-start | bytes 417800 | tf_op jit(solution)/shard_map/ppermute | solution.py:307
  5.0 5.6 %collective-permute-start = (bf16[272,256]{1,0:T(8,128)(2,1)S(1)}, bf16[272,256]{1,0:T(8,128)(2,1)S(1)}, u32[]{:S(2)}, u32[]{:S(2)}) collective-permute-start(bf16[272,256]{1,0:T(8,128)(2,1)S(1)} %get-tuple-element.70), channel_id=1, source_target_pairs={{0,1},{1,0},{2,3},{3,2},{4,5},{5,4},{6,7},{7,6},{8,9},{9,8},{10,11... | collective-permute-start | bytes 417800 | tf_op jit(solution)/shard_map/ppermute | solution.py:307
  5.2 7.1 %collective-permute-start.1 = (bf16[272,256]{1,0:T(8,128)(2,1)S(1)}, bf16[272,256]{1,0:T(8,128)(2,1)S(1)}, u32[]{:S(2)}, u32[]{:S(2)}) collective-permute-start(bf16[272,256]{1,0:T(8,128)(2,1)S(1)} %get-tuple-element.71), channel_id=1, source_target_pairs={{0,2},{1,3},{2,0},{3,1},{4,6},{5,7},{6,4},{7,5},{8,10},{9,11},{10,... | collective-permute-start | bytes 417800 | tf_op jit(solution)/shard_map/ppermute | solution.py:307
  9.0 19.3 %collective-permute-start.5 = (bf16[1280,256]{1,0:T(8,128)(2,1)S(1)}, bf16[1280,256]{1,0:T(8,128)(2,1)S(1)}, u32[]{:S(2)}, u32[]{:S(2)}) collective-permute-start(bf16[1280,256]{1,0:T(8,128)(2,1)S(1)} %slice.44), channel_id=1, source_target_pairs={{0,2},{1,3},{2,0},{3,1},{4,6},{5,7},{6,4},{7,5},{8,10},{9,11},{10,... | collective-permute-start | bytes 1966088 | tf_op jit(solution)/shard_map/ppermute | solution.py:307
  12.7 21.5 %copy-start.1 = (s32[4]{0:T(128)S(1)}, s32[4]{0:T(128)}, u32[]{:S(2)}) copy-start(s32[4]{0:T(128)} %seq_ref.9) | copy-start | bytes 52
  12.7 15.7 %collective-permute-start.3 = (bf16[1024,256]{1,0:T(8,128)(2,1)S(1)}, bf16[1024,256]{1,0:T(8,128)(2,1)S(1)}, u32[]{:S(2)}, u32[]{:S(2)}) collective-permute-start(bf16[1024,256]{1,0:T(8,128)(2,1)S(1)} %get-tuple-element.74.refs_0_), channel_id=1, source_target_pairs={{0,8},{1,9},{2,10},{3,11},{4,12},{5,13},{6,14},{7,15},{8,16},{9,17... | collective-permute-start | bytes 1572872 | tf_op jit(solution)/shard_map/ppermute | solution.py:307
  14.6 13.7 %collective-permute-start.4 = (bf16[1024,256]{1,0:T(8,128)(2,1)S(1)}, bf16[1024,256]{1,0:T(8,128)(2,1)S(1)}, u32[]{:S(2)}, u32[]{:S(2)}) collective-permute-start(bf16[1024,256]{1,0:T(8,128)(2,1)S(1)} %get-tuple-element.74.refs_0_), channel_id=1, source_target_pairs={{0,4},{1,5},{2,6},{3,7},{4,0},{5,1},{6,2},{7,3},{8,12},{9,13},{10,... | collective-permute-start | bytes 1572872 | tf_op jit(solution)/shard_map/ppermute | solution.py:307
  16.2 27.3 %collective-permute-start.8 = (bf16[1536,256]{1,0:T(8,128)(2,1)S(1)}, bf16[1536,256]{1,0:T(8,128)(2,1)S(1)}, u32[]{:S(2)}, u32[]{:S(2)}) collective-permute-start(bf16[1536,256]{1,0:T(8,128)(2,1)S(1)} %slice.45), channel_id=1, source_target_pairs={{0,2},{1,3},{2,0},{3,1},{4,6},{5,7},{6,4},{7,5},{8,10},{9,11},{10,... | collective-permute-start | bytes 2359304 | tf_op jit(solution)/shard_map/ppermute | solution.py:307
  28.4 2.6 %collective-permute-start.10 = (bf16[640,256]{1,0:T(8,128)(2,1)S(1)}, bf16[640,256]{1,0:T(8,128)(2,1)S(1)}, u32[]{:S(2)}, u32[]{:S(2)}) collective-permute-start(bf16[640,256]{1,0:T(8,128)(2,1)S(1)} %get-tuple-element.139), channel_id=1, source_target_pairs={{0,1},{1,0},{2,3},{3,2},{4,5},{5,4},{6,7},{7,6},{8,9},{9,8},{10,11... | collective-permute-start | bytes 983048 | tf_op jit(solution)/shard_map/ppermute | solution.py:307
  28.5 16.1 %collective-permute-start.6 = (bf16[1024,256]{1,0:T(8,128)(2,1)S(1)}, bf16[1024,256]{1,0:T(8,128)(2,1)S(1)}, u32[]{:S(2)}, u32[]{:S(2)}) collective-permute-start(bf16[1024,256]{1,0:T(8,128)(2,1)S(1)} %collective-permute-done.3.refs_2_), channel_id=1, source_target_pairs={{0,8},{1,9},{2,10},{3,11},{4,12},{5,13},{6,14},{7,15},{8,16},{9,17... | collective-permute-start | bytes 1572872 | tf_op jit(solution)/shard_map/ppermute | solution.py:307
  29.5 15.1 %collective-permute-start.7 = (bf16[1024,256]{1,0:T(8,128)(2,1)S(1)}, bf16[1024,256]{1,0:T(8,128)(2,1)S(1)}, u32[]{:S(2)}, u32[]{:S(2)}) collective-permute-start(bf16[1024,256]{1,0:T(8,128)(2,1)S(1)} %collective-permute-done.3.refs_2_), channel_id=1, source_target_pairs={{0,4},{1,5},{2,6},{3,7},{4,0},{5,1},{6,2},{7,3},{8,12},{9,13},{10,... | collective-permute-start | bytes 1572872 | tf_op jit(solution)/shard_map/ppermute | solution.py:307
  31.0 1.6 %collective-permute-start.11 = (bf16[640,256]{1,0:T(8,128)(2,1)S(1)}, bf16[640,256]{1,0:T(8,128)(2,1)S(1)}, u32[]{:S(2)}, u32[]{:S(2)}) collective-permute-start(bf16[640,256]{1,0:T(8,128)(2,1)S(1)} %get-tuple-element.138), channel_id=1, source_target_pairs={{0,1},{1,0},{2,3},{3,2},{4,5},{5,4},{6,7},{7,6},{8,9},{9,8},{10,11... | collective-permute-start | bytes 983048 | tf_op jit(solution)/shard_map/ppermute | solution.py:307
  32.7 23.7 %collective-permute-start.14 = (bf16[1200,256]{1,0:T(8,128)(2,1)S(1)}, bf16[1200,256]{1,0:T(8,128)(2,1)S(1)}, u32[]{:S(2)}, u32[]{:S(2)}) collective-permute-start(bf16[1200,256]{1,0:T(8,128)(2,1)S(1)} %slice.46), channel_id=1, source_target_pairs={{0,2},{1,3},{2,0},{3,1},{4,6},{5,7},{6,4},{7,5},{8,10},{9,11},{10,... | collective-permute-start | bytes 1843208 | tf_op jit(solution)/shard_map/ppermute | solution.py:307
  44.7 2.6 %collective-permute-start.15 = (bf16[768,256]{1,0:T(8,128)(2,1)S(1)}, bf16[768,256]{1,0:T(8,128)(2,1)S(1)}, u32[]{:S(2)}, u32[]{:S(2)}) collective-permute-start(bf16[768,256]{1,0:T(8,128)(2,1)S(1)} %get-tuple-element.137), channel_id=1, source_target_pairs={{0,1},{1,0},{2,3},{3,2},{4,5},{5,4},{6,7},{7,6},{8,9},{9,8},{10,11... | collective-permute-start | bytes 1179656 | tf_op jit(solution)/shard_map/ppermute | solution.py:307
  44.7 2.5 %collective-permute-start.16 = (bf16[768,256]{1,0:T(8,128)(2,1)S(1)}, bf16[768,256]{1,0:T(8,128)(2,1)S(1)}, u32[]{:S(2)}, u32[]{:S(2)}) collective-permute-start(bf16[768,256]{1,0:T(8,128)(2,1)S(1)} %get-tuple-element.136), channel_id=1, source_target_pairs={{0,1},{1,0},{2,3},{3,2},{4,5},{5,4},{6,7},{7,6},{8,9},{9,8},{10,11... | collective-permute-start | bytes 1179656 | tf_op jit(solution)/shard_map/ppermute | solution.py:307
  45.2 15.7 %collective-permute-start.12 = (bf16[1024,256]{1,0:T(8,128)(2,1)S(1)}, bf16[1024,256]{1,0:T(8,128)(2,1)S(1)}, u32[]{:S(2)}, u32[]{:S(2)}) collective-permute-start(bf16[1024,256]{1,0:T(8,128)(2,1)S(1)} %collective-permute-done.6.refs_4_), channel_id=1, source_target_pairs={{0,8},{1,9},{2,10},{3,11},{4,12},{5,13},{6,14},{7,15},{8,16},{9,17... | collective-permute-start | bytes 1572872 | tf_op jit(solution)/shard_map/ppermute | solution.py:307
  45.7 15.2 %collective-permute-start.13 = (bf16[1024,256]{1,0:T(8,128)(2,1)S(1)}, bf16[1024,256]{1,0:T(8,128)(2,1)S(1)}, u32[]{:S(2)}, u32[]{:S(2)}) collective-permute-start(bf16[1024,256]{1,0:T(8,128)(2,1)S(1)} %collective-permute-done.6.refs_4_), channel_id=1, source_target_pairs={{0,4},{1,5},{2,6},{3,7},{4,0},{5,1},{6,2},{7,3},{8,12},{9,13},{10,... | collective-permute-start | bytes 1572872 | tf_op jit(solution)/shard_map/ppermute | solution.py:307
  56.3 4.6 %collective-permute-start.17 = (bf16[608,256]{1,0:T(8,128)(2,1)S(1)}, bf16[608,256]{1,0:T(8,128)(2,1)S(1)}, u32[]{:S(2)}, u32[]{:S(2)}) collective-permute-start(bf16[608,256]{1,0:T(8,128)(2,1)S(1)} %slice.40), channel_id=1, source_target_pairs={{0,1},{1,0},{2,3},{3,2},{4,5},{5,4},{6,7},{7,6},{8,9},{9,8},{10,11... | collective-permute-start | bytes 933896 | tf_op jit(solution)/shard_map/ppermute | solution.py:307
  56.5 4.5 %collective-permute-start.18 = (bf16[592,256]{1,0:T(8,128)(2,1)S(1)}, bf16[592,256]{1,0:T(8,128)(2,1)S(1)}, u32[]{:S(2)}, u32[]{:S(2)}) collective-permute-start(bf16[592,256]{1,0:T(8,128)(2,1)S(1)} %slice.41), channel_id=1, source_target_pairs={{0,1},{1,0},{2,3},{3,2},{4,5},{5,4},{6,7},{7,6},{8,9},{9,8},{10,11... | collective-permute-start | bytes 909320 | tf_op jit(solution)/shard_map/ppermute | solution.py:307
  61.0 11.9 %collective-permute-start.19 = (bf16[512,256]{1,0:T(8,128)(2,1)S(1)}, bf16[512,256]{1,0:T(8,128)(2,1)S(1)}, u32[]{:S(2)}, u32[]{:S(2)}) collective-permute-start(bf16[512,256]{1,0:T(8,128)(2,1)S(1)} %slice.42), channel_id=1, source_target_pairs={{0,4},{1,5},{2,6},{3,7},{4,0},{5,1},{6,2},{7,3},{8,12},{9,13},{10,... | collective-permute-start | bytes 786440 | tf_op jit(solution)/shard_map/ppermute | solution.py:307
  62.6 10.3 %collective-permute-start.20 = (bf16[512,256]{1,0:T(8,128)(2,1)S(1)}, bf16[512,256]{1,0:T(8,128)(2,1)S(1)}, u32[]{:S(2)}, u32[]{:S(2)}) collective-permute-start(bf16[512,256]{1,0:T(8,128)(2,1)S(1)} %slice.43), channel_id=1, source_target_pairs={{0,8},{1,9},{2,10},{3,11},{4,12},{5,13},{6,14},{7,15},{8,16},{9,17... | collective-permute-start | bytes 786440 | tf_op jit(solution)/shard_map/ppermute | solution.py:307
  73.6 5.3 %collective-permute-start.21 = (f32[4,8,256]{2,1,0:T(8,128)S(1)}, f32[4,8,256]{2,1,0:T(8,128)S(1)}, u32[]{:S(2)}, u32[]{:S(2)}) collective-permute-start(f32[4,8,256]{2,1,0:T(8,128)S(1)} %logits.7.refs_0_), channel_id=1, source_target_pairs={{0,12},{1,13},{2,14},{3,15},{4,8},{5,9},{6,10},{7,11},{8,4},{9,5},... | collective-permute-start | bytes 98312 | tf_op jit(solution)/shard_map/ppermute | solution.py:307
  77.0 3.9 %collective-permute-start.22 = (f32[4,8,256]{2,1,0:T(8,128)S(1)}, f32[4,8,256]{2,1,0:T(8,128)S(1)}, u32[]{:S(2)}, u32[]{:S(2)}) collective-permute-start(f32[4,8,256]{2,1,0:T(8,128)S(1)} %logits.7.refs_0_), channel_id=1, source_target_pairs={{0,8},{1,9},{2,10},{3,11},{4,12},{5,13},{6,14},{7,15},{8,0},{9,1},... | collective-permute-start | bytes 98312 | tf_op jit(solution)/shard_map/ppermute | solution.py:307
  77.1 3.9 %collective-permute-start.23 = (f32[4,8,256]{2,1,0:T(8,128)S(1)}, f32[4,8,256]{2,1,0:T(8,128)S(1)}, u32[]{:S(2)}, u32[]{:S(2)}) collective-permute-start(f32[4,8,256]{2,1,0:T(8,128)S(1)} %logits.7.refs_0_), channel_id=1, source_target_pairs={{0,4},{1,5},{2,6},{3,7},{4,0},{5,1},{6,2},{7,3},{8,12},{9,13},{10,... | collective-permute-start | bytes 98312 | tf_op jit(solution)/shard_map/ppermute | solution.py:307
  81.1 5.6 %collective-permute-start.24 = (f32[4,4,256]{2,1,0:T(4,128)S(1)}, f32[4,4,256]{2,1,0:T(4,128)S(1)}, u32[]{:S(2)}, u32[]{:S(2)}) collective-permute-start(f32[4,4,256]{2,1,0:T(4,128)S(1)} %get-tuple-element.132), channel_id=1, source_target_pairs={{0,18},{1,19},{2,16},{3,17},{4,22},{5,23},{6,20},{7,21},{8,26},{9,... | collective-permute-start | bytes 49160 | tf_op jit(solution)/shard_map/ppermute | solution.py:307
  83.7 4.6 %collective-permute-start.25 = (f32[4,4,256]{2,1,0:T(4,128)S(1)}, f32[4,4,256]{2,1,0:T(4,128)S(1)}, u32[]{:S(2)}, u32[]{:S(2)}) collective-permute-start(f32[4,4,256]{2,1,0:T(4,128)S(1)} %get-tuple-element.133.a_ref), channel_id=1, source_target_pairs={{0,16},{1,17},{2,18},{3,19},{4,20},{5,21},{6,22},{7,23},{8,24},{9,... | collective-permute-start | bytes 49160 | tf_op jit(solution)/shard_map/ppermute | solution.py:307
  85.0 3.7 %collective-permute-start.26 = (f32[4,4,256]{2,1,0:T(4,128)S(1)}, f32[4,4,256]{2,1,0:T(4,128)S(1)}, u32[]{:S(2)}, u32[]{:S(2)}) collective-permute-start(f32[4,4,256]{2,1,0:T(4,128)S(1)} %get-tuple-element.132), channel_id=1, source_target_pairs={{0,2},{1,3},{2,0},{3,1},{4,6},{5,7},{6,4},{7,5},{8,10},{9,11},{10,... | collective-permute-start | bytes 49160 | tf_op jit(solution)/shard_map/ppermute | solution.py:307
  88.8 1.2 %collective-permute-start.27 = (f32[8,256]{1,0:T(8,128)S(1)}, f32[8,256]{1,0:T(8,128)S(1)}, u32[]{:S(2)}, u32[]{:S(2)}) collective-permute-start(f32[8,256]{1,0:T(8,128)S(1)} %get-tuple-element.135), channel_id=1, source_target_pairs={{0,1},{1,0},{2,3},{3,2},{4,5},{5,4},{6,7},{7,6},{8,9},{9,8},{10,11... | collective-permute-start | bytes 24584 | tf_op jit(solution)/shard_map/ppermute | solution.py:307

commit v5 on v4

--- a/solution.py
+++ b/solution.py
@@ -283,7 +283,7 @@
     )(*args)
 
 
-def chunk_spans(columns, shares=(0.32, 0.701)):
+def chunk_spans(columns, shares=(0.32, 0.685)):
     ends = [0] + [64 * round(columns * share / 64) for share in shares] + [columns]
     return [(a, b - a) for a, b in zip(ends, ends[1:])]
 
@@ -415,6 +415,8 @@
         if far:
             near_chunk(dz - 1, far)
         whole = len(chunks)
+        if dz == 0:
+            tied["near"] = near
         if dz < len(spans):
             tied["far"] = far_chunk(dz, pieces[-1:])
         if fast and dz:
@@ -429,6 +431,7 @@
         onward, arrived, tied = lax.optimization_barrier((onward, arrived, tied))
         states = tied.get("states", states)
         far = tied.get("far", {})
+        near = tied.get("near", near)
         chunks[whole:] = tied.get("last", [])
         groups.update(arrived)
         if not end:

time: 91.4 us -> 91.5 us (level)
  Pallas kernels: 23.6 us -> 20.5 us
  starting transfers between devices: 28.5 us -> 30.3 us
  waiting for transfers between devices: 36.8 us -> 38 us
    pallas_call x9, Pallas kernels: 23.6 us -> 20.5 us  [call(): pl.pallas_call(kernel, out_shape=out_shape, in_specs=[SMEM] * smem + [HBM...]
    ppermute x28, starting transfers between devices: 28.5 us -> 30.3 us  [on_device(): move = lambda value, perm: lax.ppermute(value, AXES, perm)]
    ppermute x28, waiting for transfers between devices: 36.8 us -> 38 us  [on_device(): move = lambda value, perm: lax.ppermute(value, AXES, perm)]
  transfers between devices with their start and end apart: 28 -> 28, of which waited for: 15 -> 15; matrix products, arithmetic and copies ran while one was open for 2% -> 2% of each run, Pallas kernels for 22% -> 19%
where the time goes in v5:
time: 91.5 us; the launch traced here: 91 us
  waiting for transfers between devices  38 us (42%)
  starting transfers between devices  30.3 us (33%)
  Pallas kernels  20.5 us (22%)
  local copies, waits for them, and re-layouts  1.41 us (2%)
    ppermute x28, waiting for transfers between devices, on_device(): move = lambda value, perm: lax.ppermute(value, AXES, perm)  38 us
    ppermute x28, starting transfers between devices, on_device(): move = lambda value, perm: lax.ppermute(value, AXES, perm)  30.3 us
    pallas_call x9, Pallas kernels, call(): pl.pallas_call(kernel, out_shape=out_shape, in_specs=[SMEM] * smem + [HBM...  20.5 us
  transfers between devices with their start and end apart: 28, of which 15 were waited for; matrix products, arithmetic and copies ran while one was open for 2% of the time, Pallas kernels for 19%

profile of v5, /device:TPU:0, one launch (start us, length us, event | category | flops | bytes accessed | tf_op | source)
XLA Modules:
  0.0 91.0 jit_solution(12830840579517514309)
XLA Ops:
  0.6 0.5 collective-permute-start.6
  1.2 1.3 %send.1 = (bf16[272,256]{1,0:T(8,128)(2,1)S(1)}, bf16[272,256]{1,0:T(8,128)(2,1)S(1)}, bf16[272,256]{1,0:T(8,128)(2,1)S(1)}, bf16[272,256]{1,0:T(8,128)(2,1)S(1)}) custom-call(bf16[1024,256]{1,0:T(8,128)(2,1)} %h_ref.1, f32[256]{0:T(256)} %gain_hbm.1, s32[2048]{0:T(1024)} %ids_hbm.1), custom_call_target="tpu_custom_call" | custom-call | tf_op jit(solution)/shard_map/send/pallas_call | solution.py:274
  2.4 2.6 %collective-permute-start.2 = (bf16[272,256]{1,0:T(8,128)(2,1)S(1)}, bf16[272,256]{1,0:T(8,128)(2,1)S(1)}, u32[]{:S(2)}, u32[]{:S(2)}) collective-permute-start(bf16[272,256]{1,0:T(8,128)(2,1)S(1)} %get-tuple-element.73), channel_id=1, source_target_pairs={{0,3},{1,2},{2,1},{3,0},{4,7},{5,6},{6,5},{7,4},{8,11},{9,10},{10,... | collective-permute-start | bytes 417800 | tf_op jit(solution)/shard_map/ppermute | solution.py:307
  5.0 0.2 collective-permute-start
  5.2 0.3 collective-permute-start.1
  5.5 1.1 %slice.44 = bf16[1280,256]{1,0:T(8,128)(2,1)S(1)} slice(bf16[4016,256]{1,0:T(8,128)(2,1)} %bitcast.2), slice={[0:1280], [0:256]} | slice | bytes 1310720 | tf_op jit(solution)/shard_map/slice | solution.py:339
  6.6 2.4 %collective-permute-done.2.refs_3_ = bf16[272,256]{1,0:T(8,128)(2,1)S(1)} collective-permute-done((bf16[272,256]{1,0:T(8,128)(2,1)S(1)}, bf16[272,256]{1,0:T(8,128)(2,1)S(1)}, u32[]{:S(2)}, u32[]{:S(2)}) %collective-permute-start.2) | collective-permute-done | bytes 139296 | tf_op jit(solution)/shard_map/ppermute | solution.py:307
  9.0 1.6 %collective-permute-start.5 = (bf16[1280,256]{1,0:T(8,128)(2,1)S(1)}, bf16[1280,256]{1,0:T(8,128)(2,1)S(1)}, u32[]{:S(2)}, u32[]{:S(2)}) collective-permute-start(bf16[1280,256]{1,0:T(8,128)(2,1)S(1)} %slice.44), channel_id=1, source_target_pairs={{0,2},{1,3},{2,0},{3,1},{4,6},{5,7},{6,4},{7,5},{8,10},{9,11},{10,... | collective-permute-start | bytes 1966088 | tf_op jit(solution)/shard_map/ppermute | solution.py:307
  10.6 1.7 %collective-permute-done.1.refs_2_ = bf16[272,256]{1,0:T(8,128)(2,1)S(1)} collective-permute-done((bf16[272,256]{1,0:T(8,128)(2,1)S(1)}, bf16[272,256]{1,0:T(8,128)(2,1)S(1)}, u32[]{:S(2)}, u32[]{:S(2)}) %collective-permute-start.1) | collective-permute-done | bytes 139296 | tf_op jit(solution)/shard_map/ppermute | solution.py:307
  12.3 0.4 norm.1
  12.7 1.9 %collective-permute-start.3 = (bf16[1024,256]{1,0:T(8,128)(2,1)S(1)}, bf16[1024,256]{1,0:T(8,128)(2,1)S(1)}, u32[]{:S(2)}, u32[]{:S(2)}) collective-permute-start(bf16[1024,256]{1,0:T(8,128)(2,1)S(1)} %get-tuple-element.75.refs_0_), channel_id=1, source_target_pairs={{0,8},{1,9},{2,10},{3,11},{4,12},{5,13},{6,14},{7,15},{8,16},{9,17... | collective-permute-start | bytes 1572872 | tf_op jit(solution)/shard_map/ppermute | solution.py:307
  14.6 1.5 %collective-permute-start.4 = (bf16[1024,256]{1,0:T(8,128)(2,1)S(1)}, bf16[1024,256]{1,0:T(8,128)(2,1)S(1)}, u32[]{:S(2)}, u32[]{:S(2)}) collective-permute-start(bf16[1024,256]{1,0:T(8,128)(2,1)S(1)} %get-tuple-element.75.refs_0_), channel_id=1, source_target_pairs={{0,4},{1,5},{2,6},{3,7},{4,0},{5,1},{6,2},{7,3},{8,12},{9,13},{10,... | collective-permute-start | bytes 1572872 | tf_op jit(solution)/shard_map/ppermute | solution.py:307
  16.2 1.6 %collective-permute-start.9 = (bf16[1472,256]{1,0:T(8,128)(2,1)S(1)}, bf16[1472,256]{1,0:T(8,128)(2,1)S(1)}, u32[]{:S(2)}, u32[]{:S(2)}) collective-permute-start(bf16[1472,256]{1,0:T(8,128)(2,1)S(1)} %slice.45), channel_id=1, source_target_pairs={{0,2},{1,3},{2,0},{3,1},{4,6},{5,7},{6,4},{7,5},{8,10},{9,11},{10,... | collective-permute-start | bytes 2261000 | tf_op jit(solution)/shard_map/ppermute | solution.py:307
  17.8 10.6 %collective-permute-done.3.refs_2_ = bf16[1024,256]{1,0:T(8,128)(2,1)S(1)} collective-permute-done((bf16[1024,256]{1,0:T(8,128)(2,1)S(1)}, bf16[1024,256]{1,0:T(8,128)(2,1)S(1)}, u32[]{:S(2)}, u32[]{:S(2)}) %collective-permute-start.3) | collective-permute-done | bytes 524320 | tf_op jit(solution)/shard_map/ppermute | solution.py:307
  28.4 1.0 %collective-permute-start.7 = (bf16[1024,256]{1,0:T(8,128)(2,1)S(1)}, bf16[1024,256]{1,0:T(8,128)(2,1)S(1)}, u32[]{:S(2)}, u32[]{:S(2)}) collective-permute-start(bf16[1024,256]{1,0:T(8,128)(2,1)S(1)} %collective-permute-done.3.refs_2_), channel_id=1, source_target_pairs={{0,8},{1,9},{2,10},{3,11},{4,12},{5,13},{6,14},{7,15},{8,16},{9,17... | collective-permute-start | bytes 1572872 | tf_op jit(solution)/shard_map/ppermute | solution.py:307
  29.4 1.5 %collective-permute-start.8 = (bf16[1024,256]{1,0:T(8,128)(2,1)S(1)}, bf16[1024,256]{1,0:T(8,128)(2,1)S(1)}, u32[]{:S(2)}, u32[]{:S(2)}) collective-permute-start(bf16[1024,256]{1,0:T(8,128)(2,1)S(1)} %collective-permute-done.3.refs_2_), channel_id=1, source_target_pairs={{0,4},{1,5},{2,6},{3,7},{4,0},{5,1},{6,2},{7,3},{8,12},{9,13},{10,... | collective-permute-start | bytes 1572872 | tf_op jit(solution)/shard_map/ppermute | solution.py:307
  30.9 0.1 collective-permute-start.10
  31.0 0.5 collective-permute-start.11
  31.5 1.1 %collective-permute-done.10.refs_6_.refs_8_.refs_10_.refs_5_ = bf16[640,256]{1,0:T(8,128)(2,1)S(1)} collective-permute-done((bf16[640,256]{1,0:T(8,128)(2,1)S(1)}, bf16[640,256]{1,0:T(8,128)(2,1)S(1)}, u32[]{:S(2)}, u32[]{:S(2)}) %collective-permute-start.10) | collective-permute-done | bytes 327712 | tf_op jit(solution)/shard_map/ppermute | solution.py:307
  32.6 1.5 %collective-permute-start.14 = (bf16[1264,256]{1,0:T(8,128)(2,1)S(1)}, bf16[1264,256]{1,0:T(8,128)(2,1)S(1)}, u32[]{:S(2)}, u32[]{:S(2)}) collective-permute-start(bf16[1264,256]{1,0:T(8,128)(2,1)S(1)} %slice.46), channel_id=1, source_target_pairs={{0,2},{1,3},{2,0},{3,1},{4,6},{5,7},{6,4},{7,5},{8,10},{9,11},{10,... | collective-permute-start | bytes 1941512 | tf_op jit(solution)/shard_map/ppermute | solution.py:307
  34.1 2.6 %logits.4 = (f32[4,8,256]{2,1,0:T(8,128)S(1)}, f32[4,8,256]{2,1,0:T(8,128)S(1)}, f32[4,8,256]{2,1,0:T(8,128)S(1)}) custom-call(s32[4]{0:T(128)S(1)} %copy-done.1, s32[8,256]{1,0:T(8,128)S(1)} %get-tuple-element.74.ids_ref, bf16[1024,256]{1,0:T(8,128)(2,1)S(1)} %get-tuple-element.75.refs_0_, bf16[1024,256]{1,0:T(8,128)(2,1)S(1)} %collective-permute-done.4.refs_1_, ...), custom_call_target="tpu_custom_call" | custom-call | tf_op jit(solution)/shard_map/logits/pallas_call | solution.py:274
  36.8 6.0 %collective-permute-done.9.refs_10_.refs_12_.refs_7_ = bf16[1472,256]{1,0:T(8,128)(2,1)S(1)} collective-permute-done((bf16[1472,256]{1,0:T(8,128)(2,1)S(1)}, bf16[1472,256]{1,0:T(8,128)(2,1)S(1)}, u32[]{:S(2)}, u32[]{:S(2)}) %collective-permute-start.9) | collective-permute-done | bytes 753696 | tf_op jit(solution)/shard_map/ppermute | solution.py:307
  42.7 0.3 collective-permute-done.7.refs_4_
  43.1 0.1 collective-permute-start.15
  43.2 0.5 collective-permute-start.16
  43.7 1.3 %collective-permute-start.12 = (bf16[1024,256]{1,0:T(8,128)(2,1)S(1)}, bf16[1024,256]{1,0:T(8,128)(2,1)S(1)}, u32[]{:S(2)}, u32[]{:S(2)}) collective-permute-start(bf16[1024,256]{1,0:T(8,128)(2,1)S(1)} %collective-permute-done.7.refs_4_), channel_id=1, source_target_pairs={{0,8},{1,9},{2,10},{3,11},{4,12},{5,13},{6,14},{7,15},{8,16},{9,17... | collective-permute-start | bytes 1572872 | tf_op jit(solution)/shard_map/ppermute | solution.py:307
  45.0 1.5 %collective-permute-start.13 = (bf16[1024,256]{1,0:T(8,128)(2,1)S(1)}, bf16[1024,256]{1,0:T(8,128)(2,1)S(1)}, u32[]{:S(2)}, u32[]{:S(2)}) collective-permute-start(bf16[1024,256]{1,0:T(8,128)(2,1)S(1)} %collective-permute-done.7.refs_4_), channel_id=1, source_target_pairs={{0,4},{1,5},{2,6},{3,7},{4,0},{5,1},{6,2},{7,3},{8,12},{9,13},{10,... | collective-permute-start | bytes 1572872 | tf_op jit(solution)/shard_map/ppermute | solution.py:307
  46.5 5.0 %logits.5 = (f32[4,8,256]{2,1,0:T(8,128)S(1)}, f32[4,8,256]{2,1,0:T(8,128)S(1)}, f32[4,8,256]{2,1,0:T(8,128)S(1)}, f32[4,8,256]{2,1,0:T(8,128)S(1)}, f32[4,8,256]{2,1,0:T(8,128)S(1)}) custom-call(s32[4]{0:T(128)S(1)} %copy-done.1, s32[8,256]{1,0:T(8,128)S(1)} %get-tuple-element.74.ids_ref, bf16[1024,256]{1,0:T(8,128)(2,1)S(1)} %get-tuple-element.75.refs_0_, ...), custom_call_target="tpu_custom_call" | custom-call | tf_op jit(solution)/shard_map/logits/pallas_call | solution.py:274
  51.6 4.7 %collective-permute-done.14.refs_17_.refs_21_.refs_12_.refs_16_ = bf16[1264,256]{1,0:T(8,128)(2,1)S(1)} collective-permute-done((bf16[1264,256]{1,0:T(8,128)(2,1)S(1)}, bf16[1264,256]{1,0:T(8,128)(2,1)S(1)}, u32[]{:S(2)}, u32[]{:S(2)}) %collective-permute-start.14) | collective-permute-done | bytes 647200 | tf_op jit(solution)/shard_map/ppermute | solution.py:307
  56.3 0.1 collective-permute-start.17
  56.5 0.6 collective-permute-start.18
  57.0 2.4 %collective-permute-done.12.refs_6_ = bf16[1024,256]{1,0:T(8,128)(2,1)S(1)} collective-permute-done((bf16[1024,256]{1,0:T(8,128)(2,1)S(1)}, bf16[1024,256]{1,0:T(8,128)(2,1)S(1)}, u32[]{:S(2)}, u32[]{:S(2)}) %collective-permute-start.12) | collective-permute-done | bytes 524320 | tf_op jit(solution)/shard_map/ppermute | solution.py:307
  59.4 1.4 %collective-permute-start.19 = (bf16[512,256]{1,0:T(8,128)(2,1)S(1)}, bf16[512,256]{1,0:T(8,128)(2,1)S(1)}, u32[]{:S(2)}, u32[]{:S(2)}) collective-permute-start(bf16[512,256]{1,0:T(8,128)(2,1)S(1)} %slice.42), channel_id=1, source_target_pairs={{0,4},{1,5},{2,6},{3,7},{4,0},{5,1},{6,2},{7,3},{8,12},{9,13},{10,... | collective-permute-start | bytes 786440 | tf_op jit(solution)/shard_map/ppermute | solution.py:307
  60.9 1.1 %collective-permute-start.20 = (bf16[512,256]{1,0:T(8,128)(2,1)S(1)}, bf16[512,256]{1,0:T(8,128)(2,1)S(1)}, u32[]{:S(2)}, u32[]{:S(2)}) collective-permute-start(bf16[512,256]{1,0:T(8,128)(2,1)S(1)} %slice.43), channel_id=1, source_target_pairs={{0,8},{1,9},{2,10},{3,11},{4,12},{5,13},{6,14},{7,15},{8,16},{9,17... | collective-permute-start | bytes 786440 | tf_op jit(solution)/shard_map/ppermute | solution.py:307
  62.0 9.3 %logits.6 = (f32[4,8,256]{2,1,0:T(8,128)S(1)}, f32[4,8,256]{2,1,0:T(8,128)S(1)}, f32[4,8,256]{2,1,0:T(8,128)S(1)}, f32[4,8,256]{2,1,0:T(8,128)S(1)}, f32[4,8,256...) custom-call(s32[4]{0:T(128)S(1)} %copy-done.1, s32[8,256]{1,0:T(8,128)S(1)} %get-tuple-element.74.ids_ref, ...), custom_call_target="tpu_custom_call" | custom-call | tf_op jit(solution)/shard_map/logits/pallas_call | solution.py:274
  71.3 0.7 logits.7.refs_0_
  72.0 1.8 %collective-permute-start.21 = (f32[4,8,256]{2,1,0:T(8,128)S(1)}, f32[4,8,256]{2,1,0:T(8,128)S(1)}, u32[]{:S(2)}, u32[]{:S(2)}) collective-permute-start(f32[4,8,256]{2,1,0:T(8,128)S(1)} %logits.7.refs_0_), channel_id=1, source_target_pairs={{0,12},{1,13},{2,14},{3,15},{4,8},{5,9},{6,10},{7,11},{8,4},{9,5},... | collective-permute-start | bytes 98312 | tf_op jit(solution)/shard_map/ppermute | solution.py:307
  73.8 2.2 %collective-permute-start.22 = (f32[4,8,256]{2,1,0:T(8,128)S(1)}, f32[4,8,256]{2,1,0:T(8,128)S(1)}, u32[]{:S(2)}, u32[]{:S(2)}) collective-permute-start(f32[4,8,256]{2,1,0:T(8,128)S(1)} %logits.7.refs_0_), channel_id=1, source_target_pairs={{0,8},{1,9},{2,10},{3,11},{4,12},{5,13},{6,14},{7,15},{8,0},{9,1},... | collective-permute-start | bytes 98312 | tf_op jit(solution)/shard_map/ppermute | solution.py:307
  75.9 0.9 %collective-permute-done.21.refs_1_ = f32[4,8,256]{2,1,0:T(8,128)S(1)} collective-permute-done((f32[4,8,256]{2,1,0:T(8,128)S(1)}, f32[4,8,256]{2,1,0:T(8,128)S(1)}, u32[]{:S(2)}, u32[]{:S(2)}) %collective-permute-start.21) | collective-permute-done | bytes 32800 | tf_op jit(solution)/shard_map/ppermute | solution.py:307
  76.9 1.6 %collective-permute-done.22.refs_2_ = f32[4,8,256]{2,1,0:T(8,128)S(1)} collective-permute-done((f32[4,8,256]{2,1,0:T(8,128)S(1)}, f32[4,8,256]{2,1,0:T(8,128)S(1)}, u32[]{:S(2)}, u32[]{:S(2)}) %collective-permute-start.22) | collective-permute-done | bytes 32800 | tf_op jit(solution)/shard_map/ppermute | solution.py:307
  78.5 1.4 %collective-permute-done.23.refs_3_ = f32[4,8,256]{2,1,0:T(8,128)S(1)} collective-permute-done((f32[4,8,256]{2,1,0:T(8,128)S(1)}, f32[4,8,256]{2,1,0:T(8,128)S(1)}, u32[]{:S(2)}, u32[]{:S(2)}) %collective-permute-start.23) | collective-permute-done | bytes 32800 | tf_op jit(solution)/shard_map/ppermute | solution.py:307
  79.9 3.4 %collective-permute-start.24 = (f32[4,4,256]{2,1,0:T(4,128)S(1)}, f32[4,4,256]{2,1,0:T(4,128)S(1)}, u32[]{:S(2)}, u32[]{:S(2)}) collective-permute-start(f32[4,4,256]{2,1,0:T(4,128)S(1)} %get-tuple-element.134), channel_id=1, source_target_pairs={{0,18},{1,19},{2,16},{3,17},{4,22},{5,23},{6,20},{7,21},{8,26},{9,... | collective-permute-start | bytes 49160 | tf_op jit(solution)/shard_map/ppermute | solution.py:307
  83.3 1.5 %collective-permute-start.25 = (f32[4,4,256]{2,1,0:T(4,128)S(1)}, f32[4,4,256]{2,1,0:T(4,128)S(1)}, u32[]{:S(2)}, u32[]{:S(2)}) collective-permute-start(f32[4,4,256]{2,1,0:T(4,128)S(1)} %get-tuple-element.135.a_ref), channel_id=1, source_target_pairs={{0,16},{1,17},{2,18},{3,19},{4,20},{5,21},{6,22},{7,23},{8,24},{9,... | collective-permute-start | bytes 49160 | tf_op jit(solution)/shard_map/ppermute | solution.py:307
  84.8 0.7 collective-permute-done.24.d_ref
  85.5 2.4 %collective-permute-done.25.b_ref = f32[4,4,256]{2,1,0:T(4,128)S(1)} collective-permute-done((f32[4,4,256]{2,1,0:T(4,128)S(1)}, f32[4,4,256]{2,1,0:T(4,128)S(1)}, u32[]{:S(2)}, u32[]{:S(2)}) %collective-permute-start.25) | collective-permute-done | bytes 16416 | tf_op jit(solution)/shard_map/ppermute | solution.py:307
  87.9 0.6 collective-permute-done.26.c_ref
  88.7 1.2 %collective-permute-done.27.refs_1_ = f32[8,256]{1,0:T(8,128)S(1)} collective-permute-done((f32[8,256]{1,0:T(8,128)S(1)}, f32[8,256]{1,0:T(8,128)S(1)}, u32[]{:S(2)}, u32[]{:S(2)}) %collective-permute-start.27) | collective-permute-done | bytes 8224 | tf_op jit(solution)/shard_map/ppermute | solution.py:307
  89.8 1.2 %place.1 = (f32[2048]{0:T(1024)}, f32[2048]{0:T(1024)}) custom-call(s32[4]{0:T(128)S(1)} %copy-done.1, f32[8,256]{1,0:T(8,128)S(1)} %get-tuple-element.136.refs_0_, f32[8,256]{1,0:T(8,128)S(1)} %collective-permute-done.27.refs_1_), custom_call_target="tpu_custom_call" | custom-call | tf_op jit(solution)/shard_map/place/pallas_call | solution.py:274
  (30 shorter events, 0.4 us)
Async XLA Ops:
  0.6 15.5 %copy-start = (bf16[256,4016]{0,1:T(8,128)(2,1)S(1)}, bf16[256,4016]{0,1:T(8,128)(2,1)}, u32[]{:S(2)}) copy-start(bf16[256,4016]{0,1:T(8,128)(2,1)} %param.7) | copy-start | bytes 6168580
  0.6 27.7 %collective-permute-start.6 = (bf16[4016,256]{1,0:T(8,128)(2,1)}, bf16[4016,256]{1,0:T(8,128)(2,1)S(1)}, u32[]{:S(2)}, u32[]{:S(2)}) collective-permute-start(bf16[4016,256]{1,0:T(8,128)(2,1)} %bitcast.1), channel_id=1, source_target_pairs={{0,1},{1,0},{2,3},{3,2},{4,5},{5,4},{6,7},{7,6},{8,9},{9,8},{10,11... | collective-permute-start | bytes 6168584 | tf_op jit(solution)/shard_map/ppermute | solution.py:307
  2.4 6.6 %collective-permute-start.2 = (bf16[272,256]{1,0:T(8,128)(2,1)S(1)}, bf16[272,256]{1,0:T(8,128)(2,1)S(1)}, u32[]{:S(2)}, u32[]{:S(2)}) collective-permute-start(bf16[272,256]{1,0:T(8,128)(2,1)S(1)} %get-tuple-element.73), channel_id=1, source_target_pairs={{0,3},{1,2},{2,1},{3,0},{4,7},{5,6},{6,5},{7,4},{8,11},{9,10},{10,... | collective-permute-start | bytes 417800 | tf_op jit(solution)/shard_map/ppermute | solution.py:307
  5.0 5.6 %collective-permute-start = (bf16[272,256]{1,0:T(8,128)(2,1)S(1)}, bf16[272,256]{1,0:T(8,128)(2,1)S(1)}, u32[]{:S(2)}, u32[]{:S(2)}) collective-permute-start(bf16[272,256]{1,0:T(8,128)(2,1)S(1)} %get-tuple-element.71), channel_id=1, source_target_pairs={{0,1},{1,0},{2,3},{3,2},{4,5},{5,4},{6,7},{7,6},{8,9},{9,8},{10,11... | collective-permute-start | bytes 417800 | tf_op jit(solution)/shard_map/ppermute | solution.py:307
  5.2 7.1 %collective-permute-start.1 = (bf16[272,256]{1,0:T(8,128)(2,1)S(1)}, bf16[272,256]{1,0:T(8,128)(2,1)S(1)}, u32[]{:S(2)}, u32[]{:S(2)}) collective-permute-start(bf16[272,256]{1,0:T(8,128)(2,1)S(1)} %get-tuple-element.72), channel_id=1, source_target_pairs={{0,2},{1,3},{2,0},{3,1},{4,6},{5,7},{6,4},{7,5},{8,10},{9,11},{10,... | collective-permute-start | bytes 417800 | tf_op jit(solution)/shard_map/ppermute | solution.py:307
  9.0 19.3 %collective-permute-start.5 = (bf16[1280,256]{1,0:T(8,128)(2,1)S(1)}, bf16[1280,256]{1,0:T(8,128)(2,1)S(1)}, u32[]{:S(2)}, u32[]{:S(2)}) collective-permute-start(bf16[1280,256]{1,0:T(8,128)(2,1)S(1)} %slice.44), channel_id=1, source_target_pairs={{0,2},{1,3},{2,0},{3,1},{4,6},{5,7},{6,4},{7,5},{8,10},{9,11},{10,... | collective-permute-start | bytes 1966088 | tf_op jit(solution)/shard_map/ppermute | solution.py:307
  12.7 21.5 %copy-start.1 = (s32[4]{0:T(128)S(1)}, s32[4]{0:T(128)}, u32[]{:S(2)}) copy-start(s32[4]{0:T(128)} %seq_ref.9) | copy-start | bytes 52
  12.7 15.7 %collective-permute-start.3 = (bf16[1024,256]{1,0:T(8,128)(2,1)S(1)}, bf16[1024,256]{1,0:T(8,128)(2,1)S(1)}, u32[]{:S(2)}, u32[]{:S(2)}) collective-permute-start(bf16[1024,256]{1,0:T(8,128)(2,1)S(1)} %get-tuple-element.75.refs_0_), channel_id=1, source_target_pairs={{0,8},{1,9},{2,10},{3,11},{4,12},{5,13},{6,14},{7,15},{8,16},{9,17... | collective-permute-start | bytes 1572872 | tf_op jit(solution)/shard_map/ppermute | solution.py:307
  14.6 13.7 %collective-permute-start.4 = (bf16[1024,256]{1,0:T(8,128)(2,1)S(1)}, bf16[1024,256]{1,0:T(8,128)(2,1)S(1)}, u32[]{:S(2)}, u32[]{:S(2)}) collective-permute-start(bf16[1024,256]{1,0:T(8,128)(2,1)S(1)} %get-tuple-element.75.refs_0_), channel_id=1, source_target_pairs={{0,4},{1,5},{2,6},{3,7},{4,0},{5,1},{6,2},{7,3},{8,12},{9,13},{10,... | collective-permute-start | bytes 1572872 | tf_op jit(solution)/shard_map/ppermute | solution.py:307
  16.2 26.6 %collective-permute-start.9 = (bf16[1472,256]{1,0:T(8,128)(2,1)S(1)}, bf16[1472,256]{1,0:T(8,128)(2,1)S(1)}, u32[]{:S(2)}, u32[]{:S(2)}) collective-permute-start(bf16[1472,256]{1,0:T(8,128)(2,1)S(1)} %slice.45), channel_id=1, source_target_pairs={{0,2},{1,3},{2,0},{3,1},{4,6},{5,7},{6,4},{7,5},{8,10},{9,11},{10,... | collective-permute-start | bytes 2261000 | tf_op jit(solution)/shard_map/ppermute | solution.py:307
  28.4 14.7 %collective-permute-start.7 = (bf16[1024,256]{1,0:T(8,128)(2,1)S(1)}, bf16[1024,256]{1,0:T(8,128)(2,1)S(1)}, u32[]{:S(2)}, u32[]{:S(2)}) collective-permute-start(bf16[1024,256]{1,0:T(8,128)(2,1)S(1)} %collective-permute-done.3.refs_2_), channel_id=1, source_target_pairs={{0,8},{1,9},{2,10},{3,11},{4,12},{5,13},{6,14},{7,15},{8,16},{9,17... | collective-permute-start | bytes 1572872 | tf_op jit(solution)/shard_map/ppermute | solution.py:307
  29.4 13.7 %collective-permute-start.8 = (bf16[1024,256]{1,0:T(8,128)(2,1)S(1)}, bf16[1024,256]{1,0:T(8,128)(2,1)S(1)}, u32[]{:S(2)}, u32[]{:S(2)}) collective-permute-start(bf16[1024,256]{1,0:T(8,128)(2,1)S(1)} %collective-permute-done.3.refs_2_), channel_id=1, source_target_pairs={{0,4},{1,5},{2,6},{3,7},{4,0},{5,1},{6,2},{7,3},{8,12},{9,13},{10,... | collective-permute-start | bytes 1572872 | tf_op jit(solution)/shard_map/ppermute | solution.py:307
  30.9 1.7 %collective-permute-start.10 = (bf16[640,256]{1,0:T(8,128)(2,1)S(1)}, bf16[640,256]{1,0:T(8,128)(2,1)S(1)}, u32[]{:S(2)}, u32[]{:S(2)}) collective-permute-start(bf16[640,256]{1,0:T(8,128)(2,1)S(1)} %get-tuple-element.141), channel_id=1, source_target_pairs={{0,1},{1,0},{2,3},{3,2},{4,5},{5,4},{6,7},{7,6},{8,9},{9,8},{10,11... | collective-permute-start | bytes 983048 | tf_op jit(solution)/shard_map/ppermute | solution.py:307
  31.0 3.1 %collective-permute-start.11 = (bf16[640,256]{1,0:T(8,128)(2,1)S(1)}, bf16[640,256]{1,0:T(8,128)(2,1)S(1)}, u32[]{:S(2)}, u32[]{:S(2)}) collective-permute-start(bf16[640,256]{1,0:T(8,128)(2,1)S(1)} %get-tuple-element.140), channel_id=1, source_target_pairs={{0,1},{1,0},{2,3},{3,2},{4,5},{5,4},{6,7},{7,6},{8,9},{9,8},{10,11... | collective-permute-start | bytes 983048 | tf_op jit(solution)/shard_map/ppermute | solution.py:307
  32.6 23.7 %collective-permute-start.14 = (bf16[1264,256]{1,0:T(8,128)(2,1)S(1)}, bf16[1264,256]{1,0:T(8,128)(2,1)S(1)}, u32[]{:S(2)}, u32[]{:S(2)}) collective-permute-start(bf16[1264,256]{1,0:T(8,128)(2,1)S(1)} %slice.46), channel_id=1, source_target_pairs={{0,2},{1,3},{2,0},{3,1},{4,6},{5,7},{6,4},{7,5},{8,10},{9,11},{10,... | collective-permute-start | bytes 1941512 | tf_op jit(solution)/shard_map/ppermute | solution.py:307
  43.1 3.4 %collective-permute-start.15 = (bf16[736,256]{1,0:T(8,128)(2,1)S(1)}, bf16[736,256]{1,0:T(8,128)(2,1)S(1)}, u32[]{:S(2)}, u32[]{:S(2)}) collective-permute-start(bf16[736,256]{1,0:T(8,128)(2,1)S(1)} %get-tuple-element.139), channel_id=1, source_target_pairs={{0,1},{1,0},{2,3},{3,2},{4,5},{5,4},{6,7},{7,6},{8,9},{9,8},{10,11... | collective-permute-start | bytes 1130504 | tf_op jit(solution)/shard_map/ppermute | solution.py:307
  43.2 3.3 %collective-permute-start.16 = (bf16[736,256]{1,0:T(8,128)(2,1)S(1)}, bf16[736,256]{1,0:T(8,128)(2,1)S(1)}, u32[]{:S(2)}, u32[]{:S(2)}) collective-permute-start(bf16[736,256]{1,0:T(8,128)(2,1)S(1)} %get-tuple-element.138), channel_id=1, source_target_pairs={{0,1},{1,0},{2,3},{3,2},{4,5},{5,4},{6,7},{7,6},{8,9},{9,8},{10,11... | collective-permute-start | bytes 1130504 | tf_op jit(solution)/shard_map/ppermute | solution.py:307
  43.7 15.7 %collective-permute-start.12 = (bf16[1024,256]{1,0:T(8,128)(2,1)S(1)}, bf16[1024,256]{1,0:T(8,128)(2,1)S(1)}, u32[]{:S(2)}, u32[]{:S(2)}) collective-permute-start(bf16[1024,256]{1,0:T(8,128)(2,1)S(1)} %collective-permute-done.7.refs_4_), channel_id=1, source_target_pairs={{0,8},{1,9},{2,10},{3,11},{4,12},{5,13},{6,14},{7,15},{8,16},{9,17... | collective-permute-start | bytes 1572872 | tf_op jit(solution)/shard_map/ppermute | solution.py:307
  45.0 14.4 %collective-permute-start.13 = (bf16[1024,256]{1,0:T(8,128)(2,1)S(1)}, bf16[1024,256]{1,0:T(8,128)(2,1)S(1)}, u32[]{:S(2)}, u32[]{:S(2)}) collective-permute-start(bf16[1024,256]{1,0:T(8,128)(2,1)S(1)} %collective-permute-done.7.refs_4_), channel_id=1, source_target_pairs={{0,4},{1,5},{2,6},{3,7},{4,0},{5,1},{6,2},{7,3},{8,12},{9,13},{10,... | collective-permute-start | bytes 1572872 | tf_op jit(solution)/shard_map/ppermute | solution.py:307
  56.3 3.1 %collective-permute-start.17 = (bf16[640,256]{1,0:T(8,128)(2,1)S(1)}, bf16[640,256]{1,0:T(8,128)(2,1)S(1)}, u32[]{:S(2)}, u32[]{:S(2)}) collective-permute-start(bf16[640,256]{1,0:T(8,128)(2,1)S(1)} %slice.40), channel_id=1, source_target_pairs={{0,1},{1,0},{2,3},{3,2},{4,5},{5,4},{6,7},{7,6},{8,9},{9,8},{10,11... | collective-permute-start | bytes 983048 | tf_op jit(solution)/shard_map/ppermute | solution.py:307
  56.5 3.0 %collective-permute-start.18 = (bf16[624,256]{1,0:T(8,128)(2,1)S(1)}, bf16[624,256]{1,0:T(8,128)(2,1)S(1)}, u32[]{:S(2)}, u32[]{:S(2)}) collective-permute-start(bf16[624,256]{1,0:T(8,128)(2,1)S(1)} %slice.41), channel_id=1, source_target_pairs={{0,1},{1,0},{2,3},{3,2},{4,5},{5,4},{6,7},{7,6},{8,9},{9,8},{10,11... | collective-permute-start | bytes 958472 | tf_op jit(solution)/shard_map/ppermute | solution.py:307
  59.4 11.9 %collective-permute-start.19 = (bf16[512,256]{1,0:T(8,128)(2,1)S(1)}, bf16[512,256]{1,0:T(8,128)(2,1)S(1)}, u32[]{:S(2)}, u32[]{:S(2)}) collective-permute-start(bf16[512,256]{1,0:T(8,128)(2,1)S(1)} %slice.42), channel_id=1, source_target_pairs={{0,4},{1,5},{2,6},{3,7},{4,0},{5,1},{6,2},{7,3},{8,12},{9,13},{10,... | collective-permute-start | bytes 786440 | tf_op jit(solution)/shard_map/ppermute | solution.py:307
  60.9 10.5 %collective-permute-start.20 = (bf16[512,256]{1,0:T(8,128)(2,1)S(1)}, bf16[512,256]{1,0:T(8,128)(2,1)S(1)}, u32[]{:S(2)}, u32[]{:S(2)}) collective-permute-start(bf16[512,256]{1,0:T(8,128)(2,1)S(1)} %slice.43), channel_id=1, source_target_pairs={{0,8},{1,9},{2,10},{3,11},{4,12},{5,13},{6,14},{7,15},{8,16},{9,17... | collective-permute-start | bytes 786440 | tf_op jit(solution)/shard_map/ppermute | solution.py:307
  72.0 4.9 %collective-permute-start.21 = (f32[4,8,256]{2,1,0:T(8,128)S(1)}, f32[4,8,256]{2,1,0:T(8,128)S(1)}, u32[]{:S(2)}, u32[]{:S(2)}) collective-permute-start(f32[4,8,256]{2,1,0:T(8,128)S(1)} %logits.7.refs_0_), channel_id=1, source_target_pairs={{0,12},{1,13},{2,14},{3,15},{4,8},{5,9},{6,10},{7,11},{8,4},{9,5},... | collective-permute-start | bytes 98312 | tf_op jit(solution)/shard_map/ppermute | solution.py:307
  73.8 4.7 %collective-permute-start.22 = (f32[4,8,256]{2,1,0:T(8,128)S(1)}, f32[4,8,256]{2,1,0:T(8,128)S(1)}, u32[]{:S(2)}, u32[]{:S(2)}) collective-permute-start(f32[4,8,256]{2,1,0:T(8,128)S(1)} %logits.7.refs_0_), channel_id=1, source_target_pairs={{0,8},{1,9},{2,10},{3,11},{4,12},{5,13},{6,14},{7,15},{8,0},{9,1},... | collective-permute-start | bytes 98312 | tf_op jit(solution)/shard_map/ppermute | solution.py:307
  75.9 3.9 %collective-permute-start.23 = (f32[4,8,256]{2,1,0:T(8,128)S(1)}, f32[4,8,256]{2,1,0:T(8,128)S(1)}, u32[]{:S(2)}, u32[]{:S(2)}) collective-permute-start(f32[4,8,256]{2,1,0:T(8,128)S(1)} %logits.7.refs_0_), channel_id=1, source_target_pairs={{0,4},{1,5},{2,6},{3,7},{4,0},{5,1},{6,2},{7,3},{8,12},{9,13},{10,... | collective-permute-start | bytes 98312 | tf_op jit(solution)/shard_map/ppermute | solution.py:307
  79.9 5.6 %collective-permute-start.24 = (f32[4,4,256]{2,1,0:T(4,128)S(1)}, f32[4,4,256]{2,1,0:T(4,128)S(1)}, u32[]{:S(2)}, u32[]{:S(2)}) collective-permute-start(f32[4,4,256]{2,1,0:T(4,128)S(1)} %get-tuple-element.134), channel_id=1, source_target_pairs={{0,18},{1,19},{2,16},{3,17},{4,22},{5,23},{6,20},{7,21},{8,26},{9,... | collective-permute-start | bytes 49160 | tf_op jit(solution)/shard_map/ppermute | solution.py:307
  83.3 4.6 %collective-permute-start.25 = (f32[4,4,256]{2,1,0:T(4,128)S(1)}, f32[4,4,256]{2,1,0:T(4,128)S(1)}, u32[]{:S(2)}, u32[]{:S(2)}) collective-permute-start(f32[4,4,256]{2,1,0:T(4,128)S(1)} %get-tuple-element.135.a_ref), channel_id=1, source_target_pairs={{0,16},{1,17},{2,18},{3,19},{4,20},{5,21},{6,22},{7,23},{8,24},{9,... | collective-permute-start | bytes 49160 | tf_op jit(solution)/shard_map/ppermute | solution.py:307
  84.8 3.7 %collective-permute-start.26 = (f32[4,4,256]{2,1,0:T(4,128)S(1)}, f32[4,4,256]{2,1,0:T(4,128)S(1)}, u32[]{:S(2)}, u32[]{:S(2)}) collective-permute-start(f32[4,4,256]{2,1,0:T(4,128)S(1)} %get-tuple-element.134), channel_id=1, source_target_pairs={{0,2},{1,3},{2,0},{3,1},{4,6},{5,7},{6,4},{7,5},{8,10},{9,11},{10,... | collective-permute-start | bytes 49160 | tf_op jit(solution)/shard_map/ppermute | solution.py:307
  88.6 1.2 %collective-permute-start.27 = (f32[8,256]{1,0:T(8,128)S(1)}, f32[8,256]{1,0:T(8,128)S(1)}, u32[]{:S(2)}, u32[]{:S(2)}) collective-permute-start(f32[8,256]{1,0:T(8,128)S(1)} %get-tuple-element.137), channel_id=1, source_target_pairs={{0,1},{1,0},{2,3},{3,2},{4,5},{5,4},{6,7},{7,6},{8,9},{9,8},{10,11... | collective-permute-start | bytes 24584 | tf_op jit(solution)/shard_map/ppermute | solution.py:307

commit v6 on v5

--- a/solution.py
+++ b/solution.py
@@ -422,17 +422,10 @@
         if fast and dz:
             stage({key: list(range(whole)) for key in groups})
             tied["states"] = states
-        if dz == len(spans) - 1:
-            held, states = lax.optimization_barrier((tied.pop("far"), states))
-            near_chunk(dz, held)
-            tied["last"] = chunks[whole:]
-            if fast:
-                tied["states"] = states
         onward, arrived, tied = lax.optimization_barrier((onward, arrived, tied))
         states = tied.get("states", states)
         far = tied.get("far", {})
         near = tied.get("near", near)
-        chunks[whole:] = tied.get("last", [])
         groups.update(arrived)
         if not end:
             ring = onward[0]

time: 91.5 us -> 90.7 us (level)
  Pallas kernels: 20.5 us -> 26.3 us
  waiting for transfers between devices: 38 us -> 32.8 us
    pallas_call x9, Pallas kernels: 20.5 us -> 26.3 us  [call(): pl.pallas_call(kernel, out_shape=out_shape, in_specs=[SMEM] * smem + [HBM...]
    ppermute x28, waiting for transfers between devices: 38 us -> 32.8 us  [on_device(): move = lambda value, perm: lax.ppermute(value, AXES, perm)]
  transfers between devices with their start and end apart: 28 -> 28, of which waited for: 15 -> 17; matrix products, arithmetic and copies ran while one was open for 2% -> 2% of each run, Pallas kernels for 19% -> 22%
where the time goes in v6:
time: 90.7 us; the launch traced here: 90.8 us
  waiting for transfers between devices  32.8 us (36%)
  starting transfers between devices  29.5 us (33%)
  Pallas kernels  26.3 us (29%)
  local copies, waits for them, and re-layouts  1.41 us (2%)
    ppermute x28, waiting for transfers between devices, on_device(): move = lambda value, perm: lax.ppermute(value, AXES, perm)  32.8 us
    ppermute x28, starting transfers between devices, on_device(): move = lambda value, perm: lax.ppermute(value, AXES, perm)  29.5 us
    pallas_call x9, Pallas kernels, call(): pl.pallas_call(kernel, out_shape=out_shape, in_specs=[SMEM] * smem + [HBM...  26.3 us
  transfers between devices with their start and end apart: 28, of which 17 were waited for; matrix products, arithmetic and copies ran while one was open for 2% of the time, Pallas kernels for 22%

profile of v6, /device:TPU:0, one launch (start us, length us, event | category | flops | bytes accessed | tf_op | source)
XLA Modules:
  0.0 90.8 jit_solution(5302381493048233386)
XLA Ops:
  0.6 0.5 collective-permute-start.6
  1.2 1.3 %send.1 = (bf16[272,256]{1,0:T(8,128)(2,1)S(1)}, bf16[272,256]{1,0:T(8,128)(2,1)S(1)}, bf16[272,256]{1,0:T(8,128)(2,1)S(1)}, bf16[272,256]{1,0:T(8,128)(2,1)S(1)}) custom-call(bf16[1024,256]{1,0:T(8,128)(2,1)} %h_ref.1, f32[256]{0:T(256)} %gain_hbm.1, s32[2048]{0:T(1024)} %ids_hbm.1), custom_call_target="tpu_custom_call" | custom-call | tf_op jit(solution)/shard_map/send/pallas_call | solution.py:274
  2.4 2.6 %collective-permute-start.2 = (bf16[272,256]{1,0:T(8,128)(2,1)S(1)}, bf16[272,256]{1,0:T(8,128)(2,1)S(1)}, u32[]{:S(2)}, u32[]{:S(2)}) collective-permute-start(bf16[272,256]{1,0:T(8,128)(2,1)S(1)} %get-tuple-element.60), channel_id=1, source_target_pairs={{0,3},{1,2},{2,1},{3,0},{4,7},{5,6},{6,5},{7,4},{8,11},{9,10},{10,... | collective-permute-start | bytes 417800 | tf_op jit(solution)/shard_map/ppermute | solution.py:307
  5.2 0.3 collective-permute-start.1
  5.5 1.1 %slice.44 = bf16[1280,256]{1,0:T(8,128)(2,1)S(1)} slice(bf16[4016,256]{1,0:T(8,128)(2,1)} %bitcast.2), slice={[0:1280], [0:256]} | slice | bytes 1310720 | tf_op jit(solution)/shard_map/slice | solution.py:339
  6.6 2.4 %collective-permute-done.2.refs_3_ = bf16[272,256]{1,0:T(8,128)(2,1)S(1)} collective-permute-done((bf16[272,256]{1,0:T(8,128)(2,1)S(1)}, bf16[272,256]{1,0:T(8,128)(2,1)S(1)}, u32[]{:S(2)}, u32[]{:S(2)}) %collective-permute-start.2) | collective-permute-done | bytes 139296 | tf_op jit(solution)/shard_map/ppermute | solution.py:307
  9.0 1.6 %collective-permute-start.5 = (bf16[1280,256]{1,0:T(8,128)(2,1)S(1)}, bf16[1280,256]{1,0:T(8,128)(2,1)S(1)}, u32[]{:S(2)}, u32[]{:S(2)}) collective-permute-start(bf16[1280,256]{1,0:T(8,128)(2,1)S(1)} %slice.44), channel_id=1, source_target_pairs={{0,2},{1,3},{2,0},{3,1},{4,6},{5,7},{6,4},{7,5},{8,10},{9,11},{10,... | collective-permute-start | bytes 1966088 | tf_op jit(solution)/shard_map/ppermute | solution.py:307
  10.6 1.7 %collective-permute-done.1.refs_2_ = bf16[272,256]{1,0:T(8,128)(2,1)S(1)} collective-permute-done((bf16[272,256]{1,0:T(8,128)(2,1)S(1)}, bf16[272,256]{1,0:T(8,128)(2,1)S(1)}, u32[]{:S(2)}, u32[]{:S(2)}) %collective-permute-start.1) | collective-permute-done | bytes 139296 | tf_op jit(solution)/shard_map/ppermute | solution.py:307
  12.3 0.4 norm.1
  12.7 1.9 %collective-permute-start.3 = (bf16[1024,256]{1,0:T(8,128)(2,1)S(1)}, bf16[1024,256]{1,0:T(8,128)(2,1)S(1)}, u32[]{:S(2)}, u32[]{:S(2)}) collective-permute-start(bf16[1024,256]{1,0:T(8,128)(2,1)S(1)} %get-tuple-element.62.refs_0_), channel_id=1, source_target_pairs={{0,8},{1,9},{2,10},{3,11},{4,12},{5,13},{6,14},{7,15},{8,16},{9,17... | collective-permute-start | bytes 1572872 | tf_op jit(solution)/shard_map/ppermute | solution.py:307
  14.6 1.5 %collective-permute-start.4 = (bf16[1024,256]{1,0:T(8,128)(2,1)S(1)}, bf16[1024,256]{1,0:T(8,128)(2,1)S(1)}, u32[]{:S(2)}, u32[]{:S(2)}) collective-permute-start(bf16[1024,256]{1,0:T(8,128)(2,1)S(1)} %get-tuple-element.62.refs_0_), channel_id=1, source_target_pairs={{0,4},{1,5},{2,6},{3,7},{4,0},{5,1},{6,2},{7,3},{8,12},{9,13},{10,... | collective-permute-start | bytes 1572872 | tf_op jit(solution)/shard_map/ppermute | solution.py:307
  16.2 1.6 %collective-permute-start.9 = (bf16[1472,256]{1,0:T(8,128)(2,1)S(1)}, bf16[1472,256]{1,0:T(8,128)(2,1)S(1)}, u32[]{:S(2)}, u32[]{:S(2)}) collective-permute-start(bf16[1472,256]{1,0:T(8,128)(2,1)S(1)} %slice.45), channel_id=1, source_target_pairs={{0,2},{1,3},{2,0},{3,1},{4,6},{5,7},{6,4},{7,5},{8,10},{9,11},{10,... | collective-permute-start | bytes 2261000 | tf_op jit(solution)/shard_map/ppermute | solution.py:307
  17.8 10.6 %collective-permute-done.3.refs_2_ = bf16[1024,256]{1,0:T(8,128)(2,1)S(1)} collective-permute-done((bf16[1024,256]{1,0:T(8,128)(2,1)S(1)}, bf16[1024,256]{1,0:T(8,128)(2,1)S(1)}, u32[]{:S(2)}, u32[]{:S(2)}) %collective-permute-start.3) | collective-permute-done | bytes 524320 | tf_op jit(solution)/shard_map/ppermute | solution.py:307
  28.4 1.0 %collective-permute-start.7 = (bf16[1024,256]{1,0:T(8,128)(2,1)S(1)}, bf16[1024,256]{1,0:T(8,128)(2,1)S(1)}, u32[]{:S(2)}, u32[]{:S(2)}) collective-permute-start(bf16[1024,256]{1,0:T(8,128)(2,1)S(1)} %collective-permute-done.3.refs_2_), channel_id=1, source_target_pairs={{0,8},{1,9},{2,10},{3,11},{4,12},{5,13},{6,14},{7,15},{8,16},{9,17... | collective-permute-start | bytes 1572872 | tf_op jit(solution)/shard_map/ppermute | solution.py:307
  29.4 1.5 %collective-permute-start.8 = (bf16[1024,256]{1,0:T(8,128)(2,1)S(1)}, bf16[1024,256]{1,0:T(8,128)(2,1)S(1)}, u32[]{:S(2)}, u32[]{:S(2)}) collective-permute-start(bf16[1024,256]{1,0:T(8,128)(2,1)S(1)} %collective-permute-done.3.refs_2_), channel_id=1, source_target_pairs={{0,4},{1,5},{2,6},{3,7},{4,0},{5,1},{6,2},{7,3},{8,12},{9,13},{10,... | collective-permute-start | bytes 1572872 | tf_op jit(solution)/shard_map/ppermute | solution.py:307
  31.0 0.5 collective-permute-start.11
  31.5 1.1 %collective-permute-done.10.refs_6_.refs_8_.refs_10_.refs_5_ = bf16[640,256]{1,0:T(8,128)(2,1)S(1)} collective-permute-done((bf16[640,256]{1,0:T(8,128)(2,1)S(1)}, bf16[640,256]{1,0:T(8,128)(2,1)S(1)}, u32[]{:S(2)}, u32[]{:S(2)}) %collective-permute-start.10) | collective-permute-done | bytes 327712 | tf_op jit(solution)/shard_map/ppermute | solution.py:307
  32.6 1.5 %collective-permute-start.14 = (bf16[1264,256]{1,0:T(8,128)(2,1)S(1)}, bf16[1264,256]{1,0:T(8,128)(2,1)S(1)}, u32[]{:S(2)}, u32[]{:S(2)}) collective-permute-start(bf16[1264,256]{1,0:T(8,128)(2,1)S(1)} %slice.46), channel_id=1, source_target_pairs={{0,2},{1,3},{2,0},{3,1},{4,6},{5,7},{6,4},{7,5},{8,10},{9,11},{10,... | collective-permute-start | bytes 1941512 | tf_op jit(solution)/shard_map/ppermute | solution.py:307
  34.1 2.6 %logits.4 = (f32[4,8,256]{2,1,0:T(8,128)S(1)}, f32[4,8,256]{2,1,0:T(8,128)S(1)}, f32[4,8,256]{2,1,0:T(8,128)S(1)}) custom-call(s32[4]{0:T(128)S(1)} %copy-done.1, s32[8,256]{1,0:T(8,128)S(1)} %get-tuple-element.61.ids_ref, bf16[1024,256]{1,0:T(8,128)(2,1)S(1)} %get-tuple-element.62.refs_0_, bf16[1024,256]{1,0:T(8,128)(2,1)S(1)} %collective-permute-done.4.refs_1_, ...), custom_call_target="tpu_custom_call" | custom-call | tf_op jit(solution)/shard_map/logits/pallas_call | solution.py:274
  36.8 6.0 %collective-permute-done.9.refs_10_.refs_12_.refs_7_ = bf16[1472,256]{1,0:T(8,128)(2,1)S(1)} collective-permute-done((bf16[1472,256]{1,0:T(8,128)(2,1)S(1)}, bf16[1472,256]{1,0:T(8,128)(2,1)S(1)}, u32[]{:S(2)}, u32[]{:S(2)}) %collective-permute-start.9) | collective-permute-done | bytes 753696 | tf_op jit(solution)/shard_map/ppermute | solution.py:307
  42.7 0.3 collective-permute-done.7.refs_4_
  43.1 1.4 %collective-permute-start.12 = (bf16[1024,256]{1,0:T(8,128)(2,1)S(1)}, bf16[1024,256]{1,0:T(8,128)(2,1)S(1)}, u32[]{:S(2)}, u32[]{:S(2)}) collective-permute-start(bf16[1024,256]{1,0:T(8,128)(2,1)S(1)} %collective-permute-done.7.refs_4_), channel_id=1, source_target_pairs={{0,8},{1,9},{2,10},{3,11},{4,12},{5,13},{6,14},{7,15},{8,16},{9,17... | collective-permute-start | bytes 1572872 | tf_op jit(solution)/shard_map/ppermute | solution.py:307
  44.4 1.5 %collective-permute-start.13 = (bf16[1024,256]{1,0:T(8,128)(2,1)S(1)}, bf16[1024,256]{1,0:T(8,128)(2,1)S(1)}, u32[]{:S(2)}, u32[]{:S(2)}) collective-permute-start(bf16[1024,256]{1,0:T(8,128)(2,1)S(1)} %collective-permute-done.7.refs_4_), channel_id=1, source_target_pairs={{0,4},{1,5},{2,6},{3,7},{4,0},{5,1},{6,2},{7,3},{8,12},{9,13},{10,... | collective-permute-start | bytes 1572872 | tf_op jit(solution)/shard_map/ppermute | solution.py:307
  46.0 0.5 collective-permute-start.16
  46.5 1.2 %collective-permute-done.15.refs_11_.refs_13_.refs_8_ = bf16[736,256]{1,0:T(8,128)(2,1)S(1)} collective-permute-done((bf16[736,256]{1,0:T(8,128)(2,1)S(1)}, bf16[736,256]{1,0:T(8,128)(2,1)S(1)}, u32[]{:S(2)}, u32[]{:S(2)}) %collective-permute-start.15) | collective-permute-done | bytes 376864 | tf_op jit(solution)/shard_map/ppermute | solution.py:307
  47.7 0.5 collective-permute-done.16.refs_12_.refs_14_.refs_9_
  48.3 6.9 %logits.5 = (f32[4,8,256]{2,1,0:T(8,128)S(1)}, f32[4,8,256]{2,1,0:T(8,128)S(1)}, f32[4,8,256]{2,1,0:T(8,128)S(1)}, f32[4,8,256]{2,1,0:T(8,128)S(1)}, f32[4,8,256]{2,1,0:T(8,128)S(1)}) custom-call(s32[4]{0:T(128)S(1)} %copy-done.1, s32[8,256]{1,0:T(8,128)S(1)} %get-tuple-element.61.ids_ref, bf16[1024,256]{1,0:T(8,128)(2,1)S(1)} %get-tuple-element.62.refs_0_, ...), custom_call_target="tpu_custom_call" | custom-call | tf_op jit(solution)/shard_map/logits/pallas_call | solution.py:274
  55.2 1.1 %collective-permute-done.14.refs_15_.refs_10_ = bf16[1264,256]{1,0:T(8,128)(2,1)S(1)} collective-permute-done((bf16[1264,256]{1,0:T(8,128)(2,1)S(1)}, bf16[1264,256]{1,0:T(8,128)(2,1)S(1)}, u32[]{:S(2)}, u32[]{:S(2)}) %collective-permute-start.14) | collective-permute-done | bytes 647200 | tf_op jit(solution)/shard_map/ppermute | solution.py:307
  56.3 2.1 %collective-permute-done.12.refs_6_ = bf16[1024,256]{1,0:T(8,128)(2,1)S(1)} collective-permute-done((bf16[1024,256]{1,0:T(8,128)(2,1)S(1)}, bf16[1024,256]{1,0:T(8,128)(2,1)S(1)}, u32[]{:S(2)}, u32[]{:S(2)}) %collective-permute-start.12) | collective-permute-done | bytes 524320 | tf_op jit(solution)/shard_map/ppermute | solution.py:307
  58.6 0.6 collective-permute-start.20
  59.1 1.6 %collective-permute-start.17 = (bf16[512,256]{1,0:T(8,128)(2,1)S(1)}, bf16[512,256]{1,0:T(8,128)(2,1)S(1)}, u32[]{:S(2)}, u32[]{:S(2)}) collective-permute-start(bf16[512,256]{1,0:T(8,128)(2,1)S(1)} %slice.40), channel_id=1, source_target_pairs={{0,4},{1,5},{2,6},{3,7},{4,0},{5,1},{6,2},{7,3},{8,12},{9,13},{10,... | collective-permute-start | bytes 786440 | tf_op jit(solution)/shard_map/ppermute | solution.py:307
  60.7 1.1 %collective-permute-start.18 = (bf16[512,256]{1,0:T(8,128)(2,1)S(1)}, bf16[512,256]{1,0:T(8,128)(2,1)S(1)}, u32[]{:S(2)}, u32[]{:S(2)}) collective-permute-start(bf16[512,256]{1,0:T(8,128)(2,1)S(1)} %slice.41), channel_id=1, source_target_pairs={{0,8},{1,9},{2,10},{3,11},{4,12},{5,13},{6,14},{7,15},{8,16},{9,17... | collective-permute-start | bytes 786440 | tf_op jit(solution)/shard_map/ppermute | solution.py:307
  61.8 10.3 %logits.6 = (f32[4,8,256]{2,1,0:T(8,128)S(1)}, f32[4,8,256]{2,1,0:T(8,128)S(1)}, f32[4,8,256]{2,1,0:T(8,128)S(1)}, f32[4,8,256]{2,1,0:T(8,128)S(1)}, f32[4,8,256...) custom-call(s32[4]{0:T(128)S(1)} %copy-done.1, s32[8,256]{1,0:T(8,128)S(1)} %get-tuple-element.61.ids_ref, ...), custom_call_target="tpu_custom_call" | custom-call | tf_op jit(solution)/shard_map/logits/pallas_call | solution.py:274
  72.1 3.5 %logits.7.refs_0_ = f32[4,8,256]{2,1,0:T(8,128)S(1)} custom-call(s32[4]{0:T(128)S(1)} %copy-done.1, s32[8,256]{1,0:T(8,128)S(1)} %get-tuple-element.61.ids_ref, bf16[512,256]{1,0:T(8,128)(2,1)S(1)} %collective-permute-done.17.refs_0_, bf16[512,256]{1,0:T(8,128)(2,1)S(1)} %collective-permute-done.18.refs_1_, bf16[4016,256]{1,0:T(8,128)(2,1)S(1)} %bitcast.8, ...), custom_call_target="tpu_custom_call" | custom-call | tf_op jit(solution)/shard_map/logits/pallas_call | solution.py:274
  75.6 1.6 %collective-permute-start.21 = (f32[4,8,256]{2,1,0:T(8,128)S(1)}, f32[4,8,256]{2,1,0:T(8,128)S(1)}, u32[]{:S(2)}, u32[]{:S(2)}) collective-permute-start(f32[4,8,256]{2,1,0:T(8,128)S(1)} %logits.7.refs_0_), channel_id=1, source_target_pairs={{0,12},{1,13},{2,14},{3,15},{4,8},{5,9},{6,10},{7,11},{8,4},{9,5},... | collective-permute-start | bytes 98312 | tf_op jit(solution)/shard_map/ppermute | solution.py:307
  77.2 0.5 collective-permute-start.22
  77.7 1.5 %collective-permute-start.23 = (f32[4,8,256]{2,1,0:T(8,128)S(1)}, f32[4,8,256]{2,1,0:T(8,128)S(1)}, u32[]{:S(2)}, u32[]{:S(2)}) collective-permute-start(f32[4,8,256]{2,1,0:T(8,128)S(1)} %logits.7.refs_0_), channel_id=1, source_target_pairs={{0,4},{1,5},{2,6},{3,7},{4,0},{5,1},{6,2},{7,3},{8,12},{9,13},{10,... | collective-permute-start | bytes 98312 | tf_op jit(solution)/shard_map/ppermute | solution.py:307
  79.2 1.5 %collective-permute-done.21.refs_1_ = f32[4,8,256]{2,1,0:T(8,128)S(1)} collective-permute-done((f32[4,8,256]{2,1,0:T(8,128)S(1)}, f32[4,8,256]{2,1,0:T(8,128)S(1)}, u32[]{:S(2)}, u32[]{:S(2)}) %collective-permute-start.21) | collective-permute-done | bytes 32800 | tf_op jit(solution)/shard_map/ppermute | solution.py:307
  80.6 0.5 collective-permute-done.22.refs_2_
  81.1 0.5 collective-permute-done.23.refs_3_
  81.6 1.8 %collective-permute-start.24 = (f32[4,4,256]{2,1,0:T(4,128)S(1)}, f32[4,4,256]{2,1,0:T(4,128)S(1)}, u32[]{:S(2)}, u32[]{:S(2)}) collective-permute-start(f32[4,4,256]{2,1,0:T(4,128)S(1)} %get-tuple-element.108), channel_id=1, source_target_pairs={{0,18},{1,19},{2,16},{3,17},{4,22},{5,23},{6,20},{7,21},{8,26},{9,... | collective-permute-start | bytes 49160 | tf_op jit(solution)/shard_map/ppermute | solution.py:307
  83.5 1.1 %collective-permute-start.25 = (f32[4,4,256]{2,1,0:T(4,128)S(1)}, f32[4,4,256]{2,1,0:T(4,128)S(1)}, u32[]{:S(2)}, u32[]{:S(2)}) collective-permute-start(f32[4,4,256]{2,1,0:T(4,128)S(1)} %get-tuple-element.109.a_ref), channel_id=1, source_target_pairs={{0,16},{1,17},{2,18},{3,19},{4,20},{5,21},{6,22},{7,23},{8,24},{9,... | collective-permute-start | bytes 49160 | tf_op jit(solution)/shard_map/ppermute | solution.py:307
  84.6 1.5 %collective-permute-start.26 = (f32[4,4,256]{2,1,0:T(4,128)S(1)}, f32[4,4,256]{2,1,0:T(4,128)S(1)}, u32[]{:S(2)}, u32[]{:S(2)}) collective-permute-start(f32[4,4,256]{2,1,0:T(4,128)S(1)} %get-tuple-element.108), channel_id=1, source_target_pairs={{0,2},{1,3},{2,0},{3,1},{4,6},{5,7},{6,4},{7,5},{8,10},{9,11},{10,... | collective-permute-start | bytes 49160 | tf_op jit(solution)/shard_map/ppermute | solution.py:307
  86.1 1.1 %collective-permute-done.24.d_ref = f32[4,4,256]{2,1,0:T(4,128)S(1)} collective-permute-done((f32[4,4,256]{2,1,0:T(4,128)S(1)}, f32[4,4,256]{2,1,0:T(4,128)S(1)}, u32[]{:S(2)}, u32[]{:S(2)}) %collective-permute-start.24) | collective-permute-done | bytes 16416 | tf_op jit(solution)/shard_map/ppermute | solution.py:307
  87.2 0.9 collective-permute-done.25.b_ref
  88.1 0.2 collective-permute-done.26.c_ref
  88.4 1.2 %collective-permute-done.27.refs_1_ = f32[8,256]{1,0:T(8,128)S(1)} collective-permute-done((f32[8,256]{1,0:T(8,128)S(1)}, f32[8,256]{1,0:T(8,128)S(1)}, u32[]{:S(2)}, u32[]{:S(2)}) %collective-permute-start.27) | collective-permute-done | bytes 8224 | tf_op jit(solution)/shard_map/ppermute | solution.py:307
  89.6 1.2 %place.1 = (f32[2048]{0:T(1024)}, f32[2048]{0:T(1024)}) custom-call(s32[4]{0:T(128)S(1)} %copy-done.1, f32[8,256]{1,0:T(8,128)S(1)} %get-tuple-element.110.refs_0_, f32[8,256]{1,0:T(8,128)S(1)} %collective-permute-done.27.refs_1_), custom_call_target="tpu_custom_call" | custom-call | tf_op jit(solution)/shard_map/place/pallas_call | solution.py:274
  (30 shorter events, 0.8 us)
Async XLA Ops:
  0.6 15.5 %copy-start = (bf16[256,4016]{0,1:T(8,128)(2,1)S(1)}, bf16[256,4016]{0,1:T(8,128)(2,1)}, u32[]{:S(2)}) copy-start(bf16[256,4016]{0,1:T(8,128)(2,1)} %param.7) | copy-start | bytes 6168580
  0.6 27.7 %collective-permute-start.6 = (bf16[4016,256]{1,0:T(8,128)(2,1)}, bf16[4016,256]{1,0:T(8,128)(2,1)S(1)}, u32[]{:S(2)}, u32[]{:S(2)}) collective-permute-start(bf16[4016,256]{1,0:T(8,128)(2,1)} %bitcast.1), channel_id=1, source_target_pairs={{0,1},{1,0},{2,3},{3,2},{4,5},{5,4},{6,7},{7,6},{8,9},{9,8},{10,11... | collective-permute-start | bytes 6168584 | tf_op jit(solution)/shard_map/ppermute | solution.py:307
  2.4 6.6 %collective-permute-start.2 = (bf16[272,256]{1,0:T(8,128)(2,1)S(1)}, bf16[272,256]{1,0:T(8,128)(2,1)S(1)}, u32[]{:S(2)}, u32[]{:S(2)}) collective-permute-start(bf16[272,256]{1,0:T(8,128)(2,1)S(1)} %get-tuple-element.60), channel_id=1, source_target_pairs={{0,3},{1,2},{2,1},{3,0},{4,7},{5,6},{6,5},{7,4},{8,11},{9,10},{10,... | collective-permute-start | bytes 417800 | tf_op jit(solution)/shard_map/ppermute | solution.py:307
  5.0 5.6 %collective-permute-start = (bf16[272,256]{1,0:T(8,128)(2,1)S(1)}, bf16[272,256]{1,0:T(8,128)(2,1)S(1)}, u32[]{:S(2)}, u32[]{:S(2)}) collective-permute-start(bf16[272,256]{1,0:T(8,128)(2,1)S(1)} %get-tuple-element.58), channel_id=1, source_target_pairs={{0,1},{1,0},{2,3},{3,2},{4,5},{5,4},{6,7},{7,6},{8,9},{9,8},{10,11... | collective-permute-start | bytes 417800 | tf_op jit(solution)/shard_map/ppermute | solution.py:307
  5.2 7.1 %collective-permute-start.1 = (bf16[272,256]{1,0:T(8,128)(2,1)S(1)}, bf16[272,256]{1,0:T(8,128)(2,1)S(1)}, u32[]{:S(2)}, u32[]{:S(2)}) collective-permute-start(bf16[272,256]{1,0:T(8,128)(2,1)S(1)} %get-tuple-element.59), channel_id=1, source_target_pairs={{0,2},{1,3},{2,0},{3,1},{4,6},{5,7},{6,4},{7,5},{8,10},{9,11},{10,... | collective-permute-start | bytes 417800 | tf_op jit(solution)/shard_map/ppermute | solution.py:307
  9.0 19.3 %collective-permute-start.5 = (bf16[1280,256]{1,0:T(8,128)(2,1)S(1)}, bf16[1280,256]{1,0:T(8,128)(2,1)S(1)}, u32[]{:S(2)}, u32[]{:S(2)}) collective-permute-start(bf16[1280,256]{1,0:T(8,128)(2,1)S(1)} %slice.44), channel_id=1, source_target_pairs={{0,2},{1,3},{2,0},{3,1},{4,6},{5,7},{6,4},{7,5},{8,10},{9,11},{10,... | collective-permute-start | bytes 1966088 | tf_op jit(solution)/shard_map/ppermute | solution.py:307
  12.7 21.5 %copy-start.1 = (s32[4]{0:T(128)S(1)}, s32[4]{0:T(128)}, u32[]{:S(2)}) copy-start(s32[4]{0:T(128)} %seq_ref.9) | copy-start | bytes 52
  12.7 15.7 %collective-permute-start.3 = (bf16[1024,256]{1,0:T(8,128)(2,1)S(1)}, bf16[1024,256]{1,0:T(8,128)(2,1)S(1)}, u32[]{:S(2)}, u32[]{:S(2)}) collective-permute-start(bf16[1024,256]{1,0:T(8,128)(2,1)S(1)} %get-tuple-element.62.refs_0_), channel_id=1, source_target_pairs={{0,8},{1,9},{2,10},{3,11},{4,12},{5,13},{6,14},{7,15},{8,16},{9,17... | collective-permute-start | bytes 1572872 | tf_op jit(solution)/shard_map/ppermute | solution.py:307
  14.6 13.7 %collective-permute-start.4 = (bf16[1024,256]{1,0:T(8,128)(2,1)S(1)}, bf16[1024,256]{1,0:T(8,128)(2,1)S(1)}, u32[]{:S(2)}, u32[]{:S(2)}) collective-permute-start(bf16[1024,256]{1,0:T(8,128)(2,1)S(1)} %get-tuple-element.62.refs_0_), channel_id=1, source_target_pairs={{0,4},{1,5},{2,6},{3,7},{4,0},{5,1},{6,2},{7,3},{8,12},{9,13},{10,... | collective-permute-start | bytes 1572872 | tf_op jit(solution)/shard_map/ppermute | solution.py:307
  16.2 26.6 %collective-permute-start.9 = (bf16[1472,256]{1,0:T(8,128)(2,1)S(1)}, bf16[1472,256]{1,0:T(8,128)(2,1)S(1)}, u32[]{:S(2)}, u32[]{:S(2)}) collective-permute-start(bf16[1472,256]{1,0:T(8,128)(2,1)S(1)} %slice.45), channel_id=1, source_target_pairs={{0,2},{1,3},{2,0},{3,1},{4,6},{5,7},{6,4},{7,5},{8,10},{9,11},{10,... | collective-permute-start | bytes 2261000 | tf_op jit(solution)/shard_map/ppermute | solution.py:307
  28.4 14.7 %collective-permute-start.7 = (bf16[1024,256]{1,0:T(8,128)(2,1)S(1)}, bf16[1024,256]{1,0:T(8,128)(2,1)S(1)}, u32[]{:S(2)}, u32[]{:S(2)}) collective-permute-start(bf16[1024,256]{1,0:T(8,128)(2,1)S(1)} %collective-permute-done.3.refs_2_), channel_id=1, source_target_pairs={{0,8},{1,9},{2,10},{3,11},{4,12},{5,13},{6,14},{7,15},{8,16},{9,17... | collective-permute-start | bytes 1572872 | tf_op jit(solution)/shard_map/ppermute | solution.py:307
  29.4 13.7 %collective-permute-start.8 = (bf16[1024,256]{1,0:T(8,128)(2,1)S(1)}, bf16[1024,256]{1,0:T(8,128)(2,1)S(1)}, u32[]{:S(2)}, u32[]{:S(2)}) collective-permute-start(bf16[1024,256]{1,0:T(8,128)(2,1)S(1)} %collective-permute-done.3.refs_2_), channel_id=1, source_target_pairs={{0,4},{1,5},{2,6},{3,7},{4,0},{5,1},{6,2},{7,3},{8,12},{9,13},{10,... | collective-permute-start | bytes 1572872 | tf_op jit(solution)/shard_map/ppermute | solution.py:307
  30.9 1.7 %collective-permute-start.10 = (bf16[640,256]{1,0:T(8,128)(2,1)S(1)}, bf16[640,256]{1,0:T(8,128)(2,1)S(1)}, u32[]{:S(2)}, u32[]{:S(2)}) collective-permute-start(bf16[640,256]{1,0:T(8,128)(2,1)S(1)} %get-tuple-element.115), channel_id=1, source_target_pairs={{0,1},{1,0},{2,3},{3,2},{4,5},{5,4},{6,7},{7,6},{8,9},{9,8},{10,11... | collective-permute-start | bytes 983048 | tf_op jit(solution)/shard_map/ppermute | solution.py:307
  31.0 3.1 %collective-permute-start.11 = (bf16[640,256]{1,0:T(8,128)(2,1)S(1)}, bf16[640,256]{1,0:T(8,128)(2,1)S(1)}, u32[]{:S(2)}, u32[]{:S(2)}) collective-permute-start(bf16[640,256]{1,0:T(8,128)(2,1)S(1)} %get-tuple-element.114), channel_id=1, source_target_pairs={{0,1},{1,0},{2,3},{3,2},{4,5},{5,4},{6,7},{7,6},{8,9},{9,8},{10,11... | collective-permute-start | bytes 983048 | tf_op jit(solution)/shard_map/ppermute | solution.py:307
  32.6 23.7 %collective-permute-start.14 = (bf16[1264,256]{1,0:T(8,128)(2,1)S(1)}, bf16[1264,256]{1,0:T(8,128)(2,1)S(1)}, u32[]{:S(2)}, u32[]{:S(2)}) collective-permute-start(bf16[1264,256]{1,0:T(8,128)(2,1)S(1)} %slice.46), channel_id=1, source_target_pairs={{0,2},{1,3},{2,0},{3,1},{4,6},{5,7},{6,4},{7,5},{8,10},{9,11},{10,... | collective-permute-start | bytes 1941512 | tf_op jit(solution)/shard_map/ppermute | solution.py:307
  43.1 15.4 %collective-permute-start.12 = (bf16[1024,256]{1,0:T(8,128)(2,1)S(1)}, bf16[1024,256]{1,0:T(8,128)(2,1)S(1)}, u32[]{:S(2)}, u32[]{:S(2)}) collective-permute-start(bf16[1024,256]{1,0:T(8,128)(2,1)S(1)} %collective-permute-done.7.refs_4_), channel_id=1, source_target_pairs={{0,8},{1,9},{2,10},{3,11},{4,12},{5,13},{6,14},{7,15},{8,16},{9,17... | collective-permute-start | bytes 1572872 | tf_op jit(solution)/shard_map/ppermute | solution.py:307
  44.4 14.0 %collective-permute-start.13 = (bf16[1024,256]{1,0:T(8,128)(2,1)S(1)}, bf16[1024,256]{1,0:T(8,128)(2,1)S(1)}, u32[]{:S(2)}, u32[]{:S(2)}) collective-permute-start(bf16[1024,256]{1,0:T(8,128)(2,1)S(1)} %collective-permute-done.7.refs_4_), channel_id=1, source_target_pairs={{0,4},{1,5},{2,6},{3,7},{4,0},{5,1},{6,2},{7,3},{8,12},{9,13},{10,... | collective-permute-start | bytes 1572872 | tf_op jit(solution)/shard_map/ppermute | solution.py:307
  46.0 1.8 %collective-permute-start.15 = (bf16[736,256]{1,0:T(8,128)(2,1)S(1)}, bf16[736,256]{1,0:T(8,128)(2,1)S(1)}, u32[]{:S(2)}, u32[]{:S(2)}) collective-permute-start(bf16[736,256]{1,0:T(8,128)(2,1)S(1)} %get-tuple-element.113), channel_id=1, source_target_pairs={{0,1},{1,0},{2,3},{3,2},{4,5},{5,4},{6,7},{7,6},{8,9},{9,8},{10,11... | collective-permute-start | bytes 1130504 | tf_op jit(solution)/shard_map/ppermute | solution.py:307
  46.0 2.2 %collective-permute-start.16 = (bf16[736,256]{1,0:T(8,128)(2,1)S(1)}, bf16[736,256]{1,0:T(8,128)(2,1)S(1)}, u32[]{:S(2)}, u32[]{:S(2)}) collective-permute-start(bf16[736,256]{1,0:T(8,128)(2,1)S(1)} %get-tuple-element.112), channel_id=1, source_target_pairs={{0,1},{1,0},{2,3},{3,2},{4,5},{5,4},{6,7},{7,6},{8,9},{9,8},{10,11... | collective-permute-start | bytes 1130504 | tf_op jit(solution)/shard_map/ppermute | solution.py:307
  58.4 3.3 %collective-permute-start.19 = (bf16[640,256]{1,0:T(8,128)(2,1)S(1)}, bf16[640,256]{1,0:T(8,128)(2,1)S(1)}, u32[]{:S(2)}, u32[]{:S(2)}) collective-permute-start(bf16[640,256]{1,0:T(8,128)(2,1)S(1)} %slice.42), channel_id=1, source_target_pairs={{0,1},{1,0},{2,3},{3,2},{4,5},{5,4},{6,7},{7,6},{8,9},{9,8},{10,11... | collective-permute-start | bytes 983048 | tf_op jit(solution)/shard_map/ppermute | solution.py:307
  58.6 3.2 %collective-permute-start.20 = (bf16[624,256]{1,0:T(8,128)(2,1)S(1)}, bf16[624,256]{1,0:T(8,128)(2,1)S(1)}, u32[]{:S(2)}, u32[]{:S(2)}) collective-permute-start(bf16[624,256]{1,0:T(8,128)(2,1)S(1)} %slice.43), channel_id=1, source_target_pairs={{0,1},{1,0},{2,3},{3,2},{4,5},{5,4},{6,7},{7,6},{8,9},{9,8},{10,11... | collective-permute-start | bytes 958472 | tf_op jit(solution)/shard_map/ppermute | solution.py:307
  59.1 12.9 %collective-permute-start.17 = (bf16[512,256]{1,0:T(8,128)(2,1)S(1)}, bf16[512,256]{1,0:T(8,128)(2,1)S(1)}, u32[]{:S(2)}, u32[]{:S(2)}) collective-permute-start(bf16[512,256]{1,0:T(8,128)(2,1)S(1)} %slice.40), channel_id=1, source_target_pairs={{0,4},{1,5},{2,6},{3,7},{4,0},{5,1},{6,2},{7,3},{8,12},{9,13},{10,... | collective-permute-start | bytes 786440 | tf_op jit(solution)/shard_map/ppermute | solution.py:307
  60.7 11.4 %collective-permute-start.18 = (bf16[512,256]{1,0:T(8,128)(2,1)S(1)}, bf16[512,256]{1,0:T(8,128)(2,1)S(1)}, u32[]{:S(2)}, u32[]{:S(2)}) collective-permute-start(bf16[512,256]{1,0:T(8,128)(2,1)S(1)} %slice.41), channel_id=1, source_target_pairs={{0,8},{1,9},{2,10},{3,11},{4,12},{5,13},{6,14},{7,15},{8,16},{9,17... | collective-permute-start | bytes 786440 | tf_op jit(solution)/shard_map/ppermute | solution.py:307
  75.6 5.0 %collective-permute-start.21 = (f32[4,8,256]{2,1,0:T(8,128)S(1)}, f32[4,8,256]{2,1,0:T(8,128)S(1)}, u32[]{:S(2)}, u32[]{:S(2)}) collective-permute-start(f32[4,8,256]{2,1,0:T(8,128)S(1)} %logits.7.refs_0_), channel_id=1, source_target_pairs={{0,12},{1,13},{2,14},{3,15},{4,8},{5,9},{6,10},{7,11},{8,4},{9,5},... | collective-permute-start | bytes 98312 | tf_op jit(solution)/shard_map/ppermute | solution.py:307
  77.2 3.9 %collective-permute-start.22 = (f32[4,8,256]{2,1,0:T(8,128)S(1)}, f32[4,8,256]{2,1,0:T(8,128)S(1)}, u32[]{:S(2)}, u32[]{:S(2)}) collective-permute-start(f32[4,8,256]{2,1,0:T(8,128)S(1)} %logits.7.refs_0_), channel_id=1, source_target_pairs={{0,8},{1,9},{2,10},{3,11},{4,12},{5,13},{6,14},{7,15},{8,0},{9,1},... | collective-permute-start | bytes 98312 | tf_op jit(solution)/shard_map/ppermute | solution.py:307
  77.7 3.9 %collective-permute-start.23 = (f32[4,8,256]{2,1,0:T(8,128)S(1)}, f32[4,8,256]{2,1,0:T(8,128)S(1)}, u32[]{:S(2)}, u32[]{:S(2)}) collective-permute-start(f32[4,8,256]{2,1,0:T(8,128)S(1)} %logits.7.refs_0_), channel_id=1, source_target_pairs={{0,4},{1,5},{2,6},{3,7},{4,0},{5,1},{6,2},{7,3},{8,12},{9,13},{10,... | collective-permute-start | bytes 98312 | tf_op jit(solution)/shard_map/ppermute | solution.py:307
  81.6 5.6 %collective-permute-start.24 = (f32[4,4,256]{2,1,0:T(4,128)S(1)}, f32[4,4,256]{2,1,0:T(4,128)S(1)}, u32[]{:S(2)}, u32[]{:S(2)}) collective-permute-start(f32[4,4,256]{2,1,0:T(4,128)S(1)} %get-tuple-element.108), channel_id=1, source_target_pairs={{0,18},{1,19},{2,16},{3,17},{4,22},{5,23},{6,20},{7,21},{8,26},{9,... | collective-permute-start | bytes 49160 | tf_op jit(solution)/shard_map/ppermute | solution.py:307
  83.5 4.6 %collective-permute-start.25 = (f32[4,4,256]{2,1,0:T(4,128)S(1)}, f32[4,4,256]{2,1,0:T(4,128)S(1)}, u32[]{:S(2)}, u32[]{:S(2)}) collective-permute-start(f32[4,4,256]{2,1,0:T(4,128)S(1)} %get-tuple-element.109.a_ref), channel_id=1, source_target_pairs={{0,16},{1,17},{2,18},{3,19},{4,20},{5,21},{6,22},{7,23},{8,24},{9,... | collective-permute-start | bytes 49160 | tf_op jit(solution)/shard_map/ppermute | solution.py:307
  84.6 3.7 %collective-permute-start.26 = (f32[4,4,256]{2,1,0:T(4,128)S(1)}, f32[4,4,256]{2,1,0:T(4,128)S(1)}, u32[]{:S(2)}, u32[]{:S(2)}) collective-permute-start(f32[4,4,256]{2,1,0:T(4,128)S(1)} %get-tuple-element.108), channel_id=1, source_target_pairs={{0,2},{1,3},{2,0},{3,1},{4,6},{5,7},{6,4},{7,5},{8,10},{9,11},{10,... | collective-permute-start | bytes 49160 | tf_op jit(solution)/shard_map/ppermute | solution.py:307
  88.4 1.2 %collective-permute-start.27 = (f32[8,256]{1,0:T(8,128)S(1)}, f32[8,256]{1,0:T(8,128)S(1)}, u32[]{:S(2)}, u32[]{:S(2)}) collective-permute-start(f32[8,256]{1,0:T(8,128)S(1)} %get-tuple-element.111), channel_id=1, source_target_pairs={{0,1},{1,0},{2,3},{3,2},{4,5},{5,4},{6,7},{7,6},{8,9},{9,8},{10,11... | collective-permute-start | bytes 24584 | tf_op jit(solution)/shard_map/ppermute | solution.py:307
